TPU v7x, 128 devices: a whole 4x4x4 slice. The times are simulated.
128 devices in a mesh: dp: 4 (over z_lo, core), tm: 32 (over y, x, z_hi).
Axes of the slice: x: 4, y: 4, z: 4 (z_hi: 2, z_lo: 2; z = z_hi * 2 + z_lo), core: 2. Of those that a mesh axis runs over, the one named last changes fastest.
Arguments:
- noisy: bfloat16 [4, 32, 2, 128, 2048], P('dp', 'tm'), may hold values from -6 to 6
- clean: bfloat16 [4, 32, 128, 2048], P('dp', 'tm'), may hold values from -6 to 6
- actions: int32 [4, 32], P('dp', 'tm'), may hold values from 0 to 17
- levels: int32 [4, 32, 2], P('dp', 'tm'), may hold values from 1 to 63
- starts: int32 [4, 32], P('dp', 'tm'), may hold values from 0 to 31, as said below
- w_qkv: bfloat16 [2048, 3, 1024], replicated, may hold values from -1 to 1
- w_out: bfloat16 [1024, 2048], replicated, may hold values from -0.1875 to 0.1875
- noise_table: float32 [64, 3, 2048], replicated, may hold values from -3 to 3
- action_table: float32 [18, 3, 2048], replicated, may hold values from -3 to 3
- temps: float32 [8], replicated, may hold values from 0.5 to 16
- out_grad: bfloat16 [4, 32, 2, 128, 2048], P('dp', 'tm'), may hold values from -6 to 6
Outputs:
- grad_noisy: bfloat16 [4, 32, 2, 128, 2048], P('dp', 'tm')
- grad_qkv: bfloat16 [2048, 3, 1024], P('tm', None, 'dp')
- grad_out: bfloat16 [1024, 2048], P('tm', 'dp')
Inputs may be any that keep to these rules, and one draw needn't show every extreme that they name: starts of frame g is at most g; the last frame of rollout 0 has no clean context.
All inputs are finite; a program needn't handle non-finite values.
Results may differ from a plain program's by a relative error of at most 0.035.
Values may be sent and summed in bfloat16 or wider, within the bound.
A program may use at most 192 MiB of HBM per device.

v0:
```python
import math

import jax
import jax.numpy as jnp
from jax import lax
from jax.sharding import PartitionSpec as P

EPS = 1e-06
NEG = -1e30


def layer_norm(values):
    center = values - jnp.mean(values, axis=-1, keepdims=True)
    return center * lax.rsqrt(jnp.mean(center * center, axis=-1, keepdims=True) + EPS)


def head_norm(values, heads):
    count = values.shape[0]
    split = values.reshape(count, heads, -1)
    factor = lax.rsqrt(jnp.mean(split * split, axis=-1, keepdims=True) + EPS)
    return (split * factor).reshape(count, -1)


def contract(left, right, left_dim, right_dim):
    return lax.dot_general(
        left, right, (((left_dim,), (right_dim,)), ((), ())), preferred_element_type=jnp.float32
    )


def modulate(values, shift, scale):
    return (layer_norm(values) * (1.0 + scale) + shift).astype(jnp.bfloat16)


def attend(query, key_own, value_own, ctx_keys, ctx_vals, own_mask, ctx_mask, temps, heads):
    count = query.shape[0]
    size = query.shape[1] // heads
    q_norm = head_norm(query, heads).astype(jnp.bfloat16)
    k_norm = head_norm(key_own, heads).astype(jnp.bfloat16)
    keys = jnp.concatenate([k_norm, ctx_keys], 0)
    vals = jnp.concatenate([value_own.astype(jnp.bfloat16), ctx_vals], 0)
    allowed = jnp.concatenate([own_mask, ctx_mask], 1)
    q_heads = q_norm.reshape(count, heads, size).transpose(1, 0, 2)
    k_heads = keys.reshape(-1, heads, size).transpose(1, 0, 2)
    v_heads = vals.reshape(-1, heads, size).transpose(1, 0, 2)

    def one_head(pieces):
        q_one, k_one, v_one, temp = pieces
        scores = contract(q_one, k_one, 1, 1) * (temp / math.sqrt(size))
        scores = jnp.where(allowed, scores, NEG)
        top = lax.stop_gradient(jnp.max(scores, axis=1, keepdims=True))
        weights = jnp.exp(scores - top)
        probs = (weights / jnp.sum(weights, axis=1, keepdims=True)).astype(jnp.bfloat16)
        return jnp.dot(probs, v_one, preferred_element_type=jnp.float32).astype(jnp.bfloat16)

    mixed = lax.map(jax.checkpoint(one_head), (q_heads, k_heads, v_heads, temps))
    return mixed.transpose(1, 0, 2).reshape(count, -1)


def build_masks(starts_local, first, frames, tokens, total):
    rows = frames * 2 * tokens
    row_ids = jnp.arange(rows, dtype=jnp.int32)
    group = row_ids // tokens
    own_mask = group[:, None] == group[None, :]
    row_frame = row_ids // (2 * tokens)
    lower = jnp.repeat(starts_local, 2 * tokens, total_repeat_length=rows)
    upper = first + row_frame
    ctx_frame = jnp.arange(total, dtype=jnp.int32) // tokens
    ctx_mask = (ctx_frame[None, :] >= lower[:, None]) & (ctx_frame[None, :] < upper[:, None])
    return (own_mask, ctx_mask)


def block_terms(
    noisy_rows, grad_rows, w_flat, w_out, mods, ctx_keys, ctx_vals, own_mask, ctx_mask, temps, heads
):
    width = w_out.shape[0]
    model = w_out.shape[1]
    shift = mods[:, :model]
    scale = mods[:, model : 2 * model]
    gate = mods[:, 2 * model :]

    def front(values):
        return modulate(values, shift, scale)

    hidden, front_back = jax.vjp(front, noisy_rows.astype(jnp.float32))
    qkv = jnp.dot(hidden, w_flat, preferred_element_type=jnp.float32)

    def mixer(query, key_own, value_own):
        return attend(
            query, key_own, value_own, ctx_keys, ctx_vals, own_mask, ctx_mask, temps, heads
        )

    mixed, mixer_back = jax.vjp(
        mixer, qkv[:, :width], qkv[:, width : 2 * width], qkv[:, 2 * width :]
    )
    grad_z = (gate * grad_rows.astype(jnp.float32)).astype(jnp.bfloat16)
    grad_mixed = contract(grad_z, w_out, 1, 1).astype(jnp.bfloat16)
    parts = mixer_back(grad_mixed)
    grad_proj = jnp.concatenate(parts, 1).astype(jnp.bfloat16)
    grad_hidden = contract(grad_proj, w_flat, 1, 1).astype(jnp.bfloat16)
    grad_input = front_back(grad_hidden)[0]
    grad_noisy = (grad_input + grad_rows.astype(jnp.float32)).astype(jnp.bfloat16)
    return (grad_noisy, hidden, grad_proj, mixed, grad_z)


def rounded(values):
    return lax.optimization_barrier(values.astype(jnp.bfloat16)).astype(jnp.float32)


def on_device(
    noisy, clean, actions, levels, starts, w_qkv, w_out, noise_table, action_table, temps, out_grad
):
    frames = noisy.shape[1]
    tokens = noisy.shape[3]
    model = noisy.shape[4]
    width = w_out.shape[0]
    heads = temps.shape[0]
    level_rows = noise_table.shape[0]
    action_rows = action_table.shape[0]
    rows = frames * 2 * tokens
    w_flat = w_qkv.reshape(model, 3 * width)
    table = noise_table.reshape(level_rows, 3 * model)
    acts = action_table.reshape(action_rows, 3 * model)
    level_hot = (
        levels[0].reshape(-1, 1) == jnp.arange(level_rows, dtype=jnp.int32)[None, :]
    ).astype(jnp.float32)
    level_mods = jnp.dot(level_hot, table, precision=lax.Precision.HIGHEST).reshape(
        frames, 2, 3 * model
    )
    action_hot = (
        actions[0].reshape(-1, 1) == jnp.arange(action_rows, dtype=jnp.int32)[None, :]
    ).astype(jnp.float32)
    action_mods = jnp.dot(action_hot, acts, precision=lax.Precision.HIGHEST)
    noisy_mods = level_mods + action_mods[:, None, :]
    mods = jnp.broadcast_to(noisy_mods[:, :, None, :], (frames, 2, tokens, 3 * model)).reshape(
        rows, 3 * model
    )
    clean_mods = table[0][None, :] + action_mods
    clean_exp = jnp.broadcast_to(clean_mods[:, None, :], (frames, tokens, 3 * model)).reshape(
        frames * tokens, 3 * model
    )
    clean_rows = clean[0].reshape(frames * tokens, model).astype(jnp.float32)
    clean_hidden = modulate(clean_rows, clean_exp[:, :model], clean_exp[:, model : 2 * model])
    clean_proj = jnp.dot(clean_hidden, w_flat[:, width:], preferred_element_type=jnp.float32)
    clean_keys = head_norm(clean_proj[:, :width], heads).astype(jnp.bfloat16)
    clean_vals = clean_proj[:, width:].astype(jnp.bfloat16)
    ctx_keys, ctx_vals = (
        lax.all_gather(clean_keys, "tm", axis=0, tiled=True),
        lax.all_gather(clean_vals, "tm", axis=0, tiled=True),
    )
    first = lax.axis_index("tm") * frames
    own_mask, ctx_mask = build_masks(starts[0], first, frames, tokens, ctx_keys.shape[0])
    noisy_rows = noisy[0].reshape(rows, model)
    grad_rows = out_grad[0].reshape(rows, model)
    grad_noisy, hidden, grad_proj, mixed, grad_z = block_terms(
        noisy_rows,
        grad_rows,
        w_flat,
        w_out,
        mods,
        ctx_keys,
        ctx_vals,
        own_mask,
        ctx_mask,
        temps,
        heads,
    )
    term_qkv = contract(hidden, grad_proj, 0, 0).reshape(model, 3, width)
    term_out = contract(mixed, grad_z, 0, 0)
    block_qkv, block_out = (
        lax.psum_scatter(
            term_qkv.astype(jnp.bfloat16), "tm", scatter_dimension=0, tiled=True
        ).astype(jnp.float32),
        lax.psum_scatter(
            term_out.astype(jnp.bfloat16), "tm", scatter_dimension=0, tiled=True
        ).astype(jnp.float32),
    )
    total_qkv, total_out = (
        lax.psum_scatter(
            rounded(block_qkv).astype(jnp.bfloat16), "dp", scatter_dimension=2, tiled=True
        ).astype(jnp.float32),
        lax.psum_scatter(
            rounded(block_out).astype(jnp.bfloat16), "dp", scatter_dimension=1, tiled=True
        ).astype(jnp.float32),
    )
    return (
        grad_noisy.reshape(1, frames, 2, tokens, model),
        total_qkv.astype(jnp.bfloat16),
        total_out.astype(jnp.bfloat16),
    )


def solution(mesh):
    in_specs = (
        P("dp", "tm", None, None, None),
        P("dp", "tm", None, None),
        P("dp", "tm"),
        P("dp", "tm", None),
        P("dp", "tm"),
        P(),
        P(),
        P(),
        P(),
        P(),
        P("dp", "tm", None, None, None),
    )
    out_specs = (P("dp", "tm", None, None, None), P("tm", None, "dp"), P("tm", "dp"))
    return jax.shard_map(
        on_device, mesh=mesh, in_specs=in_specs, out_specs=out_specs, check_vma=False
    )
```

profile of v0, /device:TPU:0, one launch (start us, length us, event | category | flops | bytes accessed | tf_op | source)
XLA Modules:
  0.0 1510.3 jit_solution(6248212087640803830)
XLA Ops:
  9.5 17.0 %copy.114 = bf16[2048,3,1024]{0,2,1:T(8,128)(2,1)} copy(bf16[2048,3,1024]{2,0,1:T(8,128)(2,1)} %param.24) | data formatting | bytes 25165824 | tf_op args[5]
  28.2 6.3 fusion.19
  41.8 2.5 fusion.23
  44.3 6.9 fusion.66
  59.5 2.7 copy.137
  62.2 2.8 multiply_convert_fusion
  69.8 74.1 %all-gather.3.cloned.1.call-done = bf16[4096,1024]{1,0:T(8,128)(2,1)} async-done(((bf16[128,1024]{1,0:T(8,128)(2,1)}), bf16[4096,1024]{1,0:T(8,128)(2,1)}) %all-gather.3.cloned.1.call-update) | async-done | bytes 8388624 | tf_op jit(solution)/shard_map/all_gather | solution.py:147
  143.9 7.4 bitcast_bitcast_fusion.1
  151.3 98.4 %all-gather.5.cloned.1.call-done = bf16[4096,1024]{1,0:T(8,128)(2,1)} async-done(((bf16[128,1024]{1,0:T(8,128)(2,1)}), bf16[4096,1024]{1,0:T(8,128)(2,1)}) %all-gather.5.cloned.1.call-update) | async-done | bytes 8388624 | tf_op jit(solution)/shard_map/all_gather | solution.py:148
  249.7 7.3 bitcast_bitcast_fusion
  257.0 4.0 broadcast.386.clone
  261.1 4.0 broadcast.386.clone2
  265.9 220.3 %while.31 = (s32[]{:T(128)}, bf16[8,256,128]{1,2,0:T(8,128)(2,1)}, bf16[8,4352,128]{1,2,0:T(8,128)(2,1)}, bf16[8,4352,128]{1,2,0:T(8,128)(2,1)}, bf16[8,256,128]...) while((s32[]{:T(128)}, bf16[8,256,128]{1,2,0:T(8,128)(2,1)}, ...), condition=%wide.region_11.12_spmd, body=%wide.region_7.11_spmd.sunk | while | flops 1450016768 | bytes 95567136 | solution.py:55
  278.5 4.1 multiply_reduce_fusion.6
  286.4 2.4 copy.171
  288.7 2.4 constant_dynamic-update-slice_fusion.9
  306.1 4.1 multiply_reduce_fusion.6
  313.9 2.4 copy.171
  333.6 4.1 multiply_reduce_fusion.6
  341.4 2.4 copy.171
  343.8 2.3 constant_dynamic-update-slice_fusion.9
  361.1 4.1 multiply_reduce_fusion.6
  368.9 2.4 copy.171
  371.3 2.3 constant_dynamic-update-slice_fusion.9
  388.6 4.1 multiply_reduce_fusion.6
  396.4 2.4 copy.171
  398.8 2.3 constant_dynamic-update-slice_fusion.9
  416.1 4.1 multiply_reduce_fusion.6
  423.9 2.4 copy.171
  426.2 2.3 constant_dynamic-update-slice_fusion.9
  443.5 4.1 multiply_reduce_fusion.6
  451.3 2.4 copy.171
  453.7 2.4 constant_dynamic-update-slice_fusion.9
  471.1 4.1 multiply_reduce_fusion.6
  478.8 2.4 copy.171
  481.2 2.3 constant_dynamic-update-slice_fusion.9
  494.2 8.5 convolution_convert_fusion.4
  502.7 16.2 %copy.132 = bf16[2048,3072]{0,1:T(8,128)(2,1)} copy(bf16[2048,3072]{1,0:T(8,128)(2,1)} %convolution_convert_fusion.4) | data formatting | bytes 25165824 | tf_op jit(solution)/shard_map/convert_element_type | solution.py:171
  518.9 27.5 %copy.133 = bf16[2048,3,1024]{2,1,0:T(4,128)(2,1)} copy(bf16[2048,3,1024]{0,2,1:T(8,128)(2,1)} %bitcast.219) | data formatting | bytes 25165824 | tf_op jit(solution)/shard_map/convert_element_type | solution.py:171
  546.5 53.3 %while.32 = (s32[]{:T(128)}, bf16[8,256,128]{1,2,0:T(8,128)(2,1)S(1)}, bf16[8,256,128]{2,1,0:T(8,128)(2,1)}, bf16[8,4352,128]{2,1,0:T(8,128)(2,1)}, f32[8]{0:T(1...) while((s32[]{:T(128)}, ...), condition=%wide.region_21.22_spmd, body=%wide.region_18.21_spmd.sunk | while | flops 579370496 | bytes 17112184 | solution.py:55
  547.8 2.3 fusion.119
  550.8 2.3 fusion.121
  557.5 2.3 fusion.121
  561.0 2.3 fusion.119
  564.1 2.3 fusion.121
  570.7 2.3 fusion.121
  574.3 2.3 fusion.119
  577.4 2.3 fusion.121
  584.0 2.3 fusion.121
  587.6 2.3 fusion.119
  590.6 2.3 fusion.121
  594.2 2.3 fusion.119
  597.3 2.3 fusion.121
  599.8 3.2 convolution_convert_fusion.5
  604.8 665.2 %all-reduce.3.cloned.1.call-done = bf16[2048,3,1024]{2,1,0:T(4,128)(2,1)} async-done(((bf16[2048,3,1024]{2,1,0:T(4,128)(2,1)}), bf16[2048,3,1024]{2,1,0:T(4,128)(2,1)}) %all-reduce.3.cloned.1.call-update) | async-done | bytes 12582928
  1271.3 26.8 %copy.138 = bf16[64,3,1024]{1,0,2:T(8,128)(2,1)} copy(bf16[64,3,1024]{2,1,0:T(4,128)(2,1)S(1)} %constant_dynamic-slice_fusion) | data formatting | bytes 786432
  1298.1 25.6 %reshape.382 = bf16[1024,192]{1,0:T(8,128)(2,1)} reshape(bf16[1024,64,3]{2,1,0:T(8,128)(2,1)} %bitcast.218) | data formatting | bytes 786432
  1323.9 9.4 multiply_reduce_fusion.1
  1334.0 133.3 %reduce-scatter.6.cloned.1.call-done = bf16[32,2048]{1,0:T(8,128)(2,1)} async-done(((bf16[1024,2048]{1,0:T(8,128)(2,1)}), bf16[32,2048]{1,0:T(8,128)(2,1)}) %reduce-scatter.6.cloned.1.call-update) | async-done | bytes 131088 | tf_op jit(solution)/shard_map/reduce_scatter | solution.py:173
  1467.3 2.9 fusion.24
  1470.2 12.3 reduce-scatter.10.cloned.1.call-done
  1482.5 10.8 reshape.383
  1493.3 6.3 copy.135
  1499.6 3.7 reduce-scatter.8.cloned.1.call-done
  (359 shorter events, 198.4 us)
Async XLA Ops:
  7.2 136.7 %all-gather.3.cloned.1.call-start = ((), (), s32[]{:S(2)}) async-start(), calls=%async_computation.3 | async-start | bytes 8650752 | tf_op jit(solution)/shard_map/all_gather | solution.py:147
  9.5 18.3 %copy-start.16 = (bf16[1,1,128,2048]{3,2,1,0:T(8,128)(2,1)S(1)}, bf16[1,1,128,2048]{3,2,1,0:T(8,128)(2,1)}, u32[]{:S(2)}) copy-start(bf16[1,1,128,2048]{3,2,1,0:T(8,128)(2,1)} %param.20) | copy-start | bytes 1572868
  34.9 3.8 copy-start.2
  36.1 3.8 copy-start.25
  36.1 213.6 %all-gather.5.cloned.1.call-start = ((), (), s32[]{:S(2)}) async-start(), calls=%async_computation.4 | async-start | bytes 8650752 | tf_op jit(solution)/shard_map/all_gather | solution.py:148
  36.9 1233.1 %all-reduce.3.cloned.1.call-start = ((), (), s32[]{:S(2)}) async-start(), calls=%async_computation.8 | async-start | bytes 33554432
  38.9 2.4 copy-start.19
  39.4 1.9 copy-start.21
  40.5 1.2 copy-start.10
  41.3 3.0 copy-start.4
  44.3 6.9 copy-start.8
  51.2 1.8 copy-start.6
  58.3 3.9 copy-start.7
  62.2 3.7 copy-start.11
  62.2 3.7 copy-start.26
  67.2 76.7 %copy-start.13 = (bf16[256,1024]{1,0:T(8,128)(2,1)S(1)}, bf16[256,1024]{1,0:T(8,128)(2,1)}, u32[]{:S(2)}) copy-start(bf16[256,1024]{1,0:T(8,128)(2,1)} %get-tuple-element.361) | copy-start | bytes 1572868
  143.9 105.8 %copy-start.15 = (bf16[256,1024]{1,0:T(8,128)(2,1)S(1)}, bf16[256,1024]{1,0:T(8,128)(2,1)}, u32[]{:S(2)}) copy-start(bf16[256,1024]{1,0:T(8,128)(2,1)} %slice.113) | copy-start | bytes 1572868
  261.1 4.8 copy-start.27
  268.0 3.5 copy-start.1
  271.5 2.1 copy-start
  277.4 5.2 slice-start
  278.5 4.1 slice-start.1
  295.6 3.5 copy-start.1
  299.1 2.1 copy-start
  305.0 5.2 slice-start
  306.1 4.1 slice-start.1
  323.1 3.5 copy-start.1
  326.5 2.1 copy-start
  332.5 5.2 slice-start
  333.6 4.1 slice-start.1
  350.6 3.4 copy-start.1
  354.0 2.1 copy-start
  360.0 5.2 slice-start
  361.1 4.1 slice-start.1
  378.1 3.5 copy-start.1
  381.5 2.1 copy-start
  387.5 5.2 slice-start
  388.6 4.1 slice-start.1
  405.5 3.5 copy-start.1
  409.0 2.1 copy-start
  415.0 5.2 slice-start
  416.1 4.1 slice-start.1
  433.0 3.4 copy-start.1
  436.5 2.1 copy-start
  442.4 5.2 slice-start
  443.5 4.1 slice-start.1
  460.5 3.5 copy-start.1
  464.0 2.1 copy-start
  469.9 5.2 slice-start
  471.0 4.1 slice-start.1
  486.2 3.3 copy-start.5
  487.8 6.4 copy-start.9
  489.5 3.9 copy-start.17
  492.2 1.3 copy-start.18
  493.4 0.8 copy-start.14
  546.4 920.9 %reduce-scatter.6.cloned.1.call-start = ((), (), s32[]{:S(2)}) async-start(), calls=%async_computation.5 | async-start | bytes 4325376 | tf_op jit(solution)/shard_map/reduce_scatter | solution.py:173
  546.5 53.3 %copy-start.12 = (bf16[256,2048]{1,0:T(8,128)(2,1)S(1)}, bf16[256,2048]{1,0:T(8,128)(2,1)}, u32[]{:S(2)}) copy-start(bf16[256,2048]{1,0:T(8,128)(2,1)} %get-tuple-element.359) | copy-start | bytes 3145732
  603.0 0.7 copy-start.28
  603.0 879.5 %reduce-scatter.10.cloned.1.call-start = ((), (), s32[]{:S(2)}) async-start(), calls=%async_computation.7 | async-start | bytes 655360
  1298.1 25.8 %copy-start.3 = (bf16[1,1,2,128,2048]{4,3,2,1,0:T(8,128)(2,1)S(1)}, bf16[1,1,2,128,2048]{4,3,2,1,0:T(8,128)(2,1)}, u32[]{:S(2)}) copy-start(bf16[1,1,2,128,2048]{4,3,2,1,0:T(8,128)(2,1)} %param.19) | copy-start | bytes 3145732
  1298.1 25.8 %copy-start.20 = (f32[256]{0:T(256)S(1)}, f32[256]{0:T(256)}, u32[]{:S(2)}) copy-start(f32[256]{0:T(256)} %copy-done.19) | copy-start | bytes 3076
  1323.8 9.5 copy-start.24
  1323.8 9.5 copy-start.22
  1323.8 179.5 %reduce-scatter.8.cloned.1.call-start = ((), (), s32[]{:S(2)}) async-start(), calls=%async_computation.6 | async-start | bytes 163840 | tf_op jit(solution)/shard_map/reduce_scatter | solution.py:181
  (1 other events, 0.6 us)
Sparse Core Ops, SparseCore 0:
  36.2 107.5 all-gather.2
  146.9 102.7 all-gather.4
  546.5 723.5 all-reduce.2
  1272.3 194.8 reduce-scatter.5
  1469.5 12.9 reduce-scatter.9
  1485.3 17.9 reduce-scatter.7
where the time goes:
time: 1520 us; the launch traced here: 1510 us
  waiting for transfers between devices  987 us (65%)
  local copies, waits for them, and re-layouts  272 us (18%)
  matrix products  162 us (11%)
  other arithmetic  60.2 us (4%)
  between operations  16.8 us (1%)
    unnamed x8, waiting for transfers between devices  678 us
    reduce_scatter x1, waiting for transfers between devices, on_device(): lax.psum_scatter(term_out.astype(jnp.bfloat16), 'tm', scatter_dimension=0...  133 us
    all_gather x1, waiting for transfers between devices, on_device(): lax.all_gather(clean_vals, 'tm', axis=0, tiled=True)  98.4 us
    unnamed x67, local copies, waits for them, and re-layouts  93.4 us
    dot_general x36, matrix products, contract(): lax.dot_general(left, right, (((left_dim,), (right_dim,)), ((), ())), pre...  79.4 us
    all_gather x1, waiting for transfers between devices, on_device(): lax.all_gather(clean_keys, 'tm', axis=0, tiled=True)  74.1 us
    dot_general x24, matrix products, one_head(): jnp.dot(probs, v_one, preferred_element_type=jnp.float32)  69 us
    dynamic_update_slice x64, local copies, waits for them, and re-layouts, attend(): lax.map(jax.checkpoint(one_head), (q_heads, k_heads, v_heads, temps))  66.6 us
  transfers between devices with their start and end apart: 6, of which 6 were waited for; matrix products, arithmetic and copies ran while one was open for 12% of the time, Pallas kernels for 0%

commit v1 on v0

v1 whole, which is shorter than its diff:
```python
import functools
import math

import jax
import jax.numpy as jnp
from jax import lax
from jax.experimental import pallas as pl
from jax.experimental.pallas import tpu as pltpu
from jax.sharding import PartitionSpec as P

EPS = 1e-06
NEG = -1e30
MESH = pl.DeviceIdType.MESH
HEADS = 8
HD = 128
BF = jnp.bfloat16
F32 = jnp.float32
ANY = pl.BlockSpec(memory_space=pl.ANY)
LOG2E = 1.4426950408889634


def dot(left, right, left_dim, right_dim):
    return lax.dot_general(
        left, right, (((left_dim,), (right_dim,)), ((), ())), preferred_element_type=F32
    )


def layer_norm(values):
    center = values - jnp.mean(values, axis=-1, keepdims=True)
    return center * lax.rsqrt(jnp.mean(center * center, axis=-1, keepdims=True) + EPS)


def head_norm(values):
    count = values.shape[0]
    split = values.reshape(count, HEADS, HD)
    factor = lax.rsqrt(jnp.mean(split * split, axis=-1, keepdims=True) + EPS)
    return (split * factor).reshape(count, -1)


def lanes(start, size):
    return pl.ds(pl.multiple_of(start, 128), size)


def rows_of(start, size):
    return pl.ds(pl.multiple_of(start, size), size)


def wait_bytes(ref, sem):
    pltpu.make_async_copy(ref, ref, sem).wait()


def place(t):
    return t // 8, (t // 2) % 4, t % 2


def head_home(h, x):
    return ((h // 2) * 4 + x) * 2 + h % 2


def shifted(t, s):
    y, x, z = place(t)
    dy, dx, dz = place(s)
    return (((y + dy) % 4) * 4 + (x + dx) % 4) * 2 + (z + dz) % 2


def spread_kernel(ck, cv, qn, kn, v, do, kv_ref, own_ref, sems):
    me = lax.axis_index("tm")
    y, x, z = place(me)
    slot = y * 2 + z
    barrier = pltpu.get_barrier_semaphore()

    def greet(s, carry):
        pl.semaphore_signal(
            barrier, inc=1, device_id={"tm": shifted(me, s)}, device_id_type=MESH
        )
        return carry

    lax.fori_loop(1, 32, greet, 0)
    pl.semaphore_wait(barrier, 31)

    def send_kv(s, carry):
        t = shifted(me, s)
        ty, _, tz = place(t)
        cut = lanes((ty * 2 + tz) * HD, HD)
        for part, ref in enumerate((ck, cv)):
            pltpu.make_async_remote_copy(
                src_ref=ref.at[:, cut],
                dst_ref=kv_ref.at[me, part],
                send_sem=sems.at[0],
                recv_sem=sems.at[1],
                device_id={"tm": t},
                device_id_type=MESH,
            ).start()
        return carry

    def send_own(s, carry):
        h = (slot + s) % 8
        cut = lanes(h * HD, HD)
        for part, ref in enumerate((qn, kn, v, do)):
            pltpu.make_async_remote_copy(
                src_ref=ref.at[:, cut],
                dst_ref=own_ref.at[slot, part],
                send_sem=sems.at[2],
                recv_sem=sems.at[3],
                device_id={"tm": head_home(h, x)},
                device_id_type=MESH,
            ).start()
        return carry

    lax.fori_loop(1, 32, send_kv, 0)
    lax.fori_loop(1, 8, send_own, 0)
    cut = lanes(slot * HD, HD)
    for part, ref in enumerate((ck, cv)):
        pltpu.make_async_copy(ref.at[:, cut], kv_ref.at[me, part], sems.at[4]).start()
    for part, ref in enumerate((qn, kn, v, do)):
        pltpu.make_async_copy(ref.at[:, cut], own_ref.at[slot, part], sems.at[5]).start()
    wait_bytes(kv_ref.at[0], sems.at[4])
    wait_bytes(own_ref.at[0], sems.at[5])
    wait_bytes(kv_ref.at[pl.ds(0, 31)], sems.at[0])
    wait_bytes(own_ref.at[pl.ds(0, 7)], sems.at[2])
    wait_bytes(kv_ref.at[pl.ds(0, 31)], sems.at[1])
    wait_bytes(own_ref.at[pl.ds(0, 7)], sems.at[3])


def spread(ck, cv, qn, kn, v, do):
    frames = 32
    tokens = ck.shape[0]
    rows = qn.shape[0]
    return pl.pallas_call(
        spread_kernel,
        out_shape=(
            jax.ShapeDtypeStruct((frames, 2, tokens, HD), BF),
            jax.ShapeDtypeStruct((8, 4, rows, HD), BF),
        ),
        in_specs=[ANY] * 6,
        out_specs=(ANY, ANY),
        scratch_shapes=[pltpu.SemaphoreType.DMA((6,))],
        compiler_params=pltpu.CompilerParams(collective_id=0, has_side_effects=True),
        name="spread",
    )(ck, cv, qn, kn, v, do)


def attend_kernel(frames, starts, temp, kv, own, out, s_scr):
    i = pl.program_id(0)
    g = frames[i]
    st = starts[i]
    n = g - st
    odd = n % 2
    pairs = n // 2
    first = st + odd
    scale = temp[0]
    c2 = scale * LOG2E
    q = own[0, 0]
    ko = own[0, 1]
    vo = own[0, 2]
    do = own[0, 3]
    k_odd = kv[st, 0]
    v_odd = kv[st, 1]
    h = HD

    s_own = jnp.concatenate([dot(q[:h], ko[:h], 1, 1), dot(q[h:], ko[h:], 1, 1)], 0)
    s_odd = jnp.where(odd == 1, dot(q, k_odd, 1, 1), NEG)
    s_scr[0, :, :h] = s_own
    s_scr[0, :, h:] = s_odd

    def scores(c, top):
        k = kv[pl.ds(first + 2 * c, 2), 0].reshape(2 * h, h)
        s = dot(q, k, 1, 1)
        s_scr[c + 1] = s
        return jnp.maximum(top, jnp.maximum(s[:, :h], s[:, h:]))

    top = lax.fori_loop(0, pairs, scores, jnp.maximum(s_own, s_odd))
    m2 = jnp.max(top, axis=1, keepdims=True) * c2

    p_own = jnp.exp2(s_own * c2 - m2)
    p_odd = jnp.exp2(s_odd * c2 - m2)
    pb_own = p_own.astype(BF)
    acc = jnp.concatenate([dot(pb_own[:h], vo[:h], 1, 0), dot(pb_own[h:], vo[h:], 1, 0)], 0)
    acc = acc + dot(p_odd.astype(BF), v_odd, 1, 0)

    def weigh(c, carry):
        acc, total = carry
        p = jnp.exp2(s_scr[c + 1] * c2 - m2)
        s_scr[c + 1] = p
        v = kv[pl.ds(first + 2 * c, 2), 1].reshape(2 * h, h)
        return acc + dot(p.astype(BF), v, 1, 0), total + p[:, :h] + p[:, h:]

    acc, total = lax.fori_loop(0, pairs, weigh, (acc, p_own + p_odd))
    inv = 1.0 / jnp.sum(total, axis=1, keepdims=True)
    mixed = acc * inv
    delta = jnp.sum(mixed * do.astype(F32), axis=1, keepdims=True)
    out[0, 0] = mixed.astype(BF)

    dp_own = jnp.concatenate([dot(do[:h], vo[:h], 1, 1), dot(do[h:], vo[h:], 1, 1)], 0)
    ds_own = (p_own * (dp_own - delta)).astype(BF)
    ds_odd = (p_odd * (dot(do, v_odd, 1, 1) - delta)).astype(BF)
    dq = jnp.concatenate([dot(ds_own[:h], ko[:h], 1, 0), dot(ds_own[h:], ko[h:], 1, 0)], 0)
    dq = dq + dot(ds_odd, k_odd, 1, 0)

    def pull(c, dq):
        k = kv[pl.ds(first + 2 * c, 2), 0].reshape(2 * h, h)
        v = kv[pl.ds(first + 2 * c, 2), 1].reshape(2 * h, h)
        ds = s_scr[c + 1] * (dot(do, v, 1, 1) - delta)
        return dq + dot(ds.astype(BF), k, 1, 0)

    dq = lax.fori_loop(0, pairs, pull, dq)
    out[0, 1] = (dq * (inv * scale)).astype(BF)
    dsn = (p_own * (dp_own - delta) * (inv * scale)).astype(BF)
    pn = (p_own * inv).astype(BF)
    for j in range(2):
        cut = slice(j * h, (j + 1) * h)
        out[0, 2, cut] = dot(dsn[cut], q[cut], 0, 0).astype(BF)
        out[0, 3, cut] = dot(pn[cut], do[cut], 0, 0).astype(BF)


def attend(frames, starts, temp, kv, own):
    rows = own.shape[2]
    smem = pl.BlockSpec(memory_space=pltpu.SMEM)
    return pl.pallas_call(
        attend_kernel,
        grid=(8,),
        out_shape=jax.ShapeDtypeStruct(own.shape, BF),
        in_specs=[
            smem,
            smem,
            smem,
            pl.BlockSpec(kv.shape, lambda i: (0, 0, 0, 0)),
            pl.BlockSpec((1, 4, rows, HD), lambda i: (i, 0, 0, 0)),
        ],
        out_specs=pl.BlockSpec((1, 4, rows, HD), lambda i: (i, 0, 0, 0)),
        scratch_shapes=[pltpu.VMEM((17, rows, 2 * HD), F32)],
        compiler_params=pltpu.CompilerParams(vmem_limit_bytes=40 * 1024 * 1024),
        name="attend",
    )(frames, starts, temp, kv, own)


def bring_kernel(res, mixed, dqkv, sems):
    me = lax.axis_index("tm")
    y, x, z = place(me)
    slot = y * 2 + z
    barrier = pltpu.get_barrier_semaphore()

    def greet(s, carry):
        pl.semaphore_signal(
            barrier,
            inc=1,
            device_id={"tm": head_home((slot + s) % 8, x)},
            device_id_type=MESH,
        )
        return carry

    lax.fori_loop(1, 8, greet, 0)
    pl.semaphore_wait(barrier, 7)

    def send(s, carry):
        i = (slot + s) % 8
        for part in range(4):
            if part == 0:
                dst = mixed.at[:, lanes(slot * HD, HD)]
            else:
                dst = dqkv.at[:, lanes((part - 1) * 1024 + slot * HD, HD)]
            pltpu.make_async_remote_copy(
                src_ref=res.at[i, part],
                dst_ref=dst,
                send_sem=sems.at[0],
                recv_sem=sems.at[1 if part == 0 else 2],
                device_id={"tm": head_home(i, x)},
                device_id_type=MESH,
            ).start()
        return carry

    lax.fori_loop(1, 8, send, 0)
    cut = lanes(slot * HD, HD)
    pltpu.make_async_copy(res.at[slot, 0], mixed.at[:, cut], sems.at[3]).start()
    for part in range(1, 4):
        dst = dqkv.at[:, lanes((part - 1) * 1024 + slot * HD, HD)]
        pltpu.make_async_copy(res.at[slot, part], dst, sems.at[3]).start()
    wait_bytes(res.at[0], sems.at[3])
    wait_bytes(res.at[pl.ds(0, 7)], sems.at[0])
    wait_bytes(mixed.at[:, pl.ds(0, 7 * HD)], sems.at[1])
    wait_bytes(dqkv.at[:, pl.ds(0, 21 * HD)], sems.at[2])


def bring(res):
    rows = res.shape[2]
    return pl.pallas_call(
        bring_kernel,
        out_shape=(
            jax.ShapeDtypeStruct((rows, HEADS * HD), BF),
            jax.ShapeDtypeStruct((rows, 3 * HEADS * HD), BF),
        ),
        in_specs=[ANY],
        out_specs=(ANY, ANY),
        scratch_shapes=[pltpu.SemaphoreType.DMA((4,))],
        compiler_params=pltpu.CompilerParams(collective_id=1, has_side_effects=True),
        name="bring",
    )(res)


def swap_kernel(hidden, mixed, proj, gz, h2, m2, p2, z2, sems):
    rows = hidden.shape[0]
    d = lax.axis_index("dp")
    core = d % 2
    partner = d + 1 - 2 * core
    barrier = pltpu.get_barrier_semaphore()
    pl.semaphore_signal(barrier, inc=1, device_id={"dp": partner}, device_id_type=MESH)
    pl.semaphore_wait(barrier, 1)
    here = rows_of(core * rows, rows)
    whole = [(hidden, h2.at[here], 0), (mixed, m2.at[here], 1)]

    def halves(c):
        cuts = []
        for zl in range(2):
            for j in range(3):
                cuts.append(
                    (
                        proj.at[:, lanes(j * 1024 + zl * 512 + c * 256, 256)],
                        p2.at[here, pl.ds(zl * 768 + j * 256, 256)],
                        2,
                    )
                )
            cuts.append(
                (gz.at[:, lanes(zl * 1024 + c * 512, 512)], z2.at[here, pl.ds(zl * 512, 512)], 3)
            )
        return cuts

    for src, dst, part in whole + halves(1 - core):
        pltpu.make_async_remote_copy(
            src_ref=src,
            dst_ref=dst,
            send_sem=sems.at[0, part],
            recv_sem=sems.at[1, part],
            device_id={"dp": partner},
            device_id_type=MESH,
        ).start()
    for src, dst, part in whole + halves(core):
        pltpu.make_async_copy(src, dst, sems.at[2, part]).start()
    for way in (2, 0, 1):
        for part, ref in enumerate((h2, m2, p2, z2)):
            wait_bytes(ref.at[pl.ds(0, rows)], sems.at[way, part])


def swap(hidden, mixed, proj, gz):
    rows = hidden.shape[0]
    shapes = ((2 * rows, 2048), (2 * rows, 1024), (2 * rows, 1536), (2 * rows, 1024))
    return pl.pallas_call(
        swap_kernel,
        out_shape=tuple(jax.ShapeDtypeStruct(shape, BF) for shape in shapes),
        in_specs=[ANY] * 4,
        out_specs=(ANY,) * 4,
        scratch_shapes=[pltpu.SemaphoreType.DMA((3, 4))],
        compiler_params=pltpu.CompilerParams(collective_id=2, has_side_effects=True),
        name="swap",
    )(hidden, mixed, proj, gz)


def total_kernel(tg, to, out_g, out_o, got_g, got_o, sems):
    t = lax.axis_index("tm")
    d = lax.axis_index("dp")
    zl = d // 2
    core = d % 2
    me = zl * 32 + t
    barrier = pltpu.get_barrier_semaphore()

    def target(s):
        return shifted(t, s % 32), (zl + s // 32) % 2

    def greet(s, carry):
        tt, tz = target(s)
        pl.semaphore_signal(
            barrier, inc=1, device_id={"tm": tt, "dp": tz * 2 + core}, device_id_type=MESH
        )
        return carry

    lax.fori_loop(1, 64, greet, 0)
    pl.semaphore_wait(barrier, 63)

    def send(s, carry):
        tt, tz = target(s)
        for src, dst, sem in (
            (tg.at[rows_of(tt * 64, 64), lanes(tz * 768, 768)], got_g.at[me], 0),
            (to.at[rows_of(tt * 32, 32), lanes(tz * 512, 512)], got_o.at[me], 1),
        ):
            pltpu.make_async_remote_copy(
                src_ref=src,
                dst_ref=dst,
                send_sem=sems.at[sem],
                recv_sem=sems.at[2 + sem],
                device_id={"tm": tt, "dp": tz * 2 + core},
                device_id_type=MESH,
            ).start()
        return carry

    lax.fori_loop(1, 64, send, 0)
    own_g = tg.at[rows_of(t * 64, 64), lanes(zl * 768, 768)]
    own_o = to.at[rows_of(t * 32, 32), lanes(zl * 512, 512)]
    copies = [
        pltpu.make_async_copy(own_g, got_g.at[me], sems.at[4]),
        pltpu.make_async_copy(own_o, got_o.at[me], sems.at[5]),
    ]
    for copy in copies:
        copy.start()
    for copy in copies:
        copy.wait()
    for sem in (0, 2):
        wait_bytes(got_g.at[pl.ds(0, 63)], sems.at[sem])
        wait_bytes(got_o.at[pl.ds(0, 63)], sems.at[sem + 1])

    for j in range(3):
        cut = slice(j * 256, (j + 1) * 256)

        def add(n, acc):
            return acc + got_g[n, :, cut].astype(F32)

        out_g[j] = lax.fori_loop(0, 64, add, jnp.zeros((64, 256), F32)).astype(BF)

    def add_out(n, acc):
        return acc + got_o[n].astype(F32)

    out_o[...] = lax.fori_loop(0, 64, add_out, jnp.zeros((32, 512), F32)).astype(BF)


def total(tg, to):
    vmem = pl.BlockSpec(memory_space=pltpu.VMEM)
    return pl.pallas_call(
        total_kernel,
        out_shape=(
            jax.ShapeDtypeStruct((3, 64, 256), BF),
            jax.ShapeDtypeStruct((32, 512), BF),
        ),
        in_specs=[ANY] * 2,
        out_specs=(vmem, vmem),
        scratch_shapes=[
            pltpu.VMEM((64, 64, 768), BF),
            pltpu.VMEM((64, 32, 512), BF),
            pltpu.SemaphoreType.DMA((6,)),
        ],
        compiler_params=pltpu.CompilerParams(
            collective_id=3, has_side_effects=True, vmem_limit_bytes=40 * 1024 * 1024
        ),
        name="total",
    )(tg, to)


def on_device(
    noisy, clean, actions, levels, starts, w_qkv, w_out, noise_table, action_table, temps, out_grad
):
    tokens, model = noisy.shape[3:]
    rows = 2 * tokens
    width = w_out.shape[0]
    t = lax.axis_index("tm")
    y, x, z = place(t)
    starts_all = lax.all_gather(starts.reshape(1), "tm", axis=0, tiled=True)
    w3 = w_qkv.transpose(1, 0, 2)

    def pick(table, index):
        return lax.dynamic_index_in_dim(table, index, 0, keepdims=False)

    action_mod = pick(action_table, actions[0, 0])
    clean_mod = noise_table[0] + action_mod
    mods = jnp.stack([pick(noise_table, levels[0, 0, j]) + action_mod for j in range(2)])

    def spread_rows(part):
        return jnp.broadcast_to(mods[:, None, part, :], (2, tokens, model)).reshape(rows, model)

    shift, scale, gate = spread_rows(0), spread_rows(1), spread_rows(2)

    clean_rows = clean.reshape(tokens, model).astype(F32)
    clean_hidden = (layer_norm(clean_rows) * (1.0 + clean_mod[1]) + clean_mod[0]).astype(BF)
    ckn = head_norm(dot(clean_hidden, w3[1], 1, 0)).astype(BF)
    cv = dot(clean_hidden, w3[2], 1, 0).astype(BF)

    noisy_rows = noisy.reshape(rows, model).astype(F32)
    grad_rows = out_grad.reshape(rows, model).astype(F32)

    def front(values):
        return (layer_norm(values) * (1.0 + scale) + shift).astype(BF)

    hidden, front_back = jax.vjp(front, noisy_rows)
    q = dot(hidden, w3[0], 1, 0)
    k = dot(hidden, w3[1], 1, 0)
    v = dot(hidden, w3[2], 1, 0).astype(BF)
    qn, q_back = jax.vjp(lambda u: head_norm(u).astype(BF), q)
    kn, k_back = jax.vjp(lambda u: head_norm(u).astype(BF), k)
    grad_z = (gate * grad_rows).astype(BF)
    grad_mixed = dot(grad_z, w_out, 1, 1).astype(BF)

    kv, own = spread(ckn, cv, qn, kn, v, grad_mixed)
    slots = jnp.arange(8, dtype=jnp.int32)
    my_frames = (slots // 2) * 8 + x * 2 + slots % 2
    my_starts = starts_all.reshape(4, 4, 2)[:, x].reshape(8)
    temp = (pick(temps, y * 2 + z) / math.sqrt(HD)).reshape(1)
    res = attend(my_frames, my_starts, temp, kv, own)
    mixed, dqkv = bring(res)

    grad_proj = jnp.concatenate(
        [
            q_back(dqkv[:, :width])[0].astype(BF),
            k_back(dqkv[:, width : 2 * width])[0].astype(BF),
            dqkv[:, 2 * width :],
        ],
        1,
    )
    grad_hidden = sum(
        dot(grad_proj[:, j * width : (j + 1) * width], w3[j], 1, 1) for j in range(3)
    ).astype(BF)
    grad_noisy = (front_back(grad_hidden)[0] + grad_rows).astype(BF)

    h2, m2, p2, z2 = swap(hidden, mixed, grad_proj, grad_z)
    term_g = dot(h2, p2, 0, 0).astype(BF)
    term_o = dot(m2, z2, 0, 0).astype(BF)
    total_g, total_o = total(term_g, term_o)
    return (grad_noisy.reshape(noisy.shape), total_g.transpose(1, 0, 2), total_o)


def solution(mesh):
    in_specs = (
        P("dp", "tm", None, None, None),
        P("dp", "tm", None, None),
        P("dp", "tm"),
        P("dp", "tm", None),
        P("dp", "tm"),
        P(),
        P(),
        P(),
        P(),
        P(),
        P("dp", "tm", None, None, None),
    )
    out_specs = (P("dp", "tm", None, None, None), P("tm", None, "dp"), P("tm", "dp"))
    return jax.shard_map(
        on_device, mesh=mesh, in_specs=in_specs, out_specs=out_specs, check_vma=False
    )
```

time: 1520 us -> 489 us (0.32)
  waiting for transfers between devices: 987 us -> 0 us
  Pallas kernels: 0 us -> 355 us
  local copies, waits for them, and re-layouts: 272 us -> 41 us
  matrix products: 162 us -> 40.9 us
  other arithmetic: 60.2 us -> 16 us
  blocking collectives: 0 us -> 21.6 us
    unnamed x8 -> x0, waiting for transfers between devices: 678 us -> none
    pallas_call x0 -> x5, Pallas kernels: none -> 355 us  [the longest x1 158 us: total(): pl.pallas_call(total_kernel, out_shape=(jax.ShapeDtypeStruct((3, 64, 256)...]
    all_gather x2 -> x0, waiting for transfers between devices: 173 us -> none  [the longest x1 98.4 us: on_device(): lax.all_gather(clean_vals, 'tm', axis=0, tiled=True)]
    reduce_scatter x2 -> x0, waiting for transfers between devices: 137 us -> none  [the longest x1 133 us: on_device(): lax.psum_scatter(term_out.astype(jnp.bfloat16), 'tm', scatter_dimension=0...]
    dot_general x64 -> x11, matrix products: 162 us -> 40.9 us  [dot(): lax.dot_general(left, right, (((left_dim,), (right_dim,)), ((), ())), pre...]
    unnamed x67 -> x51, local copies, waits for them, and re-layouts: 93.4 us -> 10.7 us
    dynamic_update_slice x64 -> x0, local copies, waits for them, and re-layouts: 66.6 us -> none  [attend(): lax.map(jax.checkpoint(one_head), (q_heads, k_heads, v_heads, temps))]
    convert_element_type x2 -> x5, local copies, waits for them, and re-layouts: 43.7 us -> 4.37 us  [the longest x1 2.04 us: on_device(): kn, k_back = jax.vjp(lambda u: head_norm(u).astype(BF), k)]
  transfers between devices with their start and end apart: 6 -> 0, of which waited for: 6 -> 0; matrix products, arithmetic and copies ran while one was open for 12% -> 0% of each run, Pallas kernels for 0% -> 0%
where the time goes in v1:
time: 489 us; the launch traced here: 481 us
  Pallas kernels  355 us (73%)
  local copies, waits for them, and re-layouts  41 us (8%)
  matrix products  40.9 us (8%)
  blocking collectives  21.6 us (4%)
  other arithmetic  16 us (3%)
  between operations  6.93 us (1%)
    pallas_call x1, Pallas kernels, total(): pl.pallas_call(total_kernel, out_shape=(jax.ShapeDtypeStruct((3, 64, 256)...  158 us
    pallas_call x1, Pallas kernels, swap(): pl.pallas_call(swap_kernel, out_shape=tuple((jax.ShapeDtypeStruct(shape,...  88.6 us
    pallas_call x1, Pallas kernels, spread(): pl.pallas_call(spread_kernel, out_shape=(jax.ShapeDtypeStruct((frames, 2,...  49.6 us
    dot_general x11, matrix products, dot(): lax.dot_general(left, right, (((left_dim,), (right_dim,)), ((), ())), pre...  40.9 us
    pallas_call x1, Pallas kernels, attend(): pl.pallas_call(attend_kernel, grid=(8,), out_shape=jax.ShapeDtypeStruct(o...  30.5 us
    pallas_call x1, Pallas kernels, bring(): pl.pallas_call(bring_kernel, out_shape=(jax.ShapeDtypeStruct((rows, HEADS...  28.2 us
    unnamed x1, blocking collectives  21.6 us
    dot_general x3, local copies, waits for them, and re-layouts, dot(): lax.dot_general(left, right, (((left_dim,), (right_dim,)), ((), ())), pre...  19.3 us

profile of v1, /device:TPU:0, one launch (start us, length us, event | category | flops | bytes accessed | tf_op | source)
XLA Modules:
  0.0 480.9 jit_solution(6719998600134166767)
XLA Ops:
  0.6 0.0 copy-start.3
  0.7 1.5 convert_reduce_fusion
  2.2 1.6 multiply_reduce_fusion.1
  3.8 0.6 fusion.50
  8.3 1.2 fusion.49
  10.1 0.8 copy_add_fusion.2
  11.1 0.5 fusion.22
  11.6 6.3 %slice_bitcast_fusion.2 = (bf16[1024,2048]{0,1:T(8,128)(2,1)}, bf16[1024,2048]{0,1:T(8,128)(2,1)}) fusion(bf16[3,2048,1024]{2,1,0:T(8,128)(2,1)} %bitcast.146), kind=kLoop, calls=%fused_computation.8 | loop fusion | bytes 16777216 | tf_op jit(solution)/shard_map/dot_general | solution.py:23
  17.9 6.5 %copy.33 = bf16[1024,2048]{1,0:T(8,128)(2,1)} copy(bf16[1024,2048]{0,1:T(8,128)(2,1)} %get-tuple-element.24) | data formatting | bytes 8388608 | tf_op jit(solution)/shard_map/dot_general | solution.py:23
  24.4 3.5 multiply_reduce_fusion.5
  27.9 0.6 dynamic-slice
  29.2 0.7 bitcast_dynamic-update-slice_fusion
  29.9 0.1 reshape.390
  30.0 21.6 %all-reduce.1 = s32[4,4,2]{2,1,0:T(4,128)S(1)} all-reduce(s32[4,4,2]{2,1,0:T(4,128)S(1)} %reshape.390), channel_id=2, replica_groups=mesh['dp'=4,'tm'=32] {'tm'}, use_global_device_ids=true, to_apply=%add | all-reduce | flops 32 | bytes 256
  51.6 0.1 reshape_squeeze.3.starts
  51.7 0.6 dynamic_slice.19
  52.9 0.0 copy-start.13
  52.9 6.6 %copy.29 = bf16[1024,2048]{1,0:T(8,128)(2,1)} copy(bf16[1024,2048]{0,1:T(8,128)(2,1)} %get-tuple-element.23) | data formatting | bytes 8388608 | tf_op jit(solution)/shard_map/dot_general | solution.py:23
  59.5 0.2 convert_reduce_fusion.1
  59.7 0.3 fusion.31
  60.0 3.6 multiply_reduce_fusion.6
  63.6 0.9 copy.42.ck
  64.5 3.7 fusion.24.cv
  68.2 0.1 multiply_convert_fusion.1
  68.4 1.1 copy.43.qn
  69.4 3.8 multiply_reduce_fusion.4
  73.3 0.9 multiply_convert_fusion
  74.2 2.0 copy.44.kn
  76.2 4.7 fusion.23.v
  80.9 0.3 fusion.15.gz
  81.3 1.0 copy-done.9
  82.3 2.1 convolution_convert_fusion.2.do
  84.4 49.6 %spread.1 = (bf16[32,2,128,128]{3,2,1,0:T(8,128)(2,1)}, bf16[8,4,256,128]{3,2,1,0:T(8,128)(2,1)}) custom-call(bf16[128,1024]{1,0:T(8,128)(2,1)} %copy.42.ck, bf16[128,1024]{1,0:T(8,128)(2,1)} %fusion.24.cv, bf16[256,1024]{1,0:T(8,128)(2,1)} %copy.43.qn, bf16[256,1024]{1,0:T(8,128)(2,1)} %copy.44.kn, bf16[256,1024]{1,0:T(8,128)(2,1)} %fusion.23.v, ...), custom_call_target="tpu_custom_call" | custom-call | tf_op jit(solution)/shard_map/spread/pallas_call | solution.py:129
  134.0 1.6 copy-done.1
  135.6 1.6 copy-done.2
  137.2 30.5 %attend.1.res = bf16[8,4,256,128]{3,2,1,0:T(8,128)(2,1)S(1)} custom-call(s32[8]{0:T(128)S(1)} %fusion.39.frames, s32[8]{0:T(128)S(1)} %reshape_squeeze.3.starts, f32[1]{0:T(128)S(6)} %div.87.temp, bf16[32,2,128,128]{3,2,1,0:T(8,128)(2,1)S(1)} %copy-done.1, bf16[8,4,256,128]{3,2,1,0:T(8,128)(2,1)S(1)} %copy-done.2), custom_call_target="tpu_custom_call" | custom-call | tf_op jit(solution)/shard_map/attend/pallas_call | solution.py:219
  167.7 1.3 copy-done
  169.0 28.2 %bring.1 = (bf16[256,1024]{1,0:T(8,128)(2,1)}, bf16[256,3072]{1,0:T(8,128)(2,1)}) custom-call(bf16[8,4,256,128]{3,2,1,0:T(8,128)(2,1)} %copy-done), custom_call_target="tpu_custom_call" | custom-call | tf_op jit(solution)/shard_map/bring/pallas_call | solution.py:286
  197.3 3.0 fusion.48
  200.3 2.5 copy.47
  202.8 1.5 multiply_reduce_fusion.3
  204.3 0.1 copy-done.4
  204.3 0.2 fusion.32
  204.6 5.0 %fusion = f32[256,2048]{1,0:T(8,128)} fusion(bf16[256,1024]{0,1:T(8,128)(2,1)S(1)} %bitcast.159, bf16[3,2048,1024]{2,1,0:T(8,128)(2,1)} %bitcast.149), kind=kOutput, calls=%fused_computation.2 | convolution fusion | flops 1073741824 | bytes 6815744 | tf_op jit(solution)/shard_map/dot_general | solution.py:23
  209.6 1.6 copy.48
  211.2 0.2 multiply_reduce_fusion.2
  211.4 0.2 fusion.33
  211.6 0.8 copy-done.5
  212.4 0.6 copy-done.10
  212.9 3.5 fusion.10
  216.4 4.0 multiply_reduce_fusion
  220.5 0.6 fusion.47
  221.1 0.6 copy-done.8
  221.7 2.5 fusion.18
  224.2 0.2 copy.46
  224.4 0.2 copy.45
  224.6 0.6 copy-done.14
  225.2 1.3 pad_maximum_fusion.proj
  226.4 88.6 %swap.1 = (bf16[512,2048]{1,0:T(8,128)(2,1)}, bf16[512,1024]{1,0:T(8,128)(2,1)}, bf16[512,1536]{1,0:T(8,128)(2,1)}, bf16[512,1024]{1,0:T(8,128)(2,1)}) custom-call(bf16[256,2048]{1,0:T(8,128)(2,1)} %get-tuple-element.31.hidden, bf16[256,1024]{1,0:T(8,128)(2,1)} %get-tuple-element.16.mixed, bf16[256,3072]{1,0:T(8,128)(2,1)} %pad_maximum_fusion.proj, ...), custom_call_target="tpu_custom_call" | custom-call | tf_op jit(solution)/shard_map/swap/pallas_call | solution.py:346
  315.1 5.7 %convolution_convert_fusion.tg = bf16[2048,1536]{1,0:T(8,128)(2,1)S(1)} fusion(bf16[512,2048]{1,0:T(8,128)(2,1)} %get-tuple-element.17, bf16[512,1536]{1,0:T(8,128)(2,1)} %get-tuple-element.18), kind=kOutput, calls=%fused_computation | convolution fusion | flops 3224371200 | bytes 9961472 | tf_op jit(solution)/shard_map/dot_general | solution.py:23
  320.7 1.3 convolution_convert_fusion.1.to
  322.0 157.6 %total.1 = (bf16[3,64,256]{2,1,0:T(8,128)(2,1)S(1)}, bf16[32,512]{1,0:T(8,128)(2,1)S(1)}) custom-call(bf16[2048,1536]{1,0:T(8,128)(2,1)S(1)} %convolution_convert_fusion.tg, bf16[1024,1024]{1,0:T(8,128)(2,1)S(1)} %convolution_convert_fusion.1.to), custom_call_target="tpu_custom_call" | custom-call | tf_op jit(solution)/shard_map/total/pallas_call | solution.py:425
  479.7 0.6 copy.67
  480.3 0.6 copy.68
  (52 shorter events, 0.3 us)
Async XLA Ops:
  0.6 10.4 %copy-start.3 = (bf16[1,1,2,128,2048]{4,3,2,1,0:T(8,128)(2,1)S(1)}, bf16[1,1,2,128,2048]{4,3,2,1,0:T(8,128)(2,1)}, u32[]{:S(2)}) copy-start(bf16[1,1,2,128,2048]{4,3,2,1,0:T(8,128)(2,1)} %param.11) | copy-start | bytes 3145732
  0.6 3.2 copy-start.16
  11.6 12.8 %copy-start.15 = (bf16[2,128,2048]{2,1,0:T(8,128)(2,1)}, bf16[2,128,2048]{2,1,0:T(8,128)(2,1)S(1)}, u32[]{:S(2)}) copy-start(bf16[2,128,2048]{2,1,0:T(8,128)(2,1)S(1)} %fusion.22) | copy-start | bytes 3145732
  24.4 3.6 copy-start.21
  24.4 27.3 %copy-start.20 = (f32[8]{0:T(128)S(1)}, f32[8]{0:T(128)}, u32[]{:S(2)}) copy-start(f32[8]{0:T(128)} %param.20) | copy-start | bytes 100
  52.9 6.6 %copy-start.13 = (bf16[1,1,128,2048]{3,2,1,0:T(8,128)(2,1)S(1)}, bf16[1,1,128,2048]{3,2,1,0:T(8,128)(2,1)}, u32[]{:S(2)}) copy-start(bf16[1,1,128,2048]{3,2,1,0:T(8,128)(2,1)} %param.12) | copy-start | bytes 1572868
  76.2 4.7 copy-start.7
  76.2 6.1 %copy-start.17 = (bf16[1024,2048]{1,0:T(8,128)(2,1)S(1)}, bf16[1024,2048]{1,0:T(8,128)(2,1)}, u32[]{:S(2)}) copy-start(bf16[1024,2048]{1,0:T(8,128)(2,1)} %param.17) | copy-start | bytes 12582916
  81.3 1.0 copy-start.9
  134.0 1.6 copy-start.1
  135.6 1.6 copy-start.2
  167.7 1.3 copy-start
  202.8 1.5 copy-start.4
  204.5 5.1 %copy-start.11 = (bf16[256,8,128]{0,2,1:T(8,128)(2,1)}, bf16[256,8,128]{0,2,1:T(8,128)(2,1)S(1)}, u32[]{:S(2)}) copy-start(bf16[256,8,128]{0,2,1:T(8,128)(2,1)S(1)} %fusion.32) | copy-start | bytes 1572868
  211.2 1.8 copy-start.10
  211.6 0.8 copy-start.5
  220.4 1.2 copy-start.8
  221.7 2.5 copy-start.6
  221.7 2.7 copy-start.12
  224.1 1.0 copy-start.14
  315.0 5.7 %copy-start.18 = (bf16[512,1024]{1,0:T(8,128)(2,1)S(1)}, bf16[512,1024]{1,0:T(8,128)(2,1)}, u32[]{:S(2)}) copy-start(bf16[512,1024]{1,0:T(8,128)(2,1)} %get-tuple-element.19) | copy-start | bytes 3145732
  315.0 5.7 %copy-start.19 = (bf16[512,1024]{1,0:T(8,128)(2,1)S(1)}, bf16[512,1024]{1,0:T(8,128)(2,1)}, u32[]{:S(2)}) copy-start(bf16[512,1024]{1,0:T(8,128)(2,1)} %get-tuple-element.20) | copy-start | bytes 3145732

commit v2 on v1

--- a/solution.py
+++ b/solution.py
@@ -234,212 +234,339 @@
     )(frames, starts, temp, kv, own)
 
 
-def bring_kernel(res, mixed, dqkv, sems):
-    me = lax.axis_index("tm")
-    y, x, z = place(me)
-    slot = y * 2 + z
+ORDERS = (("x", "y", "z"), ("y", "z", "x"), ("z", "x", "y"))
+UNITS = (5, 5, 6)
+FIRST_UNIT = (0, 5, 10)
+
+
+def stream_of(unit):
+    k = 0 if unit < 5 else 1 if unit < 10 else 2
+    return k, unit - FIRST_UNIT[k]
+
+
+def close_kernel(
+    res, hidden, gz, q, k, noisy, grad, scale1, w3,
+    out_n, out_g, out_o,
+    got, proj, ph, pm, pp, pz, w, gh,
+    t0a, t0b, t0c, t1a, t1b, t1c, t2a, t2b, t2c, b0a, b0b, b0c, b1a, b1b, b1c, b2a, b2b, b2c,
+    back_sems, swap_sems, w_sem, ring_sems, last_sems,
+):
+    t = lax.axis_index("tm")
+    d = lax.axis_index("dp")
+    y, x, zh = place(t)
+    zl, core = d // 2, d % 2
+    z = zh * 2 + zl
+    slot = y * 2 + zh
+    partner = {"dp": d + 1 - 2 * core, "tm": t}
+    at = {"x": x, "y": y, "z": z}
+    rows = hidden.shape[0]
+    terms = ((t0a, t0b, t0c), (t1a, t1b, t1c), (t2a, t2b, t2c))
+    boxes = ((b0a, b0b, b0c), (b1a, b1b, b1c), (b2a, b2b, b2c))
+
+    def along(axis, step):
+        c = dict(at)
+        c[axis] = (c[axis] + step) % 4
+        return {
+            "dp": (c["z"] % 2) * 2 + core,
+            "tm": (c["y"] * 4 + c["x"]) * 2 + c["z"] // 2,
+        }
+
+    load_w = pltpu.make_async_copy(w3, w, w_sem)
+    load_w.start()
     barrier = pltpu.get_barrier_semaphore()
 
     def greet(s, carry):
         pl.semaphore_signal(
             barrier,
             inc=1,
-            device_id={"tm": head_home((slot + s) % 8, x)},
+            device_id={"dp": d, "tm": head_home((slot + s) % 8, x)},
             device_id_type=MESH,
         )
         return carry
 
     lax.fori_loop(1, 8, greet, 0)
-    pl.semaphore_wait(barrier, 7)
-
-    def send(s, carry):
-        i = (slot + s) % 8
-        for part in range(4):
-            if part == 0:
-                dst = mixed.at[:, lanes(slot * HD, HD)]
-            else:
-                dst = dqkv.at[:, lanes((part - 1) * 1024 + slot * HD, HD)]
-            pltpu.make_async_remote_copy(
-                src_ref=res.at[i, part],
-                dst_ref=dst,
-                send_sem=sems.at[0],
-                recv_sem=sems.at[1 if part == 0 else 2],
-                device_id={"tm": head_home(i, x)},
-                device_id_type=MESH,
-            ).start()
-        return carry
-
-    lax.fori_loop(1, 8, send, 0)
-    cut = lanes(slot * HD, HD)
-    pltpu.make_async_copy(res.at[slot, 0], mixed.at[:, cut], sems.at[3]).start()
-    for part in range(1, 4):
-        dst = dqkv.at[:, lanes((part - 1) * 1024 + slot * HD, HD)]
-        pltpu.make_async_copy(res.at[slot, part], dst, sems.at[3]).start()
-    wait_bytes(res.at[0], sems.at[3])
-    wait_bytes(res.at[pl.ds(0, 7)], sems.at[0])
-    wait_bytes(mixed.at[:, pl.ds(0, 7 * HD)], sems.at[1])
-    wait_bytes(dqkv.at[:, pl.ds(0, 21 * HD)], sems.at[2])
-
-
-def bring(res):
-    rows = res.shape[2]
-    return pl.pallas_call(
-        bring_kernel,
-        out_shape=(
-            jax.ShapeDtypeStruct((rows, HEADS * HD), BF),
-            jax.ShapeDtypeStruct((rows, 3 * HEADS * HD), BF),
-        ),
-        in_specs=[ANY],
-        out_specs=(ANY, ANY),
-        scratch_shapes=[pltpu.SemaphoreType.DMA((4,))],
-        compiler_params=pltpu.CompilerParams(collective_id=1, has_side_effects=True),
-        name="bring",
-    )(res)
-
-
-def swap_kernel(hidden, mixed, proj, gz, h2, m2, p2, z2, sems):
-    rows = hidden.shape[0]
-    d = lax.axis_index("dp")
-    core = d % 2
-    partner = d + 1 - 2 * core
-    barrier = pltpu.get_barrier_semaphore()
-    pl.semaphore_signal(barrier, inc=1, device_id={"dp": partner}, device_id_type=MESH)
-    pl.semaphore_wait(barrier, 1)
-    here = rows_of(core * rows, rows)
-    whole = [(hidden, h2.at[here], 0), (mixed, m2.at[here], 1)]
-
-    def halves(c):
-        cuts = []
-        for zl in range(2):
-            for j in range(3):
-                cuts.append(
-                    (
-                        proj.at[:, lanes(j * 1024 + zl * 512 + c * 256, 256)],
-                        p2.at[here, pl.ds(zl * 768 + j * 256, 256)],
-                        2,
-                    )
-                )
-            cuts.append(
-                (gz.at[:, lanes(zl * 1024 + c * 512, 512)], z2.at[here, pl.ds(zl * 512, 512)], 3)
+    for axis in "xyz":
+        for step in (1, 2, 3):
+            pl.semaphore_signal(
+                barrier, inc=1, device_id=along(axis, step), device_id_type=MESH
             )
-        return cuts
-
-    for src, dst, part in whole + halves(1 - core):
-        pltpu.make_async_remote_copy(
+    pl.semaphore_signal(barrier, inc=1, device_id=partner, device_id_type=MESH)
+    pl.semaphore_wait(barrier, 17)
+
+    def remote(src, dst, send_sem, recv_sem, device):
+        return pltpu.make_async_remote_copy(
             src_ref=src,
             dst_ref=dst,
-            send_sem=sems.at[0, part],
-            recv_sem=sems.at[1, part],
-            device_id={"dp": partner},
+            send_sem=send_sem,
+            recv_sem=recv_sem,
+            device_id=device,
             device_id_type=MESH,
+        )
+
+    def send_back(s, carry):
+        i = (slot + s) % 8
+        remote(
+            res.at[i], got.at[slot], back_sems.at[0], back_sems.at[1],
+            {"dp": d, "tm": head_home(i, x)},
         ).start()
-    for src, dst, part in whole + halves(core):
-        pltpu.make_async_copy(src, dst, sems.at[2, part]).start()
-    for way in (2, 0, 1):
-        for part, ref in enumerate((h2, m2, p2, z2)):
-            wait_bytes(ref.at[pl.ds(0, rows)], sems.at[way, part])
-
-
-def swap(hidden, mixed, proj, gz):
-    rows = hidden.shape[0]
-    shapes = ((2 * rows, 2048), (2 * rows, 1024), (2 * rows, 1536), (2 * rows, 1024))
+        return carry
+
+    lax.fori_loop(1, 8, send_back, 0)
+    own = pltpu.make_async_copy(res.at[slot], got.at[slot], back_sems.at[2])
+    own.start()
+
+    def swap(src, dst, part):
+        copy = remote(src, dst, swap_sems.at[0, part], swap_sems.at[1, part], partner)
+        copy.start()
+        return copy
+
+    other = 1 - core
+    swaps = [swap(hidden, ph, 0)]
+    for l in range(2):
+        cut = lanes(l * 1024 + other * 512, 512)
+        swaps.append(swap(gz.at[:, cut], pz.at[:, pl.ds(l * 512, 512)], 1 + l))
+
+    own.wait()
+    wait_bytes(got.at[pl.ds(0, 7)], back_sems.at[1])
+    swaps.append(swap(got.at[:, 0], pm, 3))
+
+    def norm_back(h, carry):
+        for part, u_ref in ((0, q), (1, k)):
+            u = u_ref[:, lanes(h * HD, HD)]
+            factor = lax.rsqrt(jnp.mean(u * u, axis=1, keepdims=True) + EPS)
+            hat = u * factor
+            g = got[h, 1 + part].astype(F32)
+            du = factor * (g - hat * jnp.mean(hat * g, axis=1, keepdims=True))
+            proj[:, lanes(part * 1024 + h * HD, HD)] = du.astype(BF)
+        proj[:, lanes(2048 + h * HD, HD)] = got[h, 3]
+        return carry
+
+    lax.fori_loop(0, 8, norm_back, 0)
+    for l in range(2):
+        for j in range(3):
+            swaps.append(
+                swap(
+                    proj.at[:, lanes(j * 1024 + l * 512 + other * 256, 256)],
+                    pp.at[:, pl.ds(l * 768 + j * 256, 256)],
+                    4 + l * 3 + j,
+                )
+            )
+    for copy in swaps:
+        copy.wait_recv()
+
+    def put(yb, xb, zb, unit, value):
+        s, u = stream_of(unit)
+        spot = {"x": xb, "y": yb, "z": zb}
+        terms[0][s][spot[ORDERS[s][0]], spot[ORDERS[s][1]], spot[ORDERS[s][2]], u] = value
+
+    def terms_of(yb, carry):
+        cut = lanes(yb * 512, 512)
+        left = jnp.concatenate([hidden[:, cut], ph[:, cut]], 0).T
+        for l in range(2):
+            for j in range(3):
+                mine = proj[:, lanes(j * 1024 + l * 512 + core * 256, 256)]
+                theirs = pp[:, l * 768 + j * 256 : l * 768 + (j + 1) * 256]
+                right = jnp.concatenate([mine, theirs], 0)
+                term = dot(left, right, 1, 0).astype(BF)
+                for xb in range(4):
+                    for hb in range(2):
+                        for rg in range(4):
+                            r = (xb * 2 + hb) * 64 + rg * 16
+                            put(yb, xb, hb * 2 + l, j * 4 + rg, term[r : r + 16])
+        left = jnp.concatenate(
+            [
+                jnp.concatenate([got[2 * yb, 0], got[2 * yb + 1, 0]], 1),
+                jnp.concatenate([pm[2 * yb], pm[2 * yb + 1]], 1),
+            ],
+            0,
+        ).T
+        for l in range(2):
+            mine = gz[:, lanes(l * 1024 + core * 512, 512)]
+            right = jnp.concatenate([mine, pz[:, l * 512 : (l + 1) * 512]], 0)
+            term = dot(left, right, 1, 0).astype(BF)
+            for xb in range(4):
+                for hb in range(2):
+                    for rg in range(2):
+                        for ch in range(2):
+                            r = (xb * 2 + hb) * 32 + rg * 16
+                            put(
+                                yb, xb, hb * 2 + l, 12 + rg * 2 + ch,
+                                term[r : r + 16, ch * 256 : (ch + 1) * 256],
+                            )
+        return carry
+
+    lax.fori_loop(0, 4, terms_of, 0)
+
+    travel = (pl.ds(0, 2), pl.ds(2, 2))
+
+    def ring(s, level, way, part):
+        axis = ORDERS[s][level]
+        step = 1 if way == 0 else 3
+        near, far = (at[axis] + step) % 4, (at[axis] + 2) % 4
+        src = (
+            terms[level][s].at[far, travel[way]],
+            terms[level][s].at[near, travel[1 - way]],
+            terms[level][s].at[near, travel[way]],
+        )[part]
+        sems = ring_sems.at[s, level, way, part]
+        return remote(
+            src, boxes[level][s].at[way, part], sems.at[0], sems.at[1], along(axis, step)
+        )
+
+    def ring_open(level, s):
+        for part in range(2):
+            for way in range(2):
+                ring(s, level, way, part).start()
+
+    def ring_middle(level, s):
+        axis = ORDERS[s][level]
+        for way in range(2):
+            ring(s, level, way, 0).wait_recv()
+            near = (at[axis] + (1 if way == 0 else 3)) % 4
+            spot = terms[level][s].at[near, travel[way]]
+            spot[...] = (
+                spot[...].astype(F32) + boxes[level][s][way, 0].astype(F32)
+            ).astype(BF)
+            ring(s, level, way, 2).start()
+
+    def ring_close(level, s):
+        for way in range(2):
+            ring(s, level, way, 1).wait_recv()
+            ring(s, level, way, 2).wait_recv()
+        mine = at[ORDERS[s][level]]
+        box = boxes[level][s]
+        for way in range(2):
+            terms[level + 1][s][travel[way]] = (
+                terms[level][s][mine, travel[way]].astype(F32)
+                + box[way, 2].astype(F32)
+                + box[1 - way, 1].astype(F32)
+            ).astype(BF)
+
+    for s in range(3):
+        ring_open(0, s)
+
+    load_w.wait()
+
+    def pull_hidden(n, carry):
+        cut = lanes(n * 512, 512)
+        total = dot(proj[:, :1024], w[0, cut, :], 1, 1)
+        total = total + dot(proj[:, 1024:2048], w[1, cut, :], 1, 1)
+        total = total + dot(proj[:, 2048:], w[2, cut, :], 1, 1)
+        gh[:, cut] = total.astype(BF)
+        return carry
+
+    lax.fori_loop(0, 4, pull_hidden, 0)
+    for s in range(3):
+        ring_middle(0, s)
+
+    def norm_rows(n, carry):
+        cut = rows_of(n * 16, 16)
+        level = n // 8
+        v = noisy[cut, :].astype(F32)
+        center = v - jnp.mean(v, axis=1, keepdims=True)
+        factor = lax.rsqrt(jnp.mean(center * center, axis=1, keepdims=True) + EPS)
+        hat = center * factor
+        g = gh[cut, :].astype(F32) * scale1[pl.ds(level, 1), :]
+        dv = factor * (
+            g
+            - jnp.mean(g, axis=1, keepdims=True)
+            - hat * jnp.mean(g * hat, axis=1, keepdims=True)
+        )
+        out_n[cut, :] = (dv + grad[cut, :].astype(F32)).astype(BF)
+        return carry
+
+    lax.fori_loop(0, rows // 16, norm_rows, 0)
+
+    for s in range(3):
+        ring_close(0, s)
+        ring_open(1, s)
+    for s in range(3):
+        ring_middle(1, s)
+
+    def last(s, step):
+        axis = ORDERS[s][2]
+        there = (at[axis] + step) % 4
+        sems = last_sems.at[s, step - 1]
+        return remote(
+            terms[2][s].at[there], boxes[2][s].at[step - 1], sems.at[0], sems.at[1],
+            along(axis, step),
+        )
+
+    for s in range(3):
+        ring_close(1, s)
+        for step in (1, 2, 3):
+            last(s, step).start()
+    for s in range(3):
+        for step in (1, 2, 3):
+            last(s, step).wait_recv()
+        mine = at[ORDERS[s][2]]
+        sums = terms[2][s][mine].astype(F32)
+        for step in (1, 2, 3):
+            sums = sums + boxes[2][s][step - 1].astype(F32)
+        sums = sums.astype(BF)
+        for u in range(UNITS[s]):
+            unit = FIRST_UNIT[s] + u
+            if unit < 12:
+                j, rg = unit // 4, unit % 4
+                out_g[j, rg * 16 : (rg + 1) * 16, :] = sums[u]
+            else:
+                rg, ch = (unit - 12) // 2, (unit - 12) % 2
+                out_o[rg * 16 : (rg + 1) * 16, ch * 256 : (ch + 1) * 256] = sums[u]
+
+    wait_bytes(got.at[pl.ds(0, 7)], back_sems.at[0])
+    for copy in swaps:
+        copy.wait_send()
+    for s in range(3):
+        for level in range(2):
+            for way in range(2):
+                for part in range(3):
+                    ring(s, level, way, part).wait_send()
+        for step in (1, 2, 3):
+            last(s, step).wait_send()
+
+
+def close(res, hidden, gz, q, k, noisy, grad, scale1, w3):
+    rows, model = hidden.shape
+    vmem = pl.BlockSpec(memory_space=pltpu.VMEM)
+
+    def box(*shape):
+        return [pltpu.VMEM(shape + (u, 16, 256), BF) for u in UNITS]
+
     return pl.pallas_call(
-        swap_kernel,
-        out_shape=tuple(jax.ShapeDtypeStruct(shape, BF) for shape in shapes),
-        in_specs=[ANY] * 4,
-        out_specs=(ANY,) * 4,
-        scratch_shapes=[pltpu.SemaphoreType.DMA((3, 4))],
-        compiler_params=pltpu.CompilerParams(collective_id=2, has_side_effects=True),
-        name="swap",
-    )(hidden, mixed, proj, gz)
-
-
-def total_kernel(tg, to, out_g, out_o, got_g, got_o, sems):
-    t = lax.axis_index("tm")
-    d = lax.axis_index("dp")
-    zl = d // 2
-    core = d % 2
-    me = zl * 32 + t
-    barrier = pltpu.get_barrier_semaphore()
-
-    def target(s):
-        return shifted(t, s % 32), (zl + s // 32) % 2
-
-    def greet(s, carry):
-        tt, tz = target(s)
-        pl.semaphore_signal(
-            barrier, inc=1, device_id={"tm": tt, "dp": tz * 2 + core}, device_id_type=MESH
-        )
-        return carry
-
-    lax.fori_loop(1, 64, greet, 0)
-    pl.semaphore_wait(barrier, 63)
-
-    def send(s, carry):
-        tt, tz = target(s)
-        for src, dst, sem in (
-            (tg.at[rows_of(tt * 64, 64), lanes(tz * 768, 768)], got_g.at[me], 0),
-            (to.at[rows_of(tt * 32, 32), lanes(tz * 512, 512)], got_o.at[me], 1),
-        ):
-            pltpu.make_async_remote_copy(
-                src_ref=src,
-                dst_ref=dst,
-                send_sem=sems.at[sem],
-                recv_sem=sems.at[2 + sem],
-                device_id={"tm": tt, "dp": tz * 2 + core},
-                device_id_type=MESH,
-            ).start()
-        return carry
-
-    lax.fori_loop(1, 64, send, 0)
-    own_g = tg.at[rows_of(t * 64, 64), lanes(zl * 768, 768)]
-    own_o = to.at[rows_of(t * 32, 32), lanes(zl * 512, 512)]
-    copies = [
-        pltpu.make_async_copy(own_g, got_g.at[me], sems.at[4]),
-        pltpu.make_async_copy(own_o, got_o.at[me], sems.at[5]),
-    ]
-    for copy in copies:
-        copy.start()
-    for copy in copies:
-        copy.wait()
-    for sem in (0, 2):
-        wait_bytes(got_g.at[pl.ds(0, 63)], sems.at[sem])
-        wait_bytes(got_o.at[pl.ds(0, 63)], sems.at[sem + 1])
-
-    for j in range(3):
-        cut = slice(j * 256, (j + 1) * 256)
-
-        def add(n, acc):
-            return acc + got_g[n, :, cut].astype(F32)
-
-        out_g[j] = lax.fori_loop(0, 64, add, jnp.zeros((64, 256), F32)).astype(BF)
-
-    def add_out(n, acc):
-        return acc + got_o[n].astype(F32)
-
-    out_o[...] = lax.fori_loop(0, 64, add_out, jnp.zeros((32, 512), F32)).astype(BF)
-
-
-def total(tg, to):
-    vmem = pl.BlockSpec(memory_space=pltpu.VMEM)
-    return pl.pallas_call(
-        total_kernel,
+        close_kernel,
         out_shape=(
+            jax.ShapeDtypeStruct((rows, model), BF),
             jax.ShapeDtypeStruct((3, 64, 256), BF),
             jax.ShapeDtypeStruct((32, 512), BF),
         ),
-        in_specs=[ANY] * 2,
-        out_specs=(vmem, vmem),
+        in_specs=[ANY] + [vmem] * 7 + [ANY],
+        out_specs=(vmem,) * 3,
         scratch_shapes=[
-            pltpu.VMEM((64, 64, 768), BF),
-            pltpu.VMEM((64, 32, 512), BF),
-            pltpu.SemaphoreType.DMA((6,)),
+            pltpu.VMEM((8, 4, rows, HD), BF),
+            pltpu.VMEM((rows, 3072), BF),
+            pltpu.VMEM((rows, model), BF),
+            pltpu.VMEM((8, rows, HD), BF),
+            pltpu.VMEM((rows, 1536), BF),
+            pltpu.VMEM((rows, 1024), BF),
+            pltpu.VMEM(w3.shape, BF),
+            pltpu.VMEM((rows, model), BF),
+            *box(4, 4, 4),
+            *box(4, 4),
+            *box(4),
+            *box(2, 3, 2, 4),
+            *box(2, 3, 2),
+            *box(3),
+            pltpu.SemaphoreType.DMA((3,)),
+            pltpu.SemaphoreType.DMA((2, 10)),
+            pltpu.SemaphoreType.DMA,
+            pltpu.SemaphoreType.DMA((3, 2, 2, 3, 2)),
+            pltpu.SemaphoreType.DMA((3, 3, 2)),
         ],
         compiler_params=pltpu.CompilerParams(
-            collective_id=3, has_side_effects=True, vmem_limit_bytes=40 * 1024 * 1024
+            collective_id=1, has_side_effects=True, vmem_limit_bytes=62 * 1024 * 1024
         ),
-        name="total",
-    )(tg, to)
+        name="close",
+    )(res, hidden, gz, q, k, noisy, grad, scale1, w3)
 
 
 def on_device(
@@ -447,7 +574,6 @@
 ):
     tokens, model = noisy.shape[3:]
     rows = 2 * tokens
-    width = w_out.shape[0]
     t = lax.axis_index("tm")
     y, x, z = place(t)
     starts_all = lax.all_gather(starts.reshape(1), "tm", axis=0, tiled=True)
@@ -476,12 +602,12 @@
     def front(values):
         return (layer_norm(values) * (1.0 + scale) + shift).astype(BF)
 
-    hidden, front_back = jax.vjp(front, noisy_rows)
+    hidden = front(noisy_rows)
     q = dot(hidden, w3[0], 1, 0)
     k = dot(hidden, w3[1], 1, 0)
     v = dot(hidden, w3[2], 1, 0).astype(BF)
-    qn, q_back = jax.vjp(lambda u: head_norm(u).astype(BF), q)
-    kn, k_back = jax.vjp(lambda u: head_norm(u).astype(BF), k)
+    qn = head_norm(q).astype(BF)
+    kn = head_norm(k).astype(BF)
     grad_z = (gate * grad_rows).astype(BF)
     grad_mixed = dot(grad_z, w_out, 1, 1).astype(BF)
 
@@ -491,25 +617,17 @@
     my_starts = starts_all.reshape(4, 4, 2)[:, x].reshape(8)
     temp = (pick(temps, y * 2 + z) / math.sqrt(HD)).reshape(1)
     res = attend(my_frames, my_starts, temp, kv, own)
-    mixed, dqkv = bring(res)
-
-    grad_proj = jnp.concatenate(
-        [
-            q_back(dqkv[:, :width])[0].astype(BF),
-            k_back(dqkv[:, width : 2 * width])[0].astype(BF),
-            dqkv[:, 2 * width :],
-        ],
-        1,
+    grad_noisy, total_g, total_o = close(
+        res,
+        hidden,
+        grad_z,
+        q,
+        k,
+        noisy.reshape(rows, model),
+        out_grad.reshape(rows, model),
+        1.0 + mods[:, 1, :],
+        w3,
     )
-    grad_hidden = sum(
-        dot(grad_proj[:, j * width : (j + 1) * width], w3[j], 1, 1) for j in range(3)
-    ).astype(BF)
-    grad_noisy = (front_back(grad_hidden)[0] + grad_rows).astype(BF)
-
-    h2, m2, p2, z2 = swap(hidden, mixed, grad_proj, grad_z)
-    term_g = dot(h2, p2, 0, 0).astype(BF)
-    term_o = dot(m2, z2, 0, 0).astype(BF)
-    total_g, total_o = total(term_g, term_o)
     return (grad_noisy.reshape(noisy.shape), total_g.transpose(1, 0, 2), total_o)
 
 

time: 489 us -> 266 us (0.54)
  Pallas kernels: 355 us -> 171 us
  matrix products: 40.9 us -> 21.4 us
  local copies, waits for them, and re-layouts: 41 us -> 30 us
  other arithmetic: 16 us -> 10.9 us
    pallas_call x3 -> x1, Pallas kernels: 274 us -> 91.2 us  [close(): pl.pallas_call(close_kernel, out_shape=(jax.ShapeDtypeStruct((rows, model...]
    dot_general x11 -> x6, matrix products: 40.9 us -> 21.4 us  [dot(): lax.dot_general(left, right, (((left_dim,), (right_dim,)), ((), ())), pre...]
    dot_general x3 -> x2, local copies, waits for them, and re-layouts: 19.3 us -> 11.1 us  [dot(): lax.dot_general(left, right, (((left_dim,), (right_dim,)), ((), ())), pre...]
    unnamed x51 -> x42, local copies, waits for them, and re-layouts: 10.7 us -> 14 us
where the time goes in v2:
time: 266 us; the launch traced here: 262 us
  Pallas kernels  171 us (64%)
  local copies, waits for them, and re-layouts  30 us (11%)
  blocking collectives  21.6 us (8%)
  matrix products  21.4 us (8%)
  other arithmetic  10.9 us (4%)
  between operations  6.81 us (3%)
    pallas_call x1, Pallas kernels, close(): pl.pallas_call(close_kernel, out_shape=(jax.ShapeDtypeStruct((rows, model...  91.2 us
    pallas_call x1, Pallas kernels, spread(): pl.pallas_call(spread_kernel, out_shape=(jax.ShapeDtypeStruct((frames, 2,...  49.4 us
    pallas_call x1, Pallas kernels, attend(): pl.pallas_call(attend_kernel, grid=(8,), out_shape=jax.ShapeDtypeStruct(o...  30.7 us
    unnamed x1, blocking collectives  21.6 us
    dot_general x6, matrix products, dot(): lax.dot_general(left, right, (((left_dim,), (right_dim,)), ((), ())), pre...  21.4 us
    unnamed x42, local copies, waits for them, and re-layouts  14 us
    dot_general x2, local copies, waits for them, and re-layouts, dot(): lax.dot_general(left, right, (((left_dim,), (right_dim,)), ((), ())), pre...  11.1 us

profile of v2, /device:TPU:0, one launch (start us, length us, event | category | flops | bytes accessed | tf_op | source)
XLA Modules:
  0.0 262.1 jit_solution(10494867845031881469)
XLA Ops:
  0.6 0.0 copy-start
  0.7 1.3 dynamic-slice
  2.7 0.7 bitcast_dynamic-update-slice_fusion
  3.3 0.1 reshape.347
  3.4 21.6 %all-reduce.1 = s32[4,4,2]{2,1,0:T(4,128)S(1)} all-reduce(s32[4,4,2]{2,1,0:T(4,128)S(1)} %reshape.347), channel_id=2, replica_groups=mesh['dp'=4,'tm'=32] {'tm'}, use_global_device_ids=true, to_apply=%add | all-reduce | flops 32 | bytes 256
  25.0 0.1 reshape_squeeze.3.starts
  25.1 1.2 dynamic_slice.19
  27.0 4.6 %slice_bitcast_fusion.5 = bf16[1024,2048]{0,1:T(8,128)(2,1)} fusion(bf16[3,2048,1024]{2,1,0:T(8,128)(2,1)} %bitcast.112), kind=kLoop, calls=%fused_computation.7 | loop fusion | bytes 8388608 | tf_op jit(solution)/shard_map/dot_general | solution.py:23
  31.6 6.6 %copy.32 = bf16[1024,2048]{1,0:T(8,128)(2,1)} copy(bf16[1024,2048]{0,1:T(8,128)(2,1)} %slice_bitcast_fusion.5) | data formatting | bytes 8388608 | tf_op jit(solution)/shard_map/dot_general | solution.py:23
  38.2 0.0 copy-done.15
  38.2 0.6 fusion.40
  41.3 0.0 copy-done
  43.3 1.2 dynamic-slice_add_fusion.1
  44.5 0.0 copy-done.9
  44.5 0.2 convert_reduce_fusion.1
  44.7 0.3 fusion.23
  45.0 3.6 %multiply_reduce_fusion = (f32[128,8]{0,1:T(8,128)S(1)}, f32[128,8,128]{0,2,1:T(8,128)S(1)}) fusion(bf16[8,128,2048]{2,1,0:T(8,128)(2,1)} %bitcast.120, f32[2048]{0:T(1024)S(1)} %bitcast.132, f32[2048]{0:T(1024)S(1)} %bitcast.130, f32[128]{0:T(128)S(1)} %add_rsqrt_fusion.4, f32[128]{0:T(128)S(1)} %broadcast_multiply_fusion.1, ...), kind=kOutput, calls=%fused_computation.47 | convolution fusion | flops 538704896 | bytes 5264384 | tf_op jit(solution)/shard_map/dot_general | solution.py:23
  48.6 0.9 copy.33.ck
  49.5 3.8 %fusion.16.cv = bf16[128,1024]{1,0:T(8,128)(2,1)} fusion(bf16[3,2048,1024]{2,1,0:T(8,128)(2,1)} %bitcast.113, bf16[1,1,128,2048]{3,2,1,0:T(8,128)(2,1)S(1)} %copy-done.9, f32[2048]{0:T(1024)S(1)} %bitcast.133, f32[2048]{0:T(1024)S(1)} %bitcast.131, f32[128]{0:T(128)S(1)} %add_rsqrt_fusion.4, f32[128]{0:T(128)S(1)} %broadcast_multiply_fusion.1), kind=kOutput, calls=%fused_computation.29 | convolution fusion | flops 538574848 | bytes 4998144 | tf_op jit(solution)/shard_map/dot_general | solution.py:23
  53.3 0.1 fusion.31
  53.3 0.0 copy-start.12
  53.4 0.0 copy-done.4
  53.4 0.2 convert_reduce_fusion
  53.6 0.4 fusion.12
  54.0 0.5 fusion.10
  54.6 0.0 copy-start.10
  54.6 3.8 %fusion.1.k = f32[256,1024]{1,0:T(8,128)S(1)} fusion(bf16[256,2048]{1,0:T(8,128)(2,1)S(1)} %bitcast.124, bf16[3,2048,1024]{2,1,0:T(8,128)(2,1)} %bitcast.114), kind=kOutput, calls=%fused_computation.3 | convolution fusion | flops 1073741824 | bytes 6291456 | tf_op jit(solution)/shard_map/dot_general | solution.py:23
  58.4 0.0 copy-done.10
  58.4 0.0 copy-start.5
  58.4 0.1 multiply_bitcast_fusion
  58.5 1.2 copy.37
  59.7 1.6 reduce_sum.69
  61.3 0.1 copy.30
  61.4 0.1 copy.31
  61.5 1.3 mul.156
  62.8 3.8 %fusion.q = f32[256,1024]{1,0:T(8,128)S(1)} fusion(bf16[256,2048]{1,0:T(8,128)(2,1)} %bitcast.125, bf16[3,2048,1024]{2,1,0:T(8,128)(2,1)} %bitcast.115), kind=kOutput, calls=%fused_computation.1 | convolution fusion | flops 1073741824 | bytes 6291456 | tf_op jit(solution)/shard_map/dot_general | solution.py:23
  66.6 0.0 copy-start.6
  66.6 0.1 multiply_bitcast_fusion.1
  66.7 1.3 copy.35
  68.0 0.0 copy-done.6
  68.0 1.6 reduce_sum.68
  69.6 0.1 copy.28
  69.6 0.1 copy.29
  69.8 0.3 mul.151
  70.1 0.0 copy-done.5
  70.1 0.0 copy-start.11
  70.1 3.1 %fusion.24 = (bf16[256,1024]{1,0:T(8,128)(2,1)}, bf16[256,1024]{1,0:T(8,128)(2,1)}) fusion(f32[256,1024]{1,0:T(8,128)S(1)} %fusion.1.k, f32[32,8,8,128]{3,2,1,0:T(8,128)} %bitcast.118, f32[256,1024]{1,0:T(8,128)} %copy-done.6, f32[32,8,8,128]{3,2,1,0:T(8,128)S(1)} %bitcast.119), kind=kLoop, calls=%fused_computation.38 | loop fusion | flops 1048576 | bytes 5242880 | tf_op jit(solution)/shard_map/convert_element_type | solution.py:610
  73.2 4.4 %fusion.15.v = bf16[256,1024]{1,0:T(8,128)(2,1)} fusion(bf16[256,2048]{1,0:T(8,128)(2,1)S(1)} %bitcast.126, bf16[3,2048,1024]{2,1,0:T(8,128)(2,1)} %bitcast.116), kind=kOutput, calls=%fused_computation.27 | convolution fusion | flops 1074003968 | bytes 5767168 | tf_op jit(solution)/shard_map/dot_general | solution.py:23
  77.6 0.0 copy-done.7
  77.6 1.5 fusion.13
  79.1 1.0 copy-done.8
  80.1 0.3 copy-done.16
  80.4 2.1 convolution_convert_fusion.do
  82.6 49.4 %spread.1 = (bf16[32,2,128,128]{3,2,1,0:T(8,128)(2,1)}, bf16[8,4,256,128]{3,2,1,0:T(8,128)(2,1)}) custom-call(bf16[128,1024]{1,0:T(8,128)(2,1)} %copy.33.ck, bf16[128,1024]{1,0:T(8,128)(2,1)} %fusion.16.cv, bf16[256,1024]{1,0:T(8,128)(2,1)} %get-tuple-element.32.qn, bf16[256,1024]{1,0:T(8,128)(2,1)} %get-tuple-element.31.kn, bf16[256,1024]{1,0:T(8,128)(2,1)} %fusion.15.v, ...), custom_call_target="tpu_custom_call" | custom-call | tf_op jit(solution)/shard_map/spread/pallas_call | solution.py:129
  132.0 1.6 copy-done.2
  133.6 1.6 copy-done.3
  135.2 30.7 %attend.1.res = bf16[8,4,256,128]{3,2,1,0:T(8,128)(2,1)S(1)} custom-call(s32[8]{0:T(128)S(1)} %fusion.33.frames, s32[8]{0:T(128)S(1)} %reshape_squeeze.3.starts, f32[1]{0:T(128)S(6)} %div.57.temp, bf16[32,2,128,128]{3,2,1,0:T(8,128)(2,1)S(1)} %copy-done.2, bf16[8,4,256,128]{3,2,1,0:T(8,128)(2,1)S(1)} %copy-done.3), custom_call_target="tpu_custom_call" | custom-call | tf_op jit(solution)/shard_map/attend/pallas_call | solution.py:219
  166.0 1.3 copy-done.1
  167.3 91.2 %close.1 = (bf16[256,2048]{1,0:T(8,128)(2,1)}, bf16[3,64,256]{2,1,0:T(8,128)(2,1)}, bf16[32,512]{1,0:T(8,128)(2,1)}) custom-call(bf16[8,4,256,128]{3,2,1,0:T(8,128)(2,1)} %copy-done.1, bf16[256,2048]{1,0:T(8,128)(2,1)} %get-tuple-element.29.hidden, bf16[256,2048]{1,0:T(8,128)(2,1)} %copy-done.8, f32[256,1024]{1,0:T(8,128)} %copy-done.6, ...), custom_call_target="tpu_custom_call" | custom-call | tf_op jit(solution)/shard_map/close/pallas_call | solution.py:535
  258.5 2.3 copy.50
  260.9 0.0 copy-done.13
  260.9 0.6 copy.51
  261.5 0.0 copy-done.14
  261.5 0.6 copy.52
  (26 shorter events, 0.2 us)
Async XLA Ops:
  0.6 40.7 %copy-start = (f32[18,3,2048]{2,1,0:T(4,128)S(1)}, f32[18,3,2048]{2,1,0:T(4,128)}, u32[]{:S(2)}) copy-start(f32[18,3,2048]{2,1,0:T(4,128)} %param.19) | copy-start | bytes 1327108
  31.6 6.6 %copy-start.15 = (s32[1,1,2]{2,1,0:T(1,128)S(1)}, s32[1,1,2]{2,1,0:T(1,128)}, u32[]{:S(2)}) copy-start(s32[1,1,2]{2,1,0:T(1,128)} %param.14) | copy-start | bytes 28
  31.6 12.9 %copy-start.9 = (bf16[1,1,128,2048]{3,2,1,0:T(8,128)(2,1)S(1)}, bf16[1,1,128,2048]{3,2,1,0:T(8,128)(2,1)}, u32[]{:S(2)}) copy-start(bf16[1,1,128,2048]{3,2,1,0:T(8,128)(2,1)} %param.12) | copy-start | bytes 1572868
  49.5 3.9 %copy-start.4 = (bf16[1,1,2,128,2048]{4,3,2,1,0:T(8,128)(2,1)S(1)}, bf16[1,1,2,128,2048]{4,3,2,1,0:T(8,128)(2,1)}, u32[]{:S(2)}) copy-start(bf16[1,1,2,128,2048]{4,3,2,1,0:T(8,128)(2,1)} %param.11) | copy-start | bytes 3145732
  53.3 24.3 %copy-start.12 = (f32[2,2048]{1,0:T(2,128)}, f32[2,2048]{1,0:T(2,128)S(1)}, u32[]{:S(2)}) copy-start(f32[2,2048]{1,0:T(2,128)S(1)} %get-tuple-element.17.scale1) | copy-start | bytes 49156
  54.6 3.8 %copy-start.10 = (bf16[2,128,2048]{2,1,0:T(8,128)(2,1)}, bf16[2,128,2048]{2,1,0:T(8,128)(2,1)S(1)}, u32[]{:S(2)}) copy-start(bf16[2,128,2048]{2,1,0:T(8,128)(2,1)S(1)} %fusion.10) | copy-start | bytes 3145732
  58.4 11.7 %copy-start.5 = (f32[256,1024]{1,0:T(8,128)}, f32[256,1024]{1,0:T(8,128)S(1)}, u32[]{:S(2)}) copy-start(f32[256,1024]{1,0:T(8,128)S(1)} %fusion.1.k) | copy-start | bytes 3145732
  66.6 1.4 copy-start.6
  70.1 3.1 %copy-start.11 = (bf16[2,128,2048]{2,1,0:T(8,128)(2,1)S(1)}, bf16[2,128,2048]{2,1,0:T(8,128)(2,1)}, u32[]{:S(2)}) copy-start(bf16[2,128,2048]{2,1,0:T(8,128)(2,1)} %copy-done.10) | copy-start | bytes 3145732
  73.2 4.4 %copy-start.7 = (bf16[1,1,2,128,2048]{4,3,2,1,0:T(8,128)(2,1)S(1)}, bf16[1,1,2,128,2048]{4,3,2,1,0:T(8,128)(2,1)}, u32[]{:S(2)}) copy-start(bf16[1,1,2,128,2048]{4,3,2,1,0:T(8,128)(2,1)} %param.21) | copy-start | bytes 3145732
  77.6 2.8 %copy-start.16 = (bf16[1024,2048]{1,0:T(8,128)(2,1)S(1)}, bf16[1024,2048]{1,0:T(8,128)(2,1)}, u32[]{:S(2)}) copy-start(bf16[1024,2048]{1,0:T(8,128)(2,1)} %param.17) | copy-start | bytes 12582916
  79.1 1.0 copy-start.8
  132.0 1.6 copy-start.2
  133.6 1.6 copy-start.3
  165.9 1.3 copy-start.1
  258.5 2.4 copy-start.13
  258.5 3.0 %copy-start.14 = (bf16[32,512]{1,0:T(8,128)(2,1)S(1)}, bf16[32,512]{1,0:T(8,128)(2,1)}, u32[]{:S(2)}) copy-start(bf16[32,512]{1,0:T(8,128)(2,1)} %get-tuple-element.38) | copy-start | bytes 98308

commit v3 on v2

--- a/solution.py
+++ b/solution.py
@@ -25,18 +25,6 @@
     )
 
 
-def layer_norm(values):
-    center = values - jnp.mean(values, axis=-1, keepdims=True)
-    return center * lax.rsqrt(jnp.mean(center * center, axis=-1, keepdims=True) + EPS)
-
-
-def head_norm(values):
-    count = values.shape[0]
-    split = values.reshape(count, HEADS, HD)
-    factor = lax.rsqrt(jnp.mean(split * split, axis=-1, keepdims=True) + EPS)
-    return (split * factor).reshape(count, -1)
-
-
 def lanes(start, size):
     return pl.ds(pl.multiple_of(start, 128), size)
 
@@ -57,155 +45,304 @@
     return ((h // 2) * 4 + x) * 2 + h % 2
 
 
-def shifted(t, s):
-    y, x, z = place(t)
-    dy, dx, dz = place(s)
-    return (((y + dy) % 4) * 4 + (x + dx) % 4) * 2 + (z + dz) % 2
-
-
-def spread_kernel(ck, cv, qn, kn, v, do, kv_ref, own_ref, sems):
-    me = lax.axis_index("tm")
-    y, x, z = place(me)
-    slot = y * 2 + z
+def open_kernel(
+    level, action, start, noisy, clean, grad, noise, acts, w3, w_out,
+    kv, own, stretch, hidden, gz, q, k, scale1,
+    clean_hidden, ckv, out, tile, w, wo,
+    w_sems, kv_sems, x_sems, own_sems, start_sems, local_sems,
+):
+    t = lax.axis_index("tm")
+    d = lax.axis_index("dp")
+    y, x, zh = place(t)
+    slot = y * 2 + zh
+    loads = [
+        pltpu.make_async_copy(w3.at[1], w.at[1], w_sems.at[1]),
+        pltpu.make_async_copy(w3.at[2], w.at[2], w_sems.at[2]),
+        pltpu.make_async_copy(w3.at[0], w.at[0], w_sems.at[0]),
+        pltpu.make_async_copy(w_out, wo, w_sems.at[3]),
+    ]
+    for load in loads:
+        load.start()
+
+    def peer(h):
+        return {"dp": d, "tm": head_home(h, x)}
+
+    def beside(step):
+        return {"dp": d, "tm": (y * 4 + (x + step) % 4) * 2 + zh}
+
     barrier = pltpu.get_barrier_semaphore()
 
     def greet(s, carry):
         pl.semaphore_signal(
-            barrier, inc=1, device_id={"tm": shifted(me, s)}, device_id_type=MESH
+            barrier, inc=1, device_id=peer((slot + s) % 8), device_id_type=MESH
         )
         return carry
 
-    lax.fori_loop(1, 32, greet, 0)
-    pl.semaphore_wait(barrier, 31)
+    lax.fori_loop(1, 8, greet, 0)
+    for step in (1, 2, 3):
+        pl.semaphore_signal(barrier, inc=1, device_id=beside(step), device_id_type=MESH)
+
+    def remote(src, dst, sems, device):
+        return pltpu.make_async_remote_copy(
+            src_ref=src,
+            dst_ref=dst,
+            send_sem=sems.at[0],
+            recv_sem=sems.at[1],
+            device_id=device,
+            device_id_type=MESH,
+        )
+
+    def modulated(values, shift, scale):
+        center = values - jnp.mean(values, axis=1, keepdims=True)
+        factor = lax.rsqrt(jnp.mean(center * center, axis=1, keepdims=True) + EPS)
+        return (center * factor * scale + shift).astype(BF)
+
+    act = acts[action[0]]
+    clean_shift = noise[0, 0:1, :] + act[0:1]
+    clean_scale = 1.0 + (noise[1, 0:1, :] + act[1:2])
+
+    def clean_rows(n, carry):
+        cut = rows_of(n * 16, 16)
+        clean_hidden[cut, :] = modulated(clean[cut, :].astype(F32), clean_shift, clean_scale)
+        return carry
+
+    lax.fori_loop(0, 8, clean_rows, 0, unroll=2)
+
+    def normed(u):
+        factor = lax.rsqrt(jnp.mean(u * u, axis=1, keepdims=True) + EPS)
+        return (u * factor).astype(BF)
+
+    def clean_keys(m, carry):
+        u = dot(clean_hidden[...], w[1, :, lanes(m * 256, 256)], 1, 0)
+        for i in range(2):
+            ckv[2 * m + i, 0] = normed(u[:, i * HD : (i + 1) * HD])
+        return carry
+
+    def clean_vals(m, carry):
+        u = dot(clean_hidden[...], w[2, :, lanes(m * 256, 256)], 1, 0).astype(BF)
+        for i in range(2):
+            ckv[2 * m + i, 1] = u[:, i * HD : (i + 1) * HD]
+        return carry
+
+    tile[...] = jnp.full((8, 128), start[0], jnp.int32)
+    loads[0].wait()
+    lax.fori_loop(0, 4, clean_keys, 0)
+    loads[1].wait()
+    lax.fori_loop(0, 4, clean_vals, 0)
+
+    pl.semaphore_wait(barrier, 10)
 
     def send_kv(s, carry):
-        t = shifted(me, s)
-        ty, _, tz = place(t)
-        cut = lanes((ty * 2 + tz) * HD, HD)
-        for part, ref in enumerate((ck, cv)):
-            pltpu.make_async_remote_copy(
-                src_ref=ref.at[:, cut],
-                dst_ref=kv_ref.at[me, part],
-                send_sem=sems.at[0],
-                recv_sem=sems.at[1],
-                device_id={"tm": t},
-                device_id_type=MESH,
-            ).start()
-        return carry
-
-    def send_own(s, carry):
         h = (slot + s) % 8
-        cut = lanes(h * HD, HD)
-        for part, ref in enumerate((qn, kn, v, do)):
-            pltpu.make_async_remote_copy(
-                src_ref=ref.at[:, cut],
-                dst_ref=own_ref.at[slot, part],
-                send_sem=sems.at[2],
-                recv_sem=sems.at[3],
-                device_id={"tm": head_home(h, x)},
-                device_id_type=MESH,
-            ).start()
-        return carry
-
-    lax.fori_loop(1, 32, send_kv, 0)
-    lax.fori_loop(1, 8, send_own, 0)
-    cut = lanes(slot * HD, HD)
-    for part, ref in enumerate((ck, cv)):
-        pltpu.make_async_copy(ref.at[:, cut], kv_ref.at[me, part], sems.at[4]).start()
-    for part, ref in enumerate((qn, kn, v, do)):
-        pltpu.make_async_copy(ref.at[:, cut], own_ref.at[slot, part], sems.at[5]).start()
-    wait_bytes(kv_ref.at[0], sems.at[4])
-    wait_bytes(own_ref.at[0], sems.at[5])
-    wait_bytes(kv_ref.at[pl.ds(0, 31)], sems.at[0])
-    wait_bytes(own_ref.at[pl.ds(0, 7)], sems.at[2])
-    wait_bytes(kv_ref.at[pl.ds(0, 31)], sems.at[1])
-    wait_bytes(own_ref.at[pl.ds(0, 7)], sems.at[3])
-
-
-def spread(ck, cv, qn, kn, v, do):
-    frames = 32
-    tokens = ck.shape[0]
-    rows = qn.shape[0]
+        remote(ckv.at[h], kv.at[y, x, zh], kv_sems, peer(h)).start()
+        remote(tile, stretch.at[slot], start_sems, peer(h)).start()
+        return carry
+
+    lax.fori_loop(1, 8, send_kv, 0)
+    mine = [
+        pltpu.make_async_copy(ckv.at[slot], kv.at[y, x, zh], local_sems.at[0]),
+        pltpu.make_async_copy(tile, stretch.at[slot], local_sems.at[1]),
+    ]
+    for copy in mine:
+        copy.start()
+
+    for j in range(2):
+        row = pl.ds(level[j], 1)
+        shift = noise[0, row, :] + act[0:1]
+        scale = 1.0 + (noise[1, row, :] + act[1:2])
+        gate = noise[2, row, :] + act[2:3]
+        scale1[j : j + 1, :] = scale
+
+        def noisy_rows(n, carry):
+            cut = rows_of((j * 8 + n) * 16, 16)
+            hidden[cut, :] = modulated(noisy[cut, :].astype(F32), shift, scale)
+            gz[cut, :] = (gate * grad[cut, :].astype(F32)).astype(BF)
+            return carry
+
+        lax.fori_loop(0, 8, noisy_rows, 0, unroll=2)
+
+    loads[2].wait()
+    loads[3].wait()
+
+    def project(i, carry):
+        m = (slot // 2 + 1 + i) % 4
+        cut = lanes(m * 256, 256)
+        uk = dot(hidden[...], w[1, :, cut], 1, 0)
+        uv = dot(hidden[...], w[2, :, cut], 1, 0).astype(BF)
+        uq = dot(hidden[...], w[0, :, cut], 1, 0)
+        um = dot(gz[...], wo[rows_of(m * 256, 256), :], 1, 1).astype(BF)
+        k[:, cut] = uk
+        q[:, cut] = uq
+        for a in range(2):
+            part = slice(a * HD, (a + 1) * HD)
+            out[2 * m + a, 0] = normed(uq[:, part])
+            out[2 * m + a, 1] = normed(uk[:, part])
+            out[2 * m + a, 2] = uv[:, part]
+            out[2 * m + a, 3] = um[:, part]
+        return carry
+
+    def send_own(h):
+        remote(out.at[h], own.at[slot], own_sems, peer(h)).start()
+
+    def send_pair(i):
+        m = (slot // 2 + 1 + i) % 4
+        send_own(2 * m)
+        send_own(2 * m + 1)
+
+    project(0, 0)
+    send_pair(0)
+    for copy in mine:
+        copy.wait()
+    wait_bytes(ckv.at[pl.ds(0, 7)], kv_sems.at[1])
+    for step in (1, 3, 2):
+        remote(kv.at[:, x], kv.at[:, x], x_sems, beside(step)).start()
+
+    def project_send(i, carry):
+        project(i, carry)
+        send_pair(i)
+        return carry
+
+    lax.fori_loop(1, 3, project_send, 0)
+    project(3, 0)
+    send_own(slot + 1 - 2 * (slot % 2))
+    last = pltpu.make_async_copy(out.at[slot], own.at[slot], local_sems.at[2])
+    last.start()
+    last.wait()
+    for way in (0, 1):
+        wait_bytes(stretch.at[pl.ds(0, 7)], start_sems.at[way])
+        wait_bytes(kv.at[:, pl.ds(0, 3)], x_sems.at[way])
+        wait_bytes(own.at[pl.ds(0, 7)], own_sems.at[way])
+    wait_bytes(ckv.at[pl.ds(0, 7)], kv_sems.at[0])
+
+
+def open_up(level, action, start, noisy, clean, grad, noise, acts, w3, w_out):
+    rows, model = noisy.shape
+    tokens = clean.shape[0]
+    width = w_out.shape[0]
+    vmem = pl.BlockSpec(memory_space=pltpu.VMEM)
+    smem = pl.BlockSpec(memory_space=pltpu.SMEM)
     return pl.pallas_call(
-        spread_kernel,
+        open_kernel,
         out_shape=(
-            jax.ShapeDtypeStruct((frames, 2, tokens, HD), BF),
+            jax.ShapeDtypeStruct((4, 4, 2, 2, tokens, HD), BF),
             jax.ShapeDtypeStruct((8, 4, rows, HD), BF),
+            jax.ShapeDtypeStruct((8, 8, 128), jnp.int32),
+            jax.ShapeDtypeStruct((rows, model), BF),
+            jax.ShapeDtypeStruct((rows, model), BF),
+            jax.ShapeDtypeStruct((rows, width), F32),
+            jax.ShapeDtypeStruct((rows, width), F32),
+            jax.ShapeDtypeStruct((2, model), F32),
         ),
-        in_specs=[ANY] * 6,
-        out_specs=(ANY, ANY),
-        scratch_shapes=[pltpu.SemaphoreType.DMA((6,))],
-        compiler_params=pltpu.CompilerParams(collective_id=0, has_side_effects=True),
-        name="spread",
-    )(ck, cv, qn, kn, v, do)
-
-
-def attend_kernel(frames, starts, temp, kv, own, out, s_scr):
+        in_specs=[smem] * 3 + [vmem] * 5 + [ANY] * 2,
+        out_specs=(ANY, ANY, ANY) + (vmem,) * 5,
+        scratch_shapes=[
+            pltpu.VMEM((tokens, model), BF),
+            pltpu.VMEM((8, 2, tokens, HD), BF),
+            pltpu.VMEM((8, 4, rows, HD), BF),
+            pltpu.VMEM((8, 128), jnp.int32),
+            pltpu.VMEM(w3.shape, BF),
+            pltpu.VMEM(w_out.shape, BF),
+            pltpu.SemaphoreType.DMA((4,)),
+            pltpu.SemaphoreType.DMA((2,)),
+            pltpu.SemaphoreType.DMA((2,)),
+            pltpu.SemaphoreType.DMA((2,)),
+            pltpu.SemaphoreType.DMA((2,)),
+            pltpu.SemaphoreType.DMA((3,)),
+        ],
+        compiler_params=pltpu.CompilerParams(
+            collective_id=0, has_side_effects=True, vmem_limit_bytes=60 * 1024 * 1024
+        ),
+        name="open",
+    )(level, action, start, noisy, clean, grad, noise, acts, w3, w_out)
+
+
+def attend_kernel(starts, temps, kv, own, out, s_scr):
     i = pl.program_id(0)
-    g = frames[i]
+    y, x, zh = place(lax.axis_index("tm"))
+    g = (i // 2) * 8 + x * 2 + i % 2
     st = starts[i]
     n = g - st
-    odd = n % 2
-    pairs = n // 2
-    first = st + odd
-    scale = temp[0]
+    rest = n % 4
+    steps = n // 4
+    first = st + rest
+    scale = temps[y * 2 + zh] * (1.0 / math.sqrt(HD))
     c2 = scale * LOG2E
     q = own[0, 0]
     ko = own[0, 1]
     vo = own[0, 2]
     do = own[0, 3]
-    k_odd = kv[st, 0]
-    v_odd = kv[st, 1]
     h = HD
+    near = jnp.minimum(st, 29)
+    k_near = kv[pl.ds(near, 3), 0].reshape(3 * h, h)
+    v_near = kv[pl.ds(near, 3), 1].reshape(3 * h, h)
+
+    def keys(c, part):
+        return kv[pl.ds(first + 4 * c, 4), part].reshape(4 * h, h)
+
+    def widest(s):
+        top = s[:, :h]
+        for b in range(1, s.shape[1] // h):
+            top = jnp.maximum(top, s[:, b * h : (b + 1) * h])
+        return top
+
+    def folded(p):
+        total = p[:, :h]
+        for b in range(1, p.shape[1] // h):
+            total = total + p[:, b * h : (b + 1) * h]
+        return total
 
     s_own = jnp.concatenate([dot(q[:h], ko[:h], 1, 1), dot(q[h:], ko[h:], 1, 1)], 0)
-    s_odd = jnp.where(odd == 1, dot(q, k_odd, 1, 1), NEG)
-    s_scr[0, :, :h] = s_own
-    s_scr[0, :, h:] = s_odd
+    s_near = dot(q, k_near, 1, 1)
+    s_near = jnp.concatenate(
+        [
+            jnp.where(
+                (near + b >= st) & (near + b < first), s_near[:, b * h : (b + 1) * h], NEG
+            )
+            for b in range(3)
+        ],
+        1,
+    )
 
     def scores(c, top):
-        k = kv[pl.ds(first + 2 * c, 2), 0].reshape(2 * h, h)
-        s = dot(q, k, 1, 1)
-        s_scr[c + 1] = s
-        return jnp.maximum(top, jnp.maximum(s[:, :h], s[:, h:]))
-
-    top = lax.fori_loop(0, pairs, scores, jnp.maximum(s_own, s_odd))
+        s = dot(q, keys(c, 0), 1, 1)
+        s_scr[c] = s
+        return jnp.maximum(top, widest(s))
+
+    top = lax.fori_loop(0, steps, scores, jnp.maximum(s_own, widest(s_near)))
     m2 = jnp.max(top, axis=1, keepdims=True) * c2
 
     p_own = jnp.exp2(s_own * c2 - m2)
-    p_odd = jnp.exp2(s_odd * c2 - m2)
+    p_near = jnp.exp2(s_near * c2 - m2)
     pb_own = p_own.astype(BF)
     acc = jnp.concatenate([dot(pb_own[:h], vo[:h], 1, 0), dot(pb_own[h:], vo[h:], 1, 0)], 0)
-    acc = acc + dot(p_odd.astype(BF), v_odd, 1, 0)
+    acc = acc + dot(p_near.astype(BF), v_near, 1, 0)
 
     def weigh(c, carry):
         acc, total = carry
-        p = jnp.exp2(s_scr[c + 1] * c2 - m2)
-        s_scr[c + 1] = p
-        v = kv[pl.ds(first + 2 * c, 2), 1].reshape(2 * h, h)
-        return acc + dot(p.astype(BF), v, 1, 0), total + p[:, :h] + p[:, h:]
-
-    acc, total = lax.fori_loop(0, pairs, weigh, (acc, p_own + p_odd))
+        p = jnp.exp2(s_scr[c] * c2 - m2)
+        s_scr[c] = p
+        return acc + dot(p.astype(BF), keys(c, 1), 1, 0), total + folded(p)
+
+    acc, total = lax.fori_loop(0, steps, weigh, (acc, p_own + folded(p_near)))
     inv = 1.0 / jnp.sum(total, axis=1, keepdims=True)
     mixed = acc * inv
     delta = jnp.sum(mixed * do.astype(F32), axis=1, keepdims=True)
     out[0, 0] = mixed.astype(BF)
 
     dp_own = jnp.concatenate([dot(do[:h], vo[:h], 1, 1), dot(do[h:], vo[h:], 1, 1)], 0)
-    ds_own = (p_own * (dp_own - delta)).astype(BF)
-    ds_odd = (p_odd * (dot(do, v_odd, 1, 1) - delta)).astype(BF)
-    dq = jnp.concatenate([dot(ds_own[:h], ko[:h], 1, 0), dot(ds_own[h:], ko[h:], 1, 0)], 0)
-    dq = dq + dot(ds_odd, k_odd, 1, 0)
+    ds_own = p_own * (dp_own - delta)
+    ds_near = (p_near * (dot(do, v_near, 1, 1) - delta)).astype(BF)
+    db_own = ds_own.astype(BF)
+    dq = jnp.concatenate([dot(db_own[:h], ko[:h], 1, 0), dot(db_own[h:], ko[h:], 1, 0)], 0)
+    dq = dq + dot(ds_near, k_near, 1, 0)
 
     def pull(c, dq):
-        k = kv[pl.ds(first + 2 * c, 2), 0].reshape(2 * h, h)
-        v = kv[pl.ds(first + 2 * c, 2), 1].reshape(2 * h, h)
-        ds = s_scr[c + 1] * (dot(do, v, 1, 1) - delta)
-        return dq + dot(ds.astype(BF), k, 1, 0)
-
-    dq = lax.fori_loop(0, pairs, pull, dq)
+        ds = s_scr[c] * (dot(do, keys(c, 1), 1, 1) - delta)
+        return dq + dot(ds.astype(BF), keys(c, 0), 1, 0)
+
+    dq = lax.fori_loop(0, steps, pull, dq)
     out[0, 1] = (dq * (inv * scale)).astype(BF)
-    dsn = (p_own * (dp_own - delta) * (inv * scale)).astype(BF)
+    dsn = (ds_own * (inv * scale)).astype(BF)
     pn = (p_own * inv).astype(BF)
     for j in range(2):
         cut = slice(j * h, (j + 1) * h)
@@ -213,7 +350,7 @@
         out[0, 3, cut] = dot(pn[cut], do[cut], 0, 0).astype(BF)
 
 
-def attend(frames, starts, temp, kv, own):
+def attend(starts, temps, kv, own):
     rows = own.shape[2]
     smem = pl.BlockSpec(memory_space=pltpu.SMEM)
     return pl.pallas_call(
@@ -223,15 +360,14 @@
         in_specs=[
             smem,
             smem,
-            smem,
             pl.BlockSpec(kv.shape, lambda i: (0, 0, 0, 0)),
             pl.BlockSpec((1, 4, rows, HD), lambda i: (i, 0, 0, 0)),
         ],
         out_specs=pl.BlockSpec((1, 4, rows, HD), lambda i: (i, 0, 0, 0)),
-        scratch_shapes=[pltpu.VMEM((17, rows, 2 * HD), F32)],
+        scratch_shapes=[pltpu.VMEM((8, rows, 4 * HD), F32)],
         compiler_params=pltpu.CompilerParams(vmem_limit_bytes=40 * 1024 * 1024),
         name="attend",
-    )(frames, starts, temp, kv, own)
+    )(starts, temps, kv, own)
 
 
 ORDERS = (("x", "y", "z"), ("y", "z", "x"), ("z", "x", "y"))
@@ -574,59 +710,24 @@
 ):
     tokens, model = noisy.shape[3:]
     rows = 2 * tokens
-    t = lax.axis_index("tm")
-    y, x, z = place(t)
-    starts_all = lax.all_gather(starts.reshape(1), "tm", axis=0, tiled=True)
     w3 = w_qkv.transpose(1, 0, 2)
-
-    def pick(table, index):
-        return lax.dynamic_index_in_dim(table, index, 0, keepdims=False)
-
-    action_mod = pick(action_table, actions[0, 0])
-    clean_mod = noise_table[0] + action_mod
-    mods = jnp.stack([pick(noise_table, levels[0, 0, j]) + action_mod for j in range(2)])
-
-    def spread_rows(part):
-        return jnp.broadcast_to(mods[:, None, part, :], (2, tokens, model)).reshape(rows, model)
-
-    shift, scale, gate = spread_rows(0), spread_rows(1), spread_rows(2)
-
-    clean_rows = clean.reshape(tokens, model).astype(F32)
-    clean_hidden = (layer_norm(clean_rows) * (1.0 + clean_mod[1]) + clean_mod[0]).astype(BF)
-    ckn = head_norm(dot(clean_hidden, w3[1], 1, 0)).astype(BF)
-    cv = dot(clean_hidden, w3[2], 1, 0).astype(BF)
-
-    noisy_rows = noisy.reshape(rows, model).astype(F32)
-    grad_rows = out_grad.reshape(rows, model).astype(F32)
-
-    def front(values):
-        return (layer_norm(values) * (1.0 + scale) + shift).astype(BF)
-
-    hidden = front(noisy_rows)
-    q = dot(hidden, w3[0], 1, 0)
-    k = dot(hidden, w3[1], 1, 0)
-    v = dot(hidden, w3[2], 1, 0).astype(BF)
-    qn = head_norm(q).astype(BF)
-    kn = head_norm(k).astype(BF)
-    grad_z = (gate * grad_rows).astype(BF)
-    grad_mixed = dot(grad_z, w_out, 1, 1).astype(BF)
-
-    kv, own = spread(ckn, cv, qn, kn, v, grad_mixed)
-    slots = jnp.arange(8, dtype=jnp.int32)
-    my_frames = (slots // 2) * 8 + x * 2 + slots % 2
-    my_starts = starts_all.reshape(4, 4, 2)[:, x].reshape(8)
-    temp = (pick(temps, y * 2 + z) / math.sqrt(HD)).reshape(1)
-    res = attend(my_frames, my_starts, temp, kv, own)
+    noisy_rows = noisy.reshape(rows, model)
+    grad_rows = out_grad.reshape(rows, model)
+    kv, own, stretch, hidden, grad_z, q, k, scale1 = open_up(
+        levels.reshape(2),
+        actions.reshape(1),
+        starts.reshape(1),
+        noisy_rows,
+        clean.reshape(tokens, model),
+        grad_rows,
+        noise_table.transpose(1, 0, 2),
+        action_table,
+        w3,
+        w_out,
+    )
+    res = attend(stretch[:, 0, 0], temps, kv.reshape(32, 2, tokens, HD), own)
     grad_noisy, total_g, total_o = close(
-        res,
-        hidden,
-        grad_z,
-        q,
-        k,
-        noisy.reshape(rows, model),
-        out_grad.reshape(rows, model),
-        1.0 + mods[:, 1, :],
-        w3,
+        res, hidden, grad_z, q, k, noisy_rows, grad_rows, scale1, w3
     )
     return (grad_noisy.reshape(noisy.shape), total_g.transpose(1, 0, 2), total_o)
 

time: 266 us -> 184 us (0.69); the launches traced: 262 us -> 184 us
  blocking collectives: 21.6 us -> 0 us
  matrix products: 21.4 us -> 0 us
  local copies, waits for them, and re-layouts: 30 us -> 9.11 us
  other arithmetic: 10.9 us -> 0 us
  between operations: 6.81 us -> 2 us
    unnamed x1 -> x0, blocking collectives: 21.6 us -> none
    dot_general x6 -> x0, matrix products: 21.4 us -> none  [dot(): lax.dot_general(left, right, (((left_dim,), (right_dim,)), ((), ())), pre...]
    pallas_call x1, Pallas kernels: 91.2 us -> 104 us  [close(): pl.pallas_call(close_kernel, out_shape=(jax.ShapeDtypeStruct((rows, model...]
    dot_general x2 -> x0, local copies, waits for them, and re-layouts: 11.1 us -> none  [dot(): lax.dot_general(left, right, (((left_dim,), (right_dim,)), ((), ())), pre...]
    pallas_call x1, Pallas kernels: 30.7 us -> 21.2 us  [attend(): pl.pallas_call(attend_kernel, grid=(8,), out_shape=jax.ShapeDtypeStruct(o...]
    unnamed x42 -> x15, local copies, waits for them, and re-layouts: 14 us -> 8.12 us
    convert_element_type x4 -> x0, other arithmetic: 5.18 us -> none  [the longest x1 3.08 us: on_device(): kn = head_norm(k).astype(BF)]
    reduce_sum x6 -> x0, other arithmetic: 4.22 us -> none  [the longest x2 3.14 us: head_norm(): factor = lax.rsqrt(jnp.mean(split * split, axis=-1, keepdims=True) + EPS)]
where the time goes in v3:
time: 184 us
  Pallas kernels  173 us (94%)
  local copies, waits for them, and re-layouts  9.11 us (5%)
  between operations  2 us (1%)
    pallas_call x1, Pallas kernels, close(): pl.pallas_call(close_kernel, out_shape=(jax.ShapeDtypeStruct((rows, model...  104 us
    pallas_call x1, Pallas kernels, open_up(): pl.pallas_call(open_kernel, out_shape=(jax.ShapeDtypeStruct((4, 4, 2, 2,...  47.3 us
    pallas_call x1, Pallas kernels, attend(): pl.pallas_call(attend_kernel, grid=(8,), out_shape=jax.ShapeDtypeStruct(o...  21.2 us
    unnamed x15, local copies, waits for them, and re-layouts  8.12 us

profile of v3, /device:TPU:0, one launch (start us, length us, event | category | flops | bytes accessed | tf_op | source)
XLA Modules:
  0.0 183.6 jit_solution(8148769028688974348)
XLA Ops:
  1.9 0.0 copy-start.3
  1.9 47.3 %open.1 = (bf16[4,4,2,2,128,128]{5,4,3,2,1,0:T(8,128)(2,1)}, bf16[8,4,256,128]{3,2,1,0:T(8,128)(2,1)}, s32[8,8,128]{2,1,0:T(8,128)}, bf16[256,2048]{1,0:T(8,128)...) custom-call(s32[2]{0:T(128)} %bitcast.24, ...), custom_call_target="tpu_custom_call" | custom-call | tf_op jit(solution)/shard_map/open/pallas_call | solution.py:224
  49.2 1.0 slice_reduce_fusion.starts
  50.2 0.0 copy-done.3
  50.2 0.0 copy-start.1
  50.2 1.6 copy-done.1
  51.8 0.0 copy-start.2
  51.8 1.6 copy-done.2
  53.4 21.2 %attend.1.res = bf16[8,4,256,128]{3,2,1,0:T(8,128)(2,1)S(1)} custom-call(s32[8]{0:T(128)S(1)} %slice_reduce_fusion.starts, f32[8]{0:T(128)S(1)} %copy-done.3, bf16[32,2,128,128]{3,2,1,0:T(8,128)(2,1)S(1)} %bitcast.13, bf16[8,4,256,128]{3,2,1,0:T(8,128)(2,1)S(1)} %copy-done.2), custom_call_target="tpu_custom_call" | custom-call | tf_op jit(solution)/shard_map/attend/pallas_call | solution.py:356
  74.6 0.0 copy-start
  74.6 1.3 copy-done
  76.0 104.0 %close.1 = (bf16[256,2048]{1,0:T(8,128)(2,1)}, bf16[3,64,256]{2,1,0:T(8,128)(2,1)}, bf16[32,512]{1,0:T(8,128)(2,1)}) custom-call(bf16[8,4,256,128]{3,2,1,0:T(8,128)(2,1)} %copy-done, bf16[256,2048]{1,0:T(8,128)(2,1)} %get-tuple-element.17.hidden, bf16[256,2048]{1,0:T(8,128)(2,1)} %get-tuple-element.18.gz, f32[256,1024]{1,0:T(8,128)} %get-tuple-element.19.q, ...), custom_call_target="tpu_custom_call" | custom-call | tf_op jit(solution)/shard_map/close/pallas_call | solution.py:671
  180.0 0.0 copy-start.4
  180.0 0.0 copy-start.5
  180.0 2.3 %copy.19 = bf16[1,1,2,128,2048]{4,3,2,1,0:T(8,128)(2,1)} copy(bf16[1,1,2,128,2048]{4,3,2,1,0:T(8,128)(2,1)} %bitcast.21) | data formatting | bytes 2097152
  182.4 0.0 copy-done.4
  182.4 0.6 copy.20
  183.0 0.0 copy-done.5
  183.0 0.6 copy.21
Async XLA Ops:
  1.9 48.3 %copy-start.3 = (f32[8]{0:T(128)S(1)}, f32[8]{0:T(128)}, u32[]{:S(2)}) copy-start(f32[8]{0:T(128)} %temps.1) | copy-start | bytes 100
  50.2 1.6 copy-start.1
  51.8 1.6 copy-start.2
  74.6 1.3 copy-start
  180.0 2.4 %copy-start.4 = (bf16[3,64,256]{2,1,0:T(8,128)(2,1)S(1)}, bf16[3,64,256]{2,1,0:T(8,128)(2,1)}, u32[]{:S(2)}) copy-start(bf16[3,64,256]{2,1,0:T(8,128)(2,1)} %get-tuple-element.23) | copy-start | bytes 294916
  180.0 3.0 %copy-start.5 = (bf16[32,512]{1,0:T(8,128)(2,1)S(1)}, bf16[32,512]{1,0:T(8,128)(2,1)}, u32[]{:S(2)}) copy-start(bf16[32,512]{1,0:T(8,128)(2,1)} %get-tuple-element.30) | copy-start | bytes 98308

commit v4 on v3

--- a/solution.py
+++ b/solution.py
@@ -47,9 +47,9 @@
 
 def open_kernel(
     level, action, start, noisy, clean, grad, noise, acts, w3, w_out,
-    kv, own, stretch, hidden, gz, q, k, scale1,
-    clean_hidden, ckv, out, tile, w, wo,
-    w_sems, kv_sems, x_sems, own_sems, start_sems, local_sems,
+    temps, got, hidden, gz, q, k, scale1,
+    kv, own, stretch, clean_hidden, ckv, out, tile, w, wo, s_scr, res,
+    w_sems, kv_sems, x_sems, own_sems, start_sems, local_sems, back_sems,
 ):
     t = lax.axis_index("tm")
     d = lax.axis_index("dp")
@@ -82,12 +82,12 @@
     for step in (1, 2, 3):
         pl.semaphore_signal(barrier, inc=1, device_id=beside(step), device_id_type=MESH)
 
-    def remote(src, dst, sems, device):
+    def remote(src, dst, sems, device, arrived=1):
         return pltpu.make_async_remote_copy(
             src_ref=src,
             dst_ref=dst,
             send_sem=sems.at[0],
-            recv_sem=sems.at[1],
+            recv_sem=sems.at[arrived],
             device_id=device,
             device_id_type=MESH,
         )
@@ -181,13 +181,13 @@
             out[2 * m + a, 3] = um[:, part]
         return carry
 
-    def send_own(h):
-        remote(out.at[h], own.at[slot], own_sems, peer(h)).start()
+    def send_own(h, i):
+        remote(out.at[h], own.at[slot], own_sems, peer(h), 1 + i).start()
 
     def send_pair(i):
         m = (slot // 2 + 1 + i) % 4
-        send_own(2 * m)
-        send_own(2 * m + 1)
+        send_own(2 * m, i)
+        send_own(2 * m + 1, i)
 
     project(0, 0)
     send_pair(0)
@@ -204,18 +204,122 @@
 
     lax.fori_loop(1, 3, project_send, 0)
     project(3, 0)
-    send_own(slot + 1 - 2 * (slot % 2))
+    sibling = slot + 1 - 2 * zh
+    send_own(sibling, 3)
     last = pltpu.make_async_copy(out.at[slot], own.at[slot], local_sems.at[2])
     last.start()
     last.wait()
+    wait_bytes(stretch.at[pl.ds(0, 7)], start_sems.at[1])
+    wait_bytes(kv.at[:, pl.ds(0, 3)], x_sems.at[1])
+
+    scale = temps[slot] * (1.0 / math.sqrt(HD))
+    c2 = scale * LOG2E
+    h = HD
+    pair = (0, 1)
+
+    def keys(c, part):
+        return kv[c, :, :, part].reshape(8 * h, h)
+
+    def both(left, right, left_dim, right_dim):
+        return jnp.concatenate(
+            [
+                dot(left[:h], right[:h], left_dim, right_dim),
+                dot(left[h:], right[h:], left_dim, right_dim),
+            ],
+            0,
+        )
+
+    def attend(row):
+        at = [row * 2 + n for n in pair]
+        g = [row * 8 + x * 2 + n for n in pair]
+        st = [stretch[i, 0:1, :] for i in at]
+        qs = [own[i, 0] for i in at]
+        ks = [own[i, 1] for i in at]
+        vs = [own[i, 2] for i in at]
+        ds = [own[i, 3] for i in at]
+        s_own = [both(qs[n], ks[n], 1, 1) for n in pair]
+        top = list(s_own)
+        for c in range(row + 1):
+            for n in pair:
+                s = dot(qs[n], keys(c, 0), 1, 1)
+                for b in range(8):
+                    f = c * 8 + b
+                    seen = (st[n] <= f) & (f < g[n])
+                    sb = s[:, b * h : (b + 1) * h] + jnp.where(seen, 0.0, NEG)
+                    s_scr[n, c, :, b * h : (b + 1) * h] = sb
+                    top[n] = jnp.maximum(top[n], sb)
+        m2 = [jnp.max(top[n], axis=1, keepdims=True) * c2 for n in pair]
+        p_own = [jnp.exp2(s_own[n] * c2 - m2[n]) for n in pair]
+        acc = [both(p_own[n].astype(BF), vs[n], 1, 0) for n in pair]
+        total = list(p_own)
+        for c in range(row + 1):
+            for n in pair:
+                p = jnp.exp2(s_scr[n, c] * c2 - m2[n])
+                s_scr[n, c] = p
+                for b in range(8):
+                    total[n] = total[n] + p[:, b * h : (b + 1) * h]
+                acc[n] = acc[n] + dot(p.astype(BF), keys(c, 1), 1, 0)
+        inv = [1.0 / jnp.sum(total[n], axis=1, keepdims=True) for n in pair]
+        mixed = [acc[n] * inv[n] for n in pair]
+        delta = [jnp.sum(mixed[n] * ds[n].astype(F32), axis=1, keepdims=True) for n in pair]
+        ds_own = [p_own[n] * (both(ds[n], vs[n], 1, 1) - delta[n]) for n in pair]
+        dq = [both(ds_own[n].astype(BF), ks[n], 1, 0) for n in pair]
+        for c in range(row + 1):
+            for n in pair:
+                pull = s_scr[n, c] * (dot(ds[n], keys(c, 1), 1, 1) - delta[n])
+                dq[n] = dq[n] + dot(pull.astype(BF), keys(c, 0), 1, 0)
+        for n in pair:
+            i = at[n]
+            res[i, 0] = mixed[n].astype(BF)
+            res[i, 1] = (dq[n] * (inv[n] * scale)).astype(BF)
+            dsn = (ds_own[n] * (inv[n] * scale)).astype(BF)
+            pn = (p_own[n] * inv[n]).astype(BF)
+            for j in range(2):
+                cut = slice(j * h, (j + 1) * h)
+                res[i, 2, cut] = dot(dsn[cut], qs[n][cut], 0, 0).astype(BF)
+                res[i, 3, cut] = dot(pn[cut], ds[n][cut], 0, 0).astype(BF)
+
+    def send_back(i):
+        remote(res.at[i], got.at[slot], back_sems, peer(i)).start()
+
+    def attend_row(s, carry):
+        row = (y + 3 - s) % 4
+
+        @pl.when(s < 3)
+        def _():
+            wait_bytes(own.at[pl.ds(0, 2)], own_sems.at[1 + s])
+
+        @pl.when(s == 3)
+        def _():
+            wait_bytes(own.at[0], own_sems.at[4])
+
+        for r in range(4):
+
+            @pl.when(row == r)
+            def _():
+                attend(r)
+
+        @pl.when(s < 3)
+        def _():
+            send_back(2 * row)
+            send_back(2 * row + 1)
+
+        return carry
+
+    lax.fori_loop(0, 4, attend_row, 0)
+    send_back(sibling)
+    keep = pltpu.make_async_copy(res.at[slot], got.at[slot], local_sems.at[2])
+    keep.start()
+    keep.wait()
+    wait_bytes(stretch.at[pl.ds(0, 7)], start_sems.at[0])
+    wait_bytes(kv.at[:, pl.ds(0, 3)], x_sems.at[0])
+    wait_bytes(own.at[pl.ds(0, 7)], own_sems.at[0])
+    wait_bytes(ckv.at[pl.ds(0, 7)], kv_sems.at[0])
     for way in (0, 1):
-        wait_bytes(stretch.at[pl.ds(0, 7)], start_sems.at[way])
-        wait_bytes(kv.at[:, pl.ds(0, 3)], x_sems.at[way])
-        wait_bytes(own.at[pl.ds(0, 7)], own_sems.at[way])
-    wait_bytes(ckv.at[pl.ds(0, 7)], kv_sems.at[0])
-
-
-def open_up(level, action, start, noisy, clean, grad, noise, acts, w3, w_out):
+        wait_bytes(res.at[pl.ds(0, 7)], back_sems.at[way])
+
+
+def open_up(level, action, start, noisy, clean, grad, noise, acts, w3, w_out, temps):
     rows, model = noisy.shape
     tokens = clean.shape[0]
     width = w_out.shape[0]
@@ -224,150 +328,40 @@
     return pl.pallas_call(
         open_kernel,
         out_shape=(
-            jax.ShapeDtypeStruct((4, 4, 2, 2, tokens, HD), BF),
             jax.ShapeDtypeStruct((8, 4, rows, HD), BF),
-            jax.ShapeDtypeStruct((8, 8, 128), jnp.int32),
             jax.ShapeDtypeStruct((rows, model), BF),
             jax.ShapeDtypeStruct((rows, model), BF),
             jax.ShapeDtypeStruct((rows, width), F32),
             jax.ShapeDtypeStruct((rows, width), F32),
             jax.ShapeDtypeStruct((2, model), F32),
         ),
-        in_specs=[smem] * 3 + [vmem] * 5 + [ANY] * 2,
-        out_specs=(ANY, ANY, ANY) + (vmem,) * 5,
+        in_specs=[smem] * 3 + [vmem] * 5 + [ANY] * 2 + [smem],
+        out_specs=(ANY,) + (vmem,) * 5,
         scratch_shapes=[
+            pltpu.VMEM((4, 4, 2, 2, tokens, HD), BF),
+            pltpu.VMEM((8, 4, rows, HD), BF),
+            pltpu.VMEM((8, 8, 128), jnp.int32),
             pltpu.VMEM((tokens, model), BF),
             pltpu.VMEM((8, 2, tokens, HD), BF),
             pltpu.VMEM((8, 4, rows, HD), BF),
             pltpu.VMEM((8, 128), jnp.int32),
             pltpu.VMEM(w3.shape, BF),
             pltpu.VMEM(w_out.shape, BF),
+            pltpu.VMEM((2, 4, rows, 8 * HD), F32),
+            pltpu.VMEM((8, 4, rows, HD), BF),
             pltpu.SemaphoreType.DMA((4,)),
             pltpu.SemaphoreType.DMA((2,)),
             pltpu.SemaphoreType.DMA((2,)),
-            pltpu.SemaphoreType.DMA((2,)),
+            pltpu.SemaphoreType.DMA((5,)),
             pltpu.SemaphoreType.DMA((2,)),
             pltpu.SemaphoreType.DMA((3,)),
+            pltpu.SemaphoreType.DMA((2,)),
         ],
         compiler_params=pltpu.CompilerParams(
             collective_id=0, has_side_effects=True, vmem_limit_bytes=60 * 1024 * 1024
         ),
         name="open",
-    )(level, action, start, noisy, clean, grad, noise, acts, w3, w_out)
-
-
-def attend_kernel(starts, temps, kv, own, out, s_scr):
-    i = pl.program_id(0)
-    y, x, zh = place(lax.axis_index("tm"))
-    g = (i // 2) * 8 + x * 2 + i % 2
-    st = starts[i]
-    n = g - st
-    rest = n % 4
-    steps = n // 4
-    first = st + rest
-    scale = temps[y * 2 + zh] * (1.0 / math.sqrt(HD))
-    c2 = scale * LOG2E
-    q = own[0, 0]
-    ko = own[0, 1]
-    vo = own[0, 2]
-    do = own[0, 3]
-    h = HD
-    near = jnp.minimum(st, 29)
-    k_near = kv[pl.ds(near, 3), 0].reshape(3 * h, h)
-    v_near = kv[pl.ds(near, 3), 1].reshape(3 * h, h)
-
-    def keys(c, part):
-        return kv[pl.ds(first + 4 * c, 4), part].reshape(4 * h, h)
-
-    def widest(s):
-        top = s[:, :h]
-        for b in range(1, s.shape[1] // h):
-            top = jnp.maximum(top, s[:, b * h : (b + 1) * h])
-        return top
-
-    def folded(p):
-        total = p[:, :h]
-        for b in range(1, p.shape[1] // h):
-            total = total + p[:, b * h : (b + 1) * h]
-        return total
-
-    s_own = jnp.concatenate([dot(q[:h], ko[:h], 1, 1), dot(q[h:], ko[h:], 1, 1)], 0)
-    s_near = dot(q, k_near, 1, 1)
-    s_near = jnp.concatenate(
-        [
-            jnp.where(
-                (near + b >= st) & (near + b < first), s_near[:, b * h : (b + 1) * h], NEG
-            )
-            for b in range(3)
-        ],
-        1,
-    )
-
-    def scores(c, top):
-        s = dot(q, keys(c, 0), 1, 1)
-        s_scr[c] = s
-        return jnp.maximum(top, widest(s))
-
-    top = lax.fori_loop(0, steps, scores, jnp.maximum(s_own, widest(s_near)))
-    m2 = jnp.max(top, axis=1, keepdims=True) * c2
-
-    p_own = jnp.exp2(s_own * c2 - m2)
-    p_near = jnp.exp2(s_near * c2 - m2)
-    pb_own = p_own.astype(BF)
-    acc = jnp.concatenate([dot(pb_own[:h], vo[:h], 1, 0), dot(pb_own[h:], vo[h:], 1, 0)], 0)
-    acc = acc + dot(p_near.astype(BF), v_near, 1, 0)
-
-    def weigh(c, carry):
-        acc, total = carry
-        p = jnp.exp2(s_scr[c] * c2 - m2)
-        s_scr[c] = p
-        return acc + dot(p.astype(BF), keys(c, 1), 1, 0), total + folded(p)
-
-    acc, total = lax.fori_loop(0, steps, weigh, (acc, p_own + folded(p_near)))
-    inv = 1.0 / jnp.sum(total, axis=1, keepdims=True)
-    mixed = acc * inv
-    delta = jnp.sum(mixed * do.astype(F32), axis=1, keepdims=True)
-    out[0, 0] = mixed.astype(BF)
-
-    dp_own = jnp.concatenate([dot(do[:h], vo[:h], 1, 1), dot(do[h:], vo[h:], 1, 1)], 0)
-    ds_own = p_own * (dp_own - delta)
-    ds_near = (p_near * (dot(do, v_near, 1, 1) - delta)).astype(BF)
-    db_own = ds_own.astype(BF)
-    dq = jnp.concatenate([dot(db_own[:h], ko[:h], 1, 0), dot(db_own[h:], ko[h:], 1, 0)], 0)
-    dq = dq + dot(ds_near, k_near, 1, 0)
-
-    def pull(c, dq):
-        ds = s_scr[c] * (dot(do, keys(c, 1), 1, 1) - delta)
-        return dq + dot(ds.astype(BF), keys(c, 0), 1, 0)
-
-    dq = lax.fori_loop(0, steps, pull, dq)
-    out[0, 1] = (dq * (inv * scale)).astype(BF)
-    dsn = (ds_own * (inv * scale)).astype(BF)
-    pn = (p_own * inv).astype(BF)
-    for j in range(2):
-        cut = slice(j * h, (j + 1) * h)
-        out[0, 2, cut] = dot(dsn[cut], q[cut], 0, 0).astype(BF)
-        out[0, 3, cut] = dot(pn[cut], do[cut], 0, 0).astype(BF)
-
-
-def attend(starts, temps, kv, own):
-    rows = own.shape[2]
-    smem = pl.BlockSpec(memory_space=pltpu.SMEM)
-    return pl.pallas_call(
-        attend_kernel,
-        grid=(8,),
-        out_shape=jax.ShapeDtypeStruct(own.shape, BF),
-        in_specs=[
-            smem,
-            smem,
-            pl.BlockSpec(kv.shape, lambda i: (0, 0, 0, 0)),
-            pl.BlockSpec((1, 4, rows, HD), lambda i: (i, 0, 0, 0)),
-        ],
-        out_specs=pl.BlockSpec((1, 4, rows, HD), lambda i: (i, 0, 0, 0)),
-        scratch_shapes=[pltpu.VMEM((8, rows, 4 * HD), F32)],
-        compiler_params=pltpu.CompilerParams(vmem_limit_bytes=40 * 1024 * 1024),
-        name="attend",
-    )(starts, temps, kv, own)
+    )(level, action, start, noisy, clean, grad, noise, acts, w3, w_out, temps)
 
 
 ORDERS = (("x", "y", "z"), ("y", "z", "x"), ("z", "x", "y"))
@@ -381,18 +375,17 @@
 
 
 def close_kernel(
-    res, hidden, gz, q, k, noisy, grad, scale1, w3,
+    got, hidden, gz, q, k, noisy, grad, scale1, w3,
     out_n, out_g, out_o,
-    got, proj, ph, pm, pp, pz, w, gh,
+    proj, ph, pm, pp, pz, w, gh,
     t0a, t0b, t0c, t1a, t1b, t1c, t2a, t2b, t2c, b0a, b0b, b0c, b1a, b1b, b1c, b2a, b2b, b2c,
-    back_sems, swap_sems, w_sem, ring_sems, last_sems,
+    swap_sems, w_sem, ring_sems, last_sems,
 ):
     t = lax.axis_index("tm")
     d = lax.axis_index("dp")
     y, x, zh = place(t)
     zl, core = d // 2, d % 2
     z = zh * 2 + zl
-    slot = y * 2 + zh
     partner = {"dp": d + 1 - 2 * core, "tm": t}
     at = {"x": x, "y": y, "z": z}
     rows = hidden.shape[0]
@@ -411,24 +404,12 @@
     load_w.start()
     barrier = pltpu.get_barrier_semaphore()
 
-    def greet(s, carry):
-        pl.semaphore_signal(
-            barrier,
-            inc=1,
-            device_id={"dp": d, "tm": head_home((slot + s) % 8, x)},
-            device_id_type=MESH,
-        )
-        return carry
-
-    lax.fori_loop(1, 8, greet, 0)
     for axis in "xyz":
         for step in (1, 2, 3):
             pl.semaphore_signal(
                 barrier, inc=1, device_id=along(axis, step), device_id_type=MESH
             )
     pl.semaphore_signal(barrier, inc=1, device_id=partner, device_id_type=MESH)
-    pl.semaphore_wait(barrier, 17)
-
     def remote(src, dst, send_sem, recv_sem, device):
         return pltpu.make_async_remote_copy(
             src_ref=src,
@@ -439,32 +420,10 @@
             device_id_type=MESH,
         )
 
-    def send_back(s, carry):
-        i = (slot + s) % 8
-        remote(
-            res.at[i], got.at[slot], back_sems.at[0], back_sems.at[1],
-            {"dp": d, "tm": head_home(i, x)},
-        ).start()
-        return carry
-
-    lax.fori_loop(1, 8, send_back, 0)
-    own = pltpu.make_async_copy(res.at[slot], got.at[slot], back_sems.at[2])
-    own.start()
-
     def swap(src, dst, part):
         copy = remote(src, dst, swap_sems.at[0, part], swap_sems.at[1, part], partner)
         copy.start()
         return copy
-
-    other = 1 - core
-    swaps = [swap(hidden, ph, 0)]
-    for l in range(2):
-        cut = lanes(l * 1024 + other * 512, 512)
-        swaps.append(swap(gz.at[:, cut], pz.at[:, pl.ds(l * 512, 512)], 1 + l))
-
-    own.wait()
-    wait_bytes(got.at[pl.ds(0, 7)], back_sems.at[1])
-    swaps.append(swap(got.at[:, 0], pm, 3))
 
     def norm_back(h, carry):
         for part, u_ref in ((0, q), (1, k)):
@@ -478,6 +437,13 @@
         return carry
 
     lax.fori_loop(0, 8, norm_back, 0)
+    pl.semaphore_wait(barrier, 10)
+    other = 1 - core
+    swaps = [swap(hidden, ph, 0)]
+    for l in range(2):
+        cut = lanes(l * 1024 + other * 512, 512)
+        swaps.append(swap(gz.at[:, cut], pz.at[:, pl.ds(l * 512, 512)], 1 + l))
+    swaps.append(swap(got.at[:, 0], pm, 3))
     for l in range(2):
         for j in range(3):
             swaps.append(
@@ -649,7 +615,6 @@
                 rg, ch = (unit - 12) // 2, (unit - 12) % 2
                 out_o[rg * 16 : (rg + 1) * 16, ch * 256 : (ch + 1) * 256] = sums[u]
 
-    wait_bytes(got.at[pl.ds(0, 7)], back_sems.at[0])
     for copy in swaps:
         copy.wait_send()
     for s in range(3):
@@ -661,7 +626,7 @@
             last(s, step).wait_send()
 
 
-def close(res, hidden, gz, q, k, noisy, grad, scale1, w3):
+def close(got, hidden, gz, q, k, noisy, grad, scale1, w3):
     rows, model = hidden.shape
     vmem = pl.BlockSpec(memory_space=pltpu.VMEM)
 
@@ -675,10 +640,9 @@
             jax.ShapeDtypeStruct((3, 64, 256), BF),
             jax.ShapeDtypeStruct((32, 512), BF),
         ),
-        in_specs=[ANY] + [vmem] * 7 + [ANY],
+        in_specs=[vmem] * 8 + [ANY],
         out_specs=(vmem,) * 3,
         scratch_shapes=[
-            pltpu.VMEM((8, 4, rows, HD), BF),
             pltpu.VMEM((rows, 3072), BF),
             pltpu.VMEM((rows, model), BF),
             pltpu.VMEM((8, rows, HD), BF),
@@ -692,7 +656,6 @@
             *box(2, 3, 2, 4),
             *box(2, 3, 2),
             *box(3),
-            pltpu.SemaphoreType.DMA((3,)),
             pltpu.SemaphoreType.DMA((2, 10)),
             pltpu.SemaphoreType.DMA,
             pltpu.SemaphoreType.DMA((3, 2, 2, 3, 2)),
@@ -702,7 +665,7 @@
             collective_id=1, has_side_effects=True, vmem_limit_bytes=62 * 1024 * 1024
         ),
         name="close",
-    )(res, hidden, gz, q, k, noisy, grad, scale1, w3)
+    )(got, hidden, gz, q, k, noisy, grad, scale1, w3)
 
 
 def on_device(
@@ -713,7 +676,7 @@
     w3 = w_qkv.transpose(1, 0, 2)
     noisy_rows = noisy.reshape(rows, model)
     grad_rows = out_grad.reshape(rows, model)
-    kv, own, stretch, hidden, grad_z, q, k, scale1 = open_up(
+    got, hidden, grad_z, q, k, scale1 = open_up(
         levels.reshape(2),
         actions.reshape(1),
         starts.reshape(1),
@@ -724,10 +687,10 @@
         action_table,
         w3,
         w_out,
+        temps,
     )
-    res = attend(stretch[:, 0, 0], temps, kv.reshape(32, 2, tokens, HD), own)
     grad_noisy, total_g, total_o = close(
-        res, hidden, grad_z, q, k, noisy_rows, grad_rows, scale1, w3
+        got, hidden, grad_z, q, k, noisy_rows, grad_rows, scale1, w3
     )
     return (grad_noisy.reshape(noisy.shape), total_g.transpose(1, 0, 2), total_o)
 

time: 184 us -> 153 us (0.83)
  Pallas kernels: 173 us -> 145 us
  local copies, waits for them, and re-layouts: 9.11 us -> 5.22 us
    pallas_call x1, Pallas kernels: 104 us -> 64.2 us  [close(): pl.pallas_call(close_kernel, out_shape=(jax.ShapeDtypeStruct((rows, model...]
    pallas_call x2 -> x1, Pallas kernels: 68.5 us -> 80.9 us  [open_up(): pl.pallas_call(open_kernel, out_shape=(jax.ShapeDtypeStruct((8, 4, rows,...]
    unnamed x15 -> x3, local copies, waits for them, and re-layouts: 8.12 us -> 5.22 us
where the time goes in v4:
time: 153 us; the launch traced here: 152 us
  Pallas kernels  145 us (95%)
  local copies, waits for them, and re-layouts  5.22 us (3%)
  between operations  1.94 us (1%)
    pallas_call x1, Pallas kernels, open_up(): pl.pallas_call(open_kernel, out_shape=(jax.ShapeDtypeStruct((8, 4, rows,...  80.9 us
    pallas_call x1, Pallas kernels, close(): pl.pallas_call(close_kernel, out_shape=(jax.ShapeDtypeStruct((rows, model...  64.2 us
    unnamed x3, local copies, waits for them, and re-layouts  5.22 us

profile of v4, /device:TPU:0, one launch (start us, length us, event | category | flops | bytes accessed | tf_op | source)
XLA Modules:
  0.0 152.3 jit_solution(14755385041761607893)
XLA Ops:
  1.9 80.9 %open.1 = (bf16[8,4,256,128]{3,2,1,0:T(8,128)(2,1)}, bf16[256,2048]{1,0:T(8,128)(2,1)}, bf16[256,2048]{1,0:T(8,128)(2,1)}, f32[256,1024]{1,0:T(8,128)}, f32[256,1024]{1,0:T(8,128)}, /*index=5*/f32[2,2048]{1,0:T(2,128)}) custom-call(s32[2]{0:T(128)} %bitcast.22, s32[1]{0:T(128)} %bitcast.10.action, s32[1]{0:T(128)} %bitcast.11.start, ...), custom_call_target="tpu_custom_call" | custom-call | tf_op jit(solution)/shard_map/open/pallas_call | solution.py:328
  82.9 64.2 %close.1 = (bf16[256,2048]{1,0:T(8,128)(2,1)}, bf16[3,64,256]{2,1,0:T(8,128)(2,1)}, bf16[32,512]{1,0:T(8,128)(2,1)}) custom-call(bf16[8,4,256,128]{3,2,1,0:T(8,128)(2,1)} %get-tuple-element.12.got, bf16[256,2048]{1,0:T(8,128)(2,1)} %get-tuple-element.13.hidden, bf16[256,2048]{1,0:T(8,128)(2,1)} %get-tuple-element.14.gz, f32[256,1024]{1,0:T(8,128)} %get-tuple-element.15.q, ...), custom_call_target="tpu_custom_call" | custom-call | tf_op jit(solution)/shard_map/close/pallas_call | solution.py:636
  147.1 2.3 %copy.19 = bf16[1,1,2,128,2048]{4,3,2,1,0:T(8,128)(2,1)} copy(bf16[1,1,2,128,2048]{4,3,2,1,0:T(8,128)(2,1)} %bitcast.19) | data formatting | bytes 2097152
  149.4 1.5 %copy.20 = bf16[64,3,256]{2,0,1:T(8,128)(2,1)} copy(bf16[64,3,256]{2,0,1:T(8,128)(2,1)} %bitcast.21) | data formatting | bytes 196608
  150.9 1.4 copy.21

commit v5 on v4

--- a/solution.py
+++ b/solution.py
@@ -47,9 +47,9 @@
 
 def open_kernel(
     level, action, start, noisy, clean, grad, noise, acts, w3, w_out,
-    temps, got, hidden, gz, q, k, scale1,
+    temps, got, hidden, gz, q, k, scale1, ph, pz,
     kv, own, stretch, clean_hidden, ckv, out, tile, w, wo, s_scr, res,
-    w_sems, kv_sems, x_sems, own_sems, start_sems, local_sems, back_sems,
+    w_sems, kv_sems, x_sems, own_sems, start_sems, local_sems, back_sems, swap_sems,
 ):
     t = lax.axis_index("tm")
     d = lax.axis_index("dp")
@@ -79,8 +79,10 @@
         return carry
 
     lax.fori_loop(1, 8, greet, 0)
-    for step in (1, 2, 3):
-        pl.semaphore_signal(barrier, inc=1, device_id=beside(step), device_id_type=MESH)
+    core = d % 2
+    partner = {"dp": d + 1 - 2 * core, "tm": t}
+    for device in (beside(1), beside(3), partner):
+        pl.semaphore_signal(barrier, inc=1, device_id=device, device_id_type=MESH)
 
     def remote(src, dst, sems, device, arrived=1):
         return pltpu.make_async_remote_copy(
@@ -161,6 +163,14 @@
 
         lax.fori_loop(0, 8, noisy_rows, 0, unroll=2)
 
+    swaps = [remote(hidden, ph, swap_sems.at[0], partner)]
+    for l in range(2):
+        cut = lanes(l * 1024 + (1 - core) * 512, 512)
+        swaps.append(
+            remote(gz.at[:, cut], pz.at[:, pl.ds(l * 512, 512)], swap_sems.at[1 + l], partner)
+        )
+    for copy in swaps:
+        copy.start()
     loads[2].wait()
     loads[3].wait()
 
@@ -194,8 +204,16 @@
     for copy in mine:
         copy.wait()
     wait_bytes(ckv.at[pl.ds(0, 7)], kv_sems.at[1])
-    for step in (1, 3, 2):
-        remote(kv.at[:, x], kv.at[:, x], x_sems, beside(step)).start()
+    half = (pl.ds(0, 2), pl.ds(2, 2))
+
+    def along_x(n):
+        cut = half[(0, 1, 1, 0, 0, 1)[n]]
+        whose = x if n < 4 else (x + (3 if n == 4 else 1)) % 4
+        step = (1, 1, 3, 3, 1, 3)[n]
+        return remote(kv.at[cut, whose], kv.at[cut, whose], x_sems.at[n], beside(step))
+
+    for n in (0, 2, 1, 3):
+        along_x(n).start()
 
     def project_send(i, carry):
         project(i, carry)
@@ -209,8 +227,12 @@
     last = pltpu.make_async_copy(out.at[slot], own.at[slot], local_sems.at[2])
     last.start()
     last.wait()
+    for n in (0, 2):
+        along_x(n).wait_recv()
+        along_x(4 + n // 2).start()
     wait_bytes(stretch.at[pl.ds(0, 7)], start_sems.at[1])
-    wait_bytes(kv.at[:, pl.ds(0, 3)], x_sems.at[1])
+    for n in (1, 3, 4, 5):
+        along_x(n).wait_recv()
 
     scale = temps[slot] * (1.0 / math.sqrt(HD))
     c2 = scale * LOG2E
@@ -312,7 +334,10 @@
     keep.start()
     keep.wait()
     wait_bytes(stretch.at[pl.ds(0, 7)], start_sems.at[0])
-    wait_bytes(kv.at[:, pl.ds(0, 3)], x_sems.at[0])
+    for n in range(6):
+        along_x(n).wait_send()
+    for copy in swaps:
+        copy.wait()
     wait_bytes(own.at[pl.ds(0, 7)], own_sems.at[0])
     wait_bytes(ckv.at[pl.ds(0, 7)], kv_sems.at[0])
     for way in (0, 1):
@@ -334,9 +359,11 @@
             jax.ShapeDtypeStruct((rows, width), F32),
             jax.ShapeDtypeStruct((rows, width), F32),
             jax.ShapeDtypeStruct((2, model), F32),
+            jax.ShapeDtypeStruct((rows, model), BF),
+            jax.ShapeDtypeStruct((rows, model // 2), BF),
         ),
         in_specs=[smem] * 3 + [vmem] * 5 + [ANY] * 2 + [smem],
-        out_specs=(ANY,) + (vmem,) * 5,
+        out_specs=(ANY,) + (vmem,) * 5 + (ANY, ANY),
         scratch_shapes=[
             pltpu.VMEM((4, 4, 2, 2, tokens, HD), BF),
             pltpu.VMEM((8, 4, rows, HD), BF),
@@ -351,11 +378,12 @@
             pltpu.VMEM((8, 4, rows, HD), BF),
             pltpu.SemaphoreType.DMA((4,)),
             pltpu.SemaphoreType.DMA((2,)),
-            pltpu.SemaphoreType.DMA((2,)),
+            pltpu.SemaphoreType.DMA((6, 2)),
             pltpu.SemaphoreType.DMA((5,)),
             pltpu.SemaphoreType.DMA((2,)),
             pltpu.SemaphoreType.DMA((3,)),
             pltpu.SemaphoreType.DMA((2,)),
+            pltpu.SemaphoreType.DMA((3, 2)),
         ],
         compiler_params=pltpu.CompilerParams(
             collective_id=0, has_side_effects=True, vmem_limit_bytes=60 * 1024 * 1024
@@ -365,19 +393,19 @@
 
 
 ORDERS = (("x", "y", "z"), ("y", "z", "x"), ("z", "x", "y"))
-UNITS = (5, 5, 6)
-FIRST_UNIT = (0, 5, 10)
+UNITS = (11, 11, 10)
+FIRST_UNIT = (0, 11, 22)
 
 
 def stream_of(unit):
-    k = 0 if unit < 5 else 1 if unit < 10 else 2
+    k = unit // 11
     return k, unit - FIRST_UNIT[k]
 
 
 def close_kernel(
-    got, hidden, gz, q, k, noisy, grad, scale1, w3,
+    got, hidden, gz, q, k, scale1, ph, pz, noisy_all, grad_all, w3,
     out_n, out_g, out_o,
-    proj, ph, pm, pp, pz, w, gh,
+    noisy, grad, proj, pm, pp, w, gh,
     t0a, t0b, t0c, t1a, t1b, t1c, t2a, t2b, t2c, b0a, b0b, b0c, b1a, b1b, b1c, b2a, b2b, b2c,
     swap_sems, w_sem, ring_sems, last_sems,
 ):
@@ -400,8 +428,13 @@
             "tm": (c["y"] * 4 + c["x"]) * 2 + c["z"] // 2,
         }
 
-    load_w = pltpu.make_async_copy(w3, w, w_sem)
-    load_w.start()
+    loads = [
+        pltpu.make_async_copy(w3, w, w_sem.at[0]),
+        pltpu.make_async_copy(noisy_all, noisy, w_sem.at[1]),
+        pltpu.make_async_copy(grad_all, grad, w_sem.at[2]),
+    ]
+    for load in loads:
+        load.start()
     barrier = pltpu.get_barrier_semaphore()
 
     for axis in "xyz":
@@ -439,18 +472,14 @@
     lax.fori_loop(0, 8, norm_back, 0)
     pl.semaphore_wait(barrier, 10)
     other = 1 - core
-    swaps = [swap(hidden, ph, 0)]
-    for l in range(2):
-        cut = lanes(l * 1024 + other * 512, 512)
-        swaps.append(swap(gz.at[:, cut], pz.at[:, pl.ds(l * 512, 512)], 1 + l))
-    swaps.append(swap(got.at[:, 0], pm, 3))
+    swaps = [swap(got.at[:, 0], pm, 0)]
     for l in range(2):
         for j in range(3):
             swaps.append(
                 swap(
                     proj.at[:, lanes(j * 1024 + l * 512 + other * 256, 256)],
                     pp.at[:, pl.ds(l * 768 + j * 256, 256)],
-                    4 + l * 3 + j,
+                    1 + l * 3 + j,
                 )
             )
     for copy in swaps:
@@ -461,7 +490,8 @@
         spot = {"x": xb, "y": yb, "z": zb}
         terms[0][s][spot[ORDERS[s][0]], spot[ORDERS[s][1]], spot[ORDERS[s][2]], u] = value
 
-    def terms_of(yb, carry):
+    def terms_of(n, carry):
+        yb = ((y // 2 + 1 + n // 2) % 2) * 2 + (y + n % 2 + n // 2) % 2
         cut = lanes(yb * 512, 512)
         left = jnp.concatenate([hidden[:, cut], ph[:, cut]], 0).T
         for l in range(2):
@@ -474,7 +504,11 @@
                     for hb in range(2):
                         for rg in range(4):
                             r = (xb * 2 + hb) * 64 + rg * 16
-                            put(yb, xb, hb * 2 + l, j * 4 + rg, term[r : r + 16])
+                            for ch in range(2):
+                                put(
+                                    yb, xb, hb * 2 + l, (j * 4 + rg) * 2 + ch,
+                                    term[r : r + 16, ch * 128 : (ch + 1) * 128],
+                                )
         left = jnp.concatenate(
             [
                 jnp.concatenate([got[2 * yb, 0], got[2 * yb + 1, 0]], 1),
@@ -489,26 +523,56 @@
             for xb in range(4):
                 for hb in range(2):
                     for rg in range(2):
-                        for ch in range(2):
+                        for ch in range(4):
                             r = (xb * 2 + hb) * 32 + rg * 16
                             put(
-                                yb, xb, hb * 2 + l, 12 + rg * 2 + ch,
-                                term[r : r + 16, ch * 256 : (ch + 1) * 256],
+                                yb, xb, hb * 2 + l, 24 + rg * 4 + ch,
+                                term[r : r + 16, ch * 128 : (ch + 1) * 128],
                             )
-        return carry
-
-    lax.fori_loop(0, 4, terms_of, 0)
-
-    travel = (pl.ds(0, 2), pl.ds(2, 2))
+
+        @pl.when(n == 0)
+        def _():
+            ring(1, 0, 0, 0).start()
+            ring(1, 0, 1, 0).start()
+
+        @pl.when(n == 1)
+        def _():
+            for s in (0, 2):
+                ring(s, 0, 0, 0).start()
+                ring(s, 0, 1, 1).start()
+
+        @pl.when((n == 1) & (y % 2 == 0) | (n == 2) & (y % 2 == 1))
+        def _():
+            ring(1, 0, 1, 1).start()
+
+        @pl.when((n == 1) & (y % 2 == 1) | (n == 2) & (y % 2 == 0))
+        def _():
+            ring(1, 0, 0, 1).start()
+
+        @pl.when(n == 3)
+        def _():
+            for s in (0, 2):
+                ring(s, 0, 1, 0).start()
+                ring(s, 0, 0, 1).start()
+
+        return carry
+
+    far_pair, near_pair = pl.ds((1 - y // 2) * 2, 2), pl.ds((y // 2) * 2, 2)
+
+    def half(s, level, way):
+        if level == 1 or s == 1:
+            return (pl.ds(2 * way, 2),)
+        cut = near_pair if way else far_pair
+        return (cut,) if s == 0 else (slice(None), cut)
 
     def ring(s, level, way, part):
         axis = ORDERS[s][level]
         step = 1 if way == 0 else 3
         near, far = (at[axis] + step) % 4, (at[axis] + 2) % 4
         src = (
-            terms[level][s].at[far, travel[way]],
-            terms[level][s].at[near, travel[1 - way]],
-            terms[level][s].at[near, travel[way]],
+            terms[level][s].at[(far, *half(s, level, way))],
+            terms[level][s].at[(near, *half(s, level, 1 - way))],
+            terms[level][s].at[(near, *half(s, level, way))],
         )[part]
         sems = ring_sems.at[s, level, way, part]
         return remote(
@@ -525,7 +589,7 @@
         for way in range(2):
             ring(s, level, way, 0).wait_recv()
             near = (at[axis] + (1 if way == 0 else 3)) % 4
-            spot = terms[level][s].at[near, travel[way]]
+            spot = terms[level][s].at[(near, *half(s, level, way))]
             spot[...] = (
                 spot[...].astype(F32) + boxes[level][s][way, 0].astype(F32)
             ).astype(BF)
@@ -538,16 +602,16 @@
         mine = at[ORDERS[s][level]]
         box = boxes[level][s]
         for way in range(2):
-            terms[level + 1][s][travel[way]] = (
-                terms[level][s][mine, travel[way]].astype(F32)
+            cut = half(s, level, way)
+            terms[level + 1][s][cut] = (
+                terms[level][s][(mine, *cut)].astype(F32)
                 + box[way, 2].astype(F32)
                 + box[1 - way, 1].astype(F32)
             ).astype(BF)
 
-    for s in range(3):
-        ring_open(0, s)
-
-    load_w.wait()
+    lax.fori_loop(0, 4, terms_of, 0)
+    for load in loads:
+        load.wait()
 
     def pull_hidden(n, carry):
         cut = lanes(n * 512, 512)
@@ -608,12 +672,12 @@
         sums = sums.astype(BF)
         for u in range(UNITS[s]):
             unit = FIRST_UNIT[s] + u
-            if unit < 12:
-                j, rg = unit // 4, unit % 4
-                out_g[j, rg * 16 : (rg + 1) * 16, :] = sums[u]
+            if unit < 24:
+                j, rg, ch = unit // 8, (unit // 2) % 4, unit % 2
+                out_g[j, rg * 16 : (rg + 1) * 16, ch * 128 : (ch + 1) * 128] = sums[u]
             else:
-                rg, ch = (unit - 12) // 2, (unit - 12) % 2
-                out_o[rg * 16 : (rg + 1) * 16, ch * 256 : (ch + 1) * 256] = sums[u]
+                rg, ch = (unit - 24) // 4, unit % 4
+                out_o[rg * 16 : (rg + 1) * 16, ch * 128 : (ch + 1) * 128] = sums[u]
 
     for copy in swaps:
         copy.wait_send()
@@ -626,12 +690,12 @@
             last(s, step).wait_send()
 
 
-def close(got, hidden, gz, q, k, noisy, grad, scale1, w3):
+def close(got, hidden, gz, q, k, scale1, ph, pz, noisy, grad, w3):
     rows, model = hidden.shape
     vmem = pl.BlockSpec(memory_space=pltpu.VMEM)
 
     def box(*shape):
-        return [pltpu.VMEM(shape + (u, 16, 256), BF) for u in UNITS]
+        return [pltpu.VMEM(shape + (u, 16, 128), BF) for u in UNITS]
 
     return pl.pallas_call(
         close_kernel,
@@ -640,24 +704,25 @@
             jax.ShapeDtypeStruct((3, 64, 256), BF),
             jax.ShapeDtypeStruct((32, 512), BF),
         ),
-        in_specs=[vmem] * 8 + [ANY],
+        in_specs=[vmem] * 8 + [ANY] * 3,
         out_specs=(vmem,) * 3,
         scratch_shapes=[
+            pltpu.VMEM((rows, model), BF),
+            pltpu.VMEM((rows, model), BF),
             pltpu.VMEM((rows, 3072), BF),
-            pltpu.VMEM((rows, model), BF),
             pltpu.VMEM((8, rows, HD), BF),
             pltpu.VMEM((rows, 1536), BF),
-            pltpu.VMEM((rows, 1024), BF),
             pltpu.VMEM(w3.shape, BF),
             pltpu.VMEM((rows, model), BF),
             *box(4, 4, 4),
             *box(4, 4),
             *box(4),
-            *box(2, 3, 2, 4),
+            *box(2, 3, 2, 4)[:2],
+            box(2, 3, 4, 2)[2],
             *box(2, 3, 2),
             *box(3),
-            pltpu.SemaphoreType.DMA((2, 10)),
-            pltpu.SemaphoreType.DMA,
+            pltpu.SemaphoreType.DMA((2, 7)),
+            pltpu.SemaphoreType.DMA((3,)),
             pltpu.SemaphoreType.DMA((3, 2, 2, 3, 2)),
             pltpu.SemaphoreType.DMA((3, 3, 2)),
         ],
@@ -665,7 +730,7 @@
             collective_id=1, has_side_effects=True, vmem_limit_bytes=62 * 1024 * 1024
         ),
         name="close",
-    )(got, hidden, gz, q, k, noisy, grad, scale1, w3)
+    )(got, hidden, gz, q, k, scale1, ph, pz, noisy, grad, w3)
 
 
 def on_device(
@@ -676,7 +741,7 @@
     w3 = w_qkv.transpose(1, 0, 2)
     noisy_rows = noisy.reshape(rows, model)
     grad_rows = out_grad.reshape(rows, model)
-    got, hidden, grad_z, q, k, scale1 = open_up(
+    got, hidden, grad_z, q, k, scale1, ph, pz = open_up(
         levels.reshape(2),
         actions.reshape(1),
         starts.reshape(1),
@@ -690,7 +755,7 @@
         temps,
     )
     grad_noisy, total_g, total_o = close(
-        got, hidden, grad_z, q, k, noisy_rows, grad_rows, scale1, w3
+        got, hidden, grad_z, q, k, scale1, ph, pz, noisy_rows, grad_rows, w3
     )
     return (grad_noisy.reshape(noisy.shape), total_g.transpose(1, 0, 2), total_o)
 

time: 153 us -> 140 us (0.915)
  Pallas kernels: 145 us -> 133 us
    pallas_call x1, Pallas kernels: 64.2 us -> 57.6 us  [close(): pl.pallas_call(close_kernel, out_shape=(jax.ShapeDtypeStruct((rows, model...]
    pallas_call x1, Pallas kernels: 80.9 us -> 75.1 us  [open_up(): pl.pallas_call(open_kernel, out_shape=(jax.ShapeDtypeStruct((8, 4, rows,...]
where the time goes in v5:
time: 140 us
  Pallas kernels  133 us (95%)
  local copies, waits for them, and re-layouts  5.22 us (4%)
  between operations  1.94 us (1%)
    pallas_call x1, Pallas kernels, open_up(): pl.pallas_call(open_kernel, out_shape=(jax.ShapeDtypeStruct((8, 4, rows,...  75.1 us
    pallas_call x1, Pallas kernels, close(): pl.pallas_call(close_kernel, out_shape=(jax.ShapeDtypeStruct((rows, model...  57.6 us
    unnamed x3, local copies, waits for them, and re-layouts  5.22 us

profile of v5, /device:TPU:0, one launch (start us, length us, event | category | flops | bytes accessed | tf_op | source)
XLA Modules:
  0.0 139.9 jit_solution(8228299867550393793)
XLA Ops:
  1.9 75.1 %open.1 = (bf16[8,4,256,128]{3,2,1,0:T(8,128)(2,1)}, bf16[256,2048]{1,0:T(8,128)(2,1)}, bf16[256,2048]{1,0:T(8,128)(2,1)}, f32[256,1024]{1,0:T(8,128)}, f32[256,...) custom-call(s32[2]{0:T(128)} %bitcast.22, s32[1]{0:T(128)} %bitcast.10.action, ...), custom_call_target="tpu_custom_call" | custom-call | tf_op jit(solution)/shard_map/open/pallas_call | solution.py:353
  77.1 57.6 %close.1 = (bf16[256,2048]{1,0:T(8,128)(2,1)}, bf16[3,64,256]{2,1,0:T(8,128)(2,1)}, bf16[32,512]{1,0:T(8,128)(2,1)}) custom-call(bf16[8,4,256,128]{3,2,1,0:T(8,128)(2,1)} %get-tuple-element.14.got, bf16[256,2048]{1,0:T(8,128)(2,1)} %get-tuple-element.15.hidden, bf16[256,2048]{1,0:T(8,128)(2,1)} %get-tuple-element.16.gz, f32[256,1024]{1,0:T(8,128)} %get-tuple-element.17.q, ...), custom_call_target="tpu_custom_call" | custom-call | tf_op jit(solution)/shard_map/close/pallas_call | solution.py:700
  134.7 2.3 %copy.19 = bf16[1,1,2,128,2048]{4,3,2,1,0:T(8,128)(2,1)} copy(bf16[1,1,2,128,2048]{4,3,2,1,0:T(8,128)(2,1)} %bitcast.19) | data formatting | bytes 2097152
  137.0 1.5 %copy.20 = bf16[64,3,256]{2,0,1:T(8,128)(2,1)} copy(bf16[64,3,256]{2,0,1:T(8,128)(2,1)} %bitcast.21) | data formatting | bytes 196608
  138.5 1.4 copy.21

commit v6 on v5

--- a/solution.py
+++ b/solution.py
@@ -46,22 +46,31 @@
 
 
 def open_kernel(
-    level, action, start, noisy, clean, grad, noise, acts, w3, w_out,
-    temps, got, hidden, gz, q, k, scale1, ph, pz,
-    kv, own, stretch, clean_hidden, ckv, out, tile, w, wo, s_scr, res,
-    w_sems, kv_sems, x_sems, own_sems, start_sems, local_sems, back_sems, swap_sems,
+    level, action, start, noisy_all, clean_all, grad_all, noise_all, acts_all, w3, w_out,
+    temps, got, hidden_out, gz_out, q_out, k_out, scale_out, ph, pz,
+    noisy, clean, grad, noise, acts, hidden, gz, q, k, scale1, kv, own, stretch, clean_hidden, ckv, out, tile, w, wo, s_scr, res,
+    w_sems, kv_sems, x_sems, own_sems, start_sems, local_sems, back_sems, swap_sems, in_sems, out_sems,
 ):
     t = lax.axis_index("tm")
     d = lax.axis_index("dp")
     y, x, zh = place(t)
     slot = y * 2 + zh
+    first = [
+        pltpu.make_async_copy(clean_all, clean, in_sems.at[0]),
+        pltpu.make_async_copy(noise_all, noise, in_sems.at[1]),
+        pltpu.make_async_copy(acts_all, acts, in_sems.at[2]),
+    ]
     loads = [
         pltpu.make_async_copy(w3.at[1], w.at[1], w_sems.at[1]),
         pltpu.make_async_copy(w3.at[2], w.at[2], w_sems.at[2]),
         pltpu.make_async_copy(w3.at[0], w.at[0], w_sems.at[0]),
         pltpu.make_async_copy(w_out, wo, w_sems.at[3]),
     ]
-    for load in loads:
+    second = [
+        pltpu.make_async_copy(noisy_all, noisy, in_sems.at[3]),
+        pltpu.make_async_copy(grad_all, grad, in_sems.at[4]),
+    ]
+    for load in first + loads[:2] + second + loads[2:]:
         load.start()
 
     def peer(h):
@@ -99,6 +108,8 @@
         factor = lax.rsqrt(jnp.mean(center * center, axis=1, keepdims=True) + EPS)
         return (center * factor * scale + shift).astype(BF)
 
+    for load in first:
+        load.wait()
     act = acts[action[0]]
     clean_shift = noise[0, 0:1, :] + act[0:1]
     clean_scale = 1.0 + (noise[1, 0:1, :] + act[1:2])
@@ -148,6 +159,8 @@
     for copy in mine:
         copy.start()
 
+    for load in second:
+        load.wait()
     for j in range(2):
         row = pl.ds(level[j], 1)
         shift = noise[0, row, :] + act[0:1]
@@ -170,6 +183,15 @@
             remote(gz.at[:, cut], pz.at[:, pl.ds(l * 512, 512)], swap_sems.at[1 + l], partner)
         )
     for copy in swaps:
+        copy.start()
+    results = [
+        pltpu.make_async_copy(hidden, hidden_out, out_sems.at[0]),
+        pltpu.make_async_copy(gz, gz_out, out_sems.at[1]),
+        pltpu.make_async_copy(scale1, scale_out, out_sems.at[2]),
+        pltpu.make_async_copy(q, q_out, out_sems.at[3]),
+        pltpu.make_async_copy(k, k_out, out_sems.at[4]),
+    ]
+    for copy in results[:3]:
         copy.start()
     loads[2].wait()
     loads[3].wait()
@@ -226,6 +248,8 @@
     send_own(sibling, 3)
     last = pltpu.make_async_copy(out.at[slot], own.at[slot], local_sems.at[2])
     last.start()
+    for copy in results[3:]:
+        copy.start()
     last.wait()
     for n in (0, 2):
         along_x(n).wait_recv()
@@ -336,7 +360,7 @@
     wait_bytes(stretch.at[pl.ds(0, 7)], start_sems.at[0])
     for n in range(6):
         along_x(n).wait_send()
-    for copy in swaps:
+    for copy in swaps + results:
         copy.wait()
     wait_bytes(own.at[pl.ds(0, 7)], own_sems.at[0])
     wait_bytes(ckv.at[pl.ds(0, 7)], kv_sems.at[0])
@@ -348,7 +372,6 @@
     rows, model = noisy.shape
     tokens = clean.shape[0]
     width = w_out.shape[0]
-    vmem = pl.BlockSpec(memory_space=pltpu.VMEM)
     smem = pl.BlockSpec(memory_space=pltpu.SMEM)
     return pl.pallas_call(
         open_kernel,
@@ -362,9 +385,19 @@
             jax.ShapeDtypeStruct((rows, model), BF),
             jax.ShapeDtypeStruct((rows, model // 2), BF),
         ),
-        in_specs=[smem] * 3 + [vmem] * 5 + [ANY] * 2 + [smem],
-        out_specs=(ANY,) + (vmem,) * 5 + (ANY, ANY),
+        in_specs=[smem] * 3 + [ANY] * 7 + [smem],
+        out_specs=(ANY,) * 8,
         scratch_shapes=[
+            pltpu.VMEM(noisy.shape, BF),
+            pltpu.VMEM(clean.shape, BF),
+            pltpu.VMEM(grad.shape, BF),
+            pltpu.VMEM(noise.shape, F32),
+            pltpu.VMEM(acts.shape, F32),
+            pltpu.VMEM((rows, model), BF),
+            pltpu.VMEM((rows, model), BF),
+            pltpu.VMEM((rows, width), F32),
+            pltpu.VMEM((rows, width), F32),
+            pltpu.VMEM((2, model), F32),
             pltpu.VMEM((4, 4, 2, 2, tokens, HD), BF),
             pltpu.VMEM((8, 4, rows, HD), BF),
             pltpu.VMEM((8, 8, 128), jnp.int32),
@@ -384,6 +417,8 @@
             pltpu.SemaphoreType.DMA((3,)),
             pltpu.SemaphoreType.DMA((2,)),
             pltpu.SemaphoreType.DMA((3, 2)),
+            pltpu.SemaphoreType.DMA((5,)),
+            pltpu.SemaphoreType.DMA((5,)),
         ],
         compiler_params=pltpu.CompilerParams(
             collective_id=0, has_side_effects=True, vmem_limit_bytes=60 * 1024 * 1024
@@ -403,9 +438,9 @@
 
 
 def close_kernel(
-    got, hidden, gz, q, k, scale1, ph, pz, noisy_all, grad_all, w3,
+    got_all, q_all, k_all, hidden_all, gz_all, ph_all, pz_all, scale_all, noisy_all, grad_all, w3,
     out_n, out_g, out_o,
-    noisy, grad, proj, pm, pp, w, gh,
+    got, q, k, hidden, gz, ph, pz, scale1, noisy, grad, proj, pm, pp, w, gh,
     t0a, t0b, t0c, t1a, t1b, t1c, t2a, t2b, t2c, b0a, b0b, b0c, b1a, b1b, b1c, b2a, b2b, b2c,
     swap_sems, w_sem, ring_sems, last_sems,
 ):
@@ -428,10 +463,13 @@
             "tm": (c["y"] * 4 + c["x"]) * 2 + c["z"] // 2,
         }
 
+    sources = (
+        got_all, q_all, k_all, hidden_all, gz_all, ph_all, pz_all, scale_all, noisy_all, grad_all, w3,
+    )
+    places = (got, q, k, hidden, gz, ph, pz, scale1, noisy, grad, w)
     loads = [
-        pltpu.make_async_copy(w3, w, w_sem.at[0]),
-        pltpu.make_async_copy(noisy_all, noisy, w_sem.at[1]),
-        pltpu.make_async_copy(grad_all, grad, w_sem.at[2]),
+        pltpu.make_async_copy(source, spot, w_sem.at[n])
+        for n, (source, spot) in enumerate(zip(sources, places, strict=True))
     ]
     for load in loads:
         load.start()
@@ -469,11 +507,15 @@
         proj[:, lanes(2048 + h * HD, HD)] = got[h, 3]
         return carry
 
-    lax.fori_loop(0, 8, norm_back, 0)
-    pl.semaphore_wait(barrier, 10)
+    for load in loads[:3]:
+        load.wait()
     other = 1 - core
-    swaps = [swap(got.at[:, 0], pm, 0)]
+    swaps = []
     for l in range(2):
+        lax.fori_loop(0, 2, lambda i, c: norm_back(l * 4 + other * 2 + i, c), 0)
+        if l == 0:
+            pl.semaphore_wait(barrier, 10)
+            swaps.append(swap(got.at[:, 0], pm, 0))
         for j in range(3):
             swaps.append(
                 swap(
@@ -482,6 +524,10 @@
                     1 + l * 3 + j,
                 )
             )
+    for l in range(2):
+        lax.fori_loop(0, 2, lambda i, c: norm_back(l * 4 + core * 2 + i, c), 0)
+    for load in loads[3:7]:
+        load.wait()
     for copy in swaps:
         copy.wait_recv()
 
@@ -610,7 +656,7 @@
             ).astype(BF)
 
     lax.fori_loop(0, 4, terms_of, 0)
-    for load in loads:
+    for load in loads[7:]:
         load.wait()
 
     def pull_hidden(n, carry):
@@ -690,7 +736,7 @@
             last(s, step).wait_send()
 
 
-def close(got, hidden, gz, q, k, scale1, ph, pz, noisy, grad, w3):
+def close(got, q, k, hidden, gz, ph, pz, scale1, noisy, grad, w3):
     rows, model = hidden.shape
     vmem = pl.BlockSpec(memory_space=pltpu.VMEM)
 
@@ -704,11 +750,13 @@
             jax.ShapeDtypeStruct((3, 64, 256), BF),
             jax.ShapeDtypeStruct((32, 512), BF),
         ),
-        in_specs=[vmem] * 8 + [ANY] * 3,
+        in_specs=[ANY] * 11,
         out_specs=(vmem,) * 3,
         scratch_shapes=[
-            pltpu.VMEM((rows, model), BF),
-            pltpu.VMEM((rows, model), BF),
+            *[
+                pltpu.VMEM(array.shape, array.dtype)
+                for array in (got, q, k, hidden, gz, ph, pz, scale1, noisy, grad)
+            ],
             pltpu.VMEM((rows, 3072), BF),
             pltpu.VMEM((8, rows, HD), BF),
             pltpu.VMEM((rows, 1536), BF),
@@ -722,7 +770,7 @@
             *box(2, 3, 2),
             *box(3),
             pltpu.SemaphoreType.DMA((2, 7)),
-            pltpu.SemaphoreType.DMA((3,)),
+            pltpu.SemaphoreType.DMA((11,)),
             pltpu.SemaphoreType.DMA((3, 2, 2, 3, 2)),
             pltpu.SemaphoreType.DMA((3, 3, 2)),
         ],
@@ -730,7 +778,7 @@
             collective_id=1, has_side_effects=True, vmem_limit_bytes=62 * 1024 * 1024
         ),
         name="close",
-    )(got, hidden, gz, q, k, scale1, ph, pz, noisy, grad, w3)
+    )(got, q, k, hidden, gz, ph, pz, scale1, noisy, grad, w3)
 
 
 def on_device(
@@ -755,7 +803,7 @@
         temps,
     )
     grad_noisy, total_g, total_o = close(
-        got, hidden, grad_z, q, k, scale1, ph, pz, noisy_rows, grad_rows, w3
+        got, q, k, hidden, grad_z, ph, pz, scale1, noisy_rows, grad_rows, w3
     )
     return (grad_noisy.reshape(noisy.shape), total_g.transpose(1, 0, 2), total_o)
 

time: 140 us -> 136 us (0.971)
  Pallas kernels: 133 us -> 128 us
    pallas_call x1, Pallas kernels: 57.6 us -> 54.9 us  [close(): pl.pallas_call(close_kernel, out_shape=(jax.ShapeDtypeStruct((rows, model...]
    pallas_call x1, Pallas kernels: 75.1 us -> 73.3 us  [open_up(): pl.pallas_call(open_kernel, out_shape=(jax.ShapeDtypeStruct((8, 4, rows,...]
where the time goes in v6:
time: 136 us; the launch traced here: 135 us
  Pallas kernels  128 us (94%)
  local copies, waits for them, and re-layouts  5.22 us (4%)
  between operations  1.94 us (1%)
    pallas_call x1, Pallas kernels, open_up(): pl.pallas_call(open_kernel, out_shape=(jax.ShapeDtypeStruct((8, 4, rows,...  73.3 us
    pallas_call x1, Pallas kernels, close(): pl.pallas_call(close_kernel, out_shape=(jax.ShapeDtypeStruct((rows, model...  54.9 us
    unnamed x3, local copies, waits for them, and re-layouts  5.22 us

profile of v6, /device:TPU:0, one launch (start us, length us, event | category | flops | bytes accessed | tf_op | source)
XLA Modules:
  0.0 135.3 jit_solution(18188499199003868232)
XLA Ops:
  1.9 73.3 %open.1 = (bf16[8,4,256,128]{3,2,1,0:T(8,128)(2,1)}, bf16[256,2048]{1,0:T(8,128)(2,1)}, bf16[256,2048]{1,0:T(8,128)(2,1)}, f32[256,1024]{1,0:T(8,128)}, f32[256,...) custom-call(s32[2]{0:T(128)} %bitcast.22, s32[1]{0:T(128)} %bitcast.10.action, ...), custom_call_target="tpu_custom_call" | custom-call | tf_op jit(solution)/shard_map/open/pallas_call | solution.py:376
  75.2 54.9 %close.1 = (bf16[256,2048]{1,0:T(8,128)(2,1)}, bf16[3,64,256]{2,1,0:T(8,128)(2,1)}, bf16[32,512]{1,0:T(8,128)(2,1)}) custom-call(bf16[8,4,256,128]{3,2,1,0:T(8,128)(2,1)} %get-tuple-element.14.got_all, f32[256,1024]{1,0:T(8,128)} %get-tuple-element.15.q_all, f32[256,1024]{1,0:T(8,128)} %get-tuple-element.16.k_all, ...), custom_call_target="tpu_custom_call" | custom-call | tf_op jit(solution)/shard_map/close/pallas_call | solution.py:746
  130.1 2.3 %copy.19 = bf16[1,1,2,128,2048]{4,3,2,1,0:T(8,128)(2,1)} copy(bf16[1,1,2,128,2048]{4,3,2,1,0:T(8,128)(2,1)} %bitcast.19) | data formatting | bytes 2097152
  132.4 1.5 %copy.20 = bf16[64,3,256]{2,0,1:T(8,128)(2,1)} copy(bf16[64,3,256]{2,0,1:T(8,128)(2,1)} %bitcast.21) | data formatting | bytes 196608
  134.0 1.4 %copy.21 = bf16[32,512]{1,0:T(8,128)(2,1)} copy(bf16[32,512]{1,0:T(8,128)(2,1)} %get-tuple-element.30) | data formatting | bytes 65536

commit v7 on v6

--- a/solution.py
+++ b/solution.py
@@ -439,8 +439,8 @@
 
 def close_kernel(
     got_all, q_all, k_all, hidden_all, gz_all, ph_all, pz_all, scale_all, noisy_all, grad_all, w3,
-    out_n, out_g, out_o,
-    got, q, k, hidden, gz, ph, pz, scale1, noisy, grad, proj, pm, pp, w, gh,
+    all_n, out_g, out_o,
+    out_n, got, q, k, hidden, gz, ph, pz, scale1, noisy, grad, proj, pm, pp, w, gh,
     t0a, t0b, t0c, t1a, t1b, t1c, t2a, t2b, t2c, b0a, b0b, b0c, b1a, b1b, b1c, b2a, b2b, b2c,
     swap_sems, w_sem, ring_sems, last_sems,
 ):
@@ -688,6 +688,8 @@
         return carry
 
     lax.fori_loop(0, rows // 16, norm_rows, 0)
+    leave = pltpu.make_async_copy(out_n, all_n, w_sem.at[11])
+    leave.start()
 
     for s in range(3):
         ring_close(0, s)
@@ -725,6 +727,7 @@
                 rg, ch = (unit - 24) // 4, unit % 4
                 out_o[rg * 16 : (rg + 1) * 16, ch * 128 : (ch + 1) * 128] = sums[u]
 
+    leave.wait()
     for copy in swaps:
         copy.wait_send()
     for s in range(3):
@@ -751,8 +754,9 @@
             jax.ShapeDtypeStruct((32, 512), BF),
         ),
         in_specs=[ANY] * 11,
-        out_specs=(vmem,) * 3,
+        out_specs=(ANY, vmem, vmem),
         scratch_shapes=[
+            pltpu.VMEM((rows, model), BF),
             *[
                 pltpu.VMEM(array.shape, array.dtype)
                 for array in (got, q, k, hidden, gz, ph, pz, scale1, noisy, grad)
@@ -770,7 +774,7 @@
             *box(2, 3, 2),
             *box(3),
             pltpu.SemaphoreType.DMA((2, 7)),
-            pltpu.SemaphoreType.DMA((11,)),
+            pltpu.SemaphoreType.DMA((12,)),
             pltpu.SemaphoreType.DMA((3, 2, 2, 3, 2)),
             pltpu.SemaphoreType.DMA((3, 3, 2)),
         ],
@@ -779,6 +783,34 @@
         ),
         name="close",
     )(got, q, k, hidden, gz, ph, pz, scale1, noisy, grad, w3)
+
+
+def finish_kernel(*refs):
+    sources, targets, places, sems = refs[:3], refs[3:6], refs[6:9], refs[9]
+    inward = [pltpu.make_async_copy(sources[n], places[n], sems.at[0, n]) for n in range(3)]
+    outward = [pltpu.make_async_copy(places[n], targets[n], sems.at[1, n]) for n in range(3)]
+    for copy in inward:
+        copy.start()
+    for n in range(3):
+        inward[n].wait()
+        outward[n].start()
+    for copy in outward:
+        copy.wait()
+
+
+def finish(*arrays):
+    return pl.pallas_call(
+        finish_kernel,
+        out_shape=tuple(jax.ShapeDtypeStruct(array.shape, array.dtype) for array in arrays),
+        in_specs=[ANY] * 3,
+        out_specs=(ANY,) * 3,
+        scratch_shapes=[
+            *[pltpu.VMEM(array.shape, array.dtype) for array in arrays],
+            pltpu.SemaphoreType.DMA((2, 3)),
+        ],
+        compiler_params=pltpu.CompilerParams(vmem_limit_bytes=62 * 1024 * 1024),
+        name="finish",
+    )(*arrays)
 
 
 def on_device(
@@ -802,8 +834,8 @@
         w_out,
         temps,
     )
-    grad_noisy, total_g, total_o = close(
-        got, q, k, hidden, grad_z, ph, pz, scale1, noisy_rows, grad_rows, w3
+    grad_noisy, total_g, total_o = finish(
+        *close(got, q, k, hidden, grad_z, ph, pz, scale1, noisy_rows, grad_rows, w3)
     )
     return (grad_noisy.reshape(noisy.shape), total_g.transpose(1, 0, 2), total_o)
 

time: 136 us -> 132 us (0.971)
  local copies, waits for them, and re-layouts: 5.22 us -> 0 us
  Pallas kernels: 128 us -> 130 us
    unnamed x3 -> x0, local copies, waits for them, and re-layouts: 5.22 us -> none
    pallas_call x0 -> x1, Pallas kernels: none -> 2.27 us  [finish(): pl.pallas_call(finish_kernel, out_shape=tuple((jax.ShapeDtypeStruct(array...]
where the time goes in v7:
time: 132 us
  Pallas kernels  130 us (98%)
  between operations  2.12 us (2%)
    pallas_call x1, Pallas kernels, open_up(): pl.pallas_call(open_kernel, out_shape=(jax.ShapeDtypeStruct((8, 4, rows,...  73.3 us
    pallas_call x1, Pallas kernels, close(): pl.pallas_call(close_kernel, out_shape=(jax.ShapeDtypeStruct((rows, model...  54.5 us

profile of v7, /device:TPU:0, one launch (start us, length us, event | category | flops | bytes accessed | tf_op | source)
XLA Modules:
  0.0 132.2 jit_solution(5014342351891071436)
XLA Ops:
  1.9 73.3 %open.1 = (bf16[8,4,256,128]{3,2,1,0:T(8,128)(2,1)}, bf16[256,2048]{1,0:T(8,128)(2,1)}, bf16[256,2048]{1,0:T(8,128)(2,1)}, f32[256,1024]{1,0:T(8,128)}, f32[256,...) custom-call(s32[2]{0:T(128)} %bitcast.20, s32[1]{0:T(128)} %bitcast.10.action, ...), custom_call_target="tpu_custom_call" | custom-call | tf_op jit(solution)/shard_map/open/pallas_call | solution.py:376
  75.2 54.5 %close.1 = (bf16[256,2048]{1,0:T(8,128)(2,1)}, bf16[3,64,256]{2,1,0:T(8,128)(2,1)}, bf16[32,512]{1,0:T(8,128)(2,1)}) custom-call(bf16[8,4,256,128]{3,2,1,0:T(8,128)(2,1)} %get-tuple-element.17.got_all, f32[256,1024]{1,0:T(8,128)} %get-tuple-element.18.q_all, f32[256,1024]{1,0:T(8,128)} %get-tuple-element.19.k_all, ...), custom_call_target="tpu_custom_call" | custom-call | tf_op jit(solution)/shard_map/close/pallas_call | solution.py:749
  129.7 2.3 %finish.1 = (bf16[256,2048]{1,0:T(8,128)(2,1)}, bf16[3,64,256]{2,1,0:T(8,128)(2,1)}, bf16[32,512]{1,0:T(8,128)(2,1)}) custom-call(bf16[256,2048]{1,0:T(8,128)(2,1)} %get-tuple-element.25.refs_0_, bf16[3,64,256]{2,1,0:T(8,128)(2,1)} %get-tuple-element.26.refs_1_, bf16[32,512]{1,0:T(8,128)(2,1)} %get-tuple-element.27.refs_2_), custom_call_target="tpu_custom_call" | custom-call | tf_op jit(solution)/shard_map/finish/pallas_call | solution.py:802

commit v8 on v7

--- a/solution.py
+++ b/solution.py
@@ -329,11 +329,12 @@
         remote(res.at[i], got.at[slot], back_sems, peer(i)).start()
 
     def attend_row(s, carry):
-        row = (y + 3 - s) % 4
+        row = jnp.where(s < 3, s + jnp.where(s >= y, 1, 0), y)
+        came = 1 + (y + 3 - row) % 4
 
         @pl.when(s < 3)
         def _():
-            wait_bytes(own.at[pl.ds(0, 2)], own_sems.at[1 + s])
+            wait_bytes(own.at[pl.ds(0, 2)], own_sems.at[came])
 
         @pl.when(s == 3)
         def _():

time: 132 us -> 143 us (1.083)
  Pallas kernels: 130 us -> 140 us
    pallas_call x1, Pallas kernels: 73.3 us -> 78.8 us  [open_up(): pl.pallas_call(open_kernel, out_shape=(jax.ShapeDtypeStruct((8, 4, rows,...]
    pallas_call x1, Pallas kernels: 54.5 us -> 59.3 us  [close(): pl.pallas_call(close_kernel, out_shape=(jax.ShapeDtypeStruct((rows, model...]
where the time goes in v8:
time: 143 us; the launch traced here: 142 us
  Pallas kernels  140 us (98%)
  between operations  2.12 us (1%)
    pallas_call x1, Pallas kernels, open_up(): pl.pallas_call(open_kernel, out_shape=(jax.ShapeDtypeStruct((8, 4, rows,...  78.8 us
    pallas_call x1, Pallas kernels, close(): pl.pallas_call(close_kernel, out_shape=(jax.ShapeDtypeStruct((rows, model...  59.3 us

profile of v8, /device:TPU:0, one launch (start us, length us, event | category | flops | bytes accessed | tf_op | source)
XLA Modules:
  0.0 142.5 jit_solution(2447165365610954259)
XLA Ops:
  1.9 78.8 %open.1 = (bf16[8,4,256,128]{3,2,1,0:T(8,128)(2,1)}, bf16[256,2048]{1,0:T(8,128)(2,1)}, bf16[256,2048]{1,0:T(8,128)(2,1)}, f32[256,1024]{1,0:T(8,128)}, f32[256,...) custom-call(s32[2]{0:T(128)} %bitcast.20, s32[1]{0:T(128)} %bitcast.10.action, ...), custom_call_target="tpu_custom_call" | custom-call | tf_op jit(solution)/shard_map/open/pallas_call | solution.py:377
  80.7 59.3 %close.1 = (bf16[256,2048]{1,0:T(8,128)(2,1)}, bf16[3,64,256]{2,1,0:T(8,128)(2,1)}, bf16[32,512]{1,0:T(8,128)(2,1)}) custom-call(bf16[8,4,256,128]{3,2,1,0:T(8,128)(2,1)} %get-tuple-element.17.got_all, f32[256,1024]{1,0:T(8,128)} %get-tuple-element.18.q_all, f32[256,1024]{1,0:T(8,128)} %get-tuple-element.19.k_all, ...), custom_call_target="tpu_custom_call" | custom-call | tf_op jit(solution)/shard_map/close/pallas_call | solution.py:750
  140.0 2.3 %finish.1 = (bf16[256,2048]{1,0:T(8,128)(2,1)}, bf16[3,64,256]{2,1,0:T(8,128)(2,1)}, bf16[32,512]{1,0:T(8,128)(2,1)}) custom-call(bf16[256,2048]{1,0:T(8,128)(2,1)} %get-tuple-element.25.refs_0_, bf16[3,64,256]{2,1,0:T(8,128)(2,1)} %get-tuple-element.26.refs_1_, bf16[32,512]{1,0:T(8,128)(2,1)} %get-tuple-element.27.refs_2_), custom_call_target="tpu_custom_call" | custom-call | tf_op jit(solution)/shard_map/finish/pallas_call | solution.py:803
